TPU v7x, 32 devices: a whole 2x2x4 slice. The times are simulated.
32 devices in a mesh: seq: 4 (over y, x), mp: 8 (over z, core).
Axes of the slice: x: 2, y: 2, z: 4, core: 2. Of those that a mesh axis runs over, the one named last changes fastest.
Arguments:
- hidden: bfloat16 [2, 4096, 2048], P(None, ('seq', 'mp')), may hold values from -6 to 6
- cotangent: bfloat16 [2, 4096, 2048], P(None, ('seq', 'mp')), may hold values from -6 to 6
- lengths: int32 [2], replicated, may hold values from 1024 to 4096, as said below
- gain_mix: float32 [2048], replicated, may hold values from 0.5 to 1.5
- gain_mlp: float32 [2048], replicated, may hold values from 0.5 to 1.5
- conv_weight: float32 [3, 2048], replicated, may hold values from -3 to 3
- mixer_in: bfloat16 [3, 2048, 2048], P(None, 'seq', 'mp'), may hold values from -0.125 to 0.125
- mixer_out: bfloat16 [2048, 2048], P('mp', 'seq'), may hold values from -0.125 to 0.125
- gate_up: bfloat16 [2, 2048, 8192], P(None, 'seq', 'mp'), may hold values from -0.125 to 0.125
- mlp_down: bfloat16 [8192, 2048], P('mp', 'seq'), may hold values from -0.0625 to 0.0625
Outputs:
- output: bfloat16 [2, 4096, 2048], P(None, ('seq', 'mp'))
- grad_hidden: float32 [2, 4096, 2048], P(None, ('seq', 'mp'))
- grad_gain_mix: float32 [2048], replicated
- grad_gain_mlp: float32 [2048], replicated
- grad_conv: float32 [3, 2048], replicated
- grad_mixer_in: float32 [3, 2048, 2048], P(None, 'seq', 'mp')
- grad_mixer_out: float32 [2048, 2048], P('mp', 'seq')
- grad_gate_up: float32 [2, 2048, 8192], P(None, 'seq', 'mp')
- grad_mlp_down: float32 [8192, 2048], P('mp', 'seq')
Inputs may be any that keep to these rules, and one draw needn't show every extreme that they name: `lengths`: each slot's valid tokens are its first positions; in every draw one slot, which one drawn from the seed, is valid over all 4096 positions.
All inputs are finite; a program needn't handle non-finite values.
Results may differ from a plain program's by a relative error of at most 0.012.
Values may be sent and summed in bfloat16 or wider, within the bound.
A program may use at most 192 MiB of HBM per device.

v0:
```python
import jax
import jax.numpy as jnp
from jax import lax
from jax.sharding import PartitionSpec as P

EPS = 1e-05


def shifted(value, axis, steps):
    count = lax.axis_size(axis)
    leading, last = (max(0, -steps), min(count, count - steps))
    return lax.ppermute(value, axis, [(source, source + steps) for source in range(leading, last)])


def normalize(values, gain):
    scale = lax.rsqrt(jnp.mean(values * values, axis=-1, keepdims=True) + EPS)
    return (values * scale * gain, scale)


def norm_back(grad, values, scale, gain):
    unit = values * scale
    scaled = grad * gain
    gain_grad = jnp.sum(grad * unit, axis=0)
    input_grad = scale * (scaled - unit * jnp.mean(scaled * unit, axis=-1, keepdims=True))
    return (input_grad, gain_grad)


def local(
    hidden,
    cotangent,
    lengths,
    gain_mix,
    gain_mlp,
    conv_weight,
    mixer_in,
    mixer_out,
    gate_up,
    mlp_down,
):
    model_count = lax.axis_size("mp")
    seq_pos = lax.axis_index("seq")
    model_pos = lax.axis_index("mp")
    share_rows = hidden.shape[1]
    block_rows = share_rows * model_count
    channels = mixer_in.shape[2]
    width = hidden.shape[2]
    units = gate_up.shape[2]
    taps = conv_weight.shape[0]
    local_taps = lax.dynamic_slice_in_dim(conv_weight, model_pos * channels, channels, 1)
    share_start = (seq_pos * model_count + model_pos) * share_rows
    share_pos = share_start + jnp.arange(share_rows, dtype=jnp.int32)
    in_total = jnp.zeros((3, width, channels), jnp.float32)
    out_total = jnp.zeros((channels, width), jnp.float32)
    pair_total = jnp.zeros((2, width, units), jnp.float32)
    down_total = jnp.zeros((units, width), jnp.float32)
    gain_mix_total = jnp.zeros((width,), jnp.float32)
    gain_mlp_total = jnp.zeros((width,), jnp.float32)
    taps_total = jnp.zeros((taps, channels), jnp.float32)
    outputs = []
    input_grads = []
    for slot_index in range(hidden.shape[0]):
        in_full, out_full, pair_full, down_full = (
            lax.all_gather(mixer_in, "seq", axis=1, tiled=True),
            lax.all_gather(mixer_out, "seq", axis=1, tiled=True),
            lax.all_gather(gate_up, "seq", axis=1, tiled=True),
            lax.all_gather(mlp_down, "seq", axis=1, tiled=True),
        )
        mask_rows = (share_pos < lengths[slot_index]).astype(jnp.float32)[:, None]
        source = hidden[slot_index].astype(jnp.float32)
        normed, scale_mix = normalize(source, gain_mix)
        normed_rows = lax.all_gather(normed.astype(jnp.bfloat16), "mp", axis=0, tiled=True)
        projected = jnp.einsum(
            "td,kdc->ktc", normed_rows, in_full, preferred_element_type=jnp.float32
        )
        b_gate = projected[0]
        c_gate = projected[1]
        x_value = projected[2]
        product = b_gate * x_value
        earlier = shifted(product[block_rows - (taps - 1) :], "seq", 1)
        extended = jnp.concatenate([earlier, product], axis=0)
        conv_out = jnp.zeros_like(product)
        for offset in range(taps):
            conv_out = (
                conv_out
                + local_taps[offset] * extended[taps - 1 - offset : taps - 1 - offset + block_rows]
            )
        mixed = (c_gate * conv_out).astype(jnp.bfloat16)
        mix_share = lax.psum_scatter(
            jnp.dot(mixed, out_full, preferred_element_type=jnp.float32),
            "mp",
            scatter_dimension=0,
            tiled=True,
        )
        middle = source + mix_share
        normed_two, scale_mlp = normalize(middle, gain_mlp)
        mlp_rows = lax.all_gather(normed_two.astype(jnp.bfloat16), "mp", axis=0, tiled=True)
        gated = jnp.einsum("td,kdf->ktf", mlp_rows, pair_full, preferred_element_type=jnp.float32)
        gate_part = gated[0]
        up_part = gated[1]
        activated = jax.nn.silu(gate_part)
        hidden_act = (activated * up_part).astype(jnp.bfloat16)
        mlp_share = lax.psum_scatter(
            jnp.dot(hidden_act, down_full, preferred_element_type=jnp.float32),
            "mp",
            scatter_dimension=0,
            tiled=True,
        )
        outputs.append((mask_rows * (middle + mlp_share)).astype(jnp.bfloat16))
        in_back, out_back, pair_back, down_back = (
            lax.all_gather(mixer_in, "seq", axis=1, tiled=True),
            lax.all_gather(mixer_out, "seq", axis=1, tiled=True),
            lax.all_gather(gate_up, "seq", axis=1, tiled=True),
            lax.all_gather(mlp_down, "seq", axis=1, tiled=True),
        )
        top_grad = cotangent[slot_index].astype(jnp.float32) * mask_rows
        top_rows = lax.all_gather(top_grad.astype(jnp.bfloat16), "mp", axis=0, tiled=True)
        down_total = down_total + jnp.einsum(
            "tf,td->fd", hidden_act, top_rows, preferred_element_type=jnp.float32
        )
        act_grad = jnp.einsum("td,fd->tf", top_rows, down_back, preferred_element_type=jnp.float32)
        sigma = jax.nn.sigmoid(gate_part)
        gate_grad = (act_grad * up_part * sigma * (1.0 + gate_part * (1.0 - sigma))).astype(
            jnp.bfloat16
        )
        up_grad = (act_grad * activated).astype(jnp.bfloat16)
        pair_grad = jnp.stack([gate_grad, up_grad])
        pair_total = pair_total + jnp.einsum(
            "td,ktf->kdf", mlp_rows, pair_grad, preferred_element_type=jnp.float32
        )
        normed_two_grad = lax.psum_scatter(
            jnp.einsum("ktf,kdf->td", pair_grad, pair_back, preferred_element_type=jnp.float32),
            "mp",
            scatter_dimension=0,
            tiled=True,
        )
        middle_grad, gain_part = norm_back(normed_two_grad, middle, scale_mlp, gain_mlp)
        gain_mlp_total = gain_mlp_total + gain_part
        middle_grad = middle_grad + top_grad
        mix_rows = lax.all_gather(middle_grad.astype(jnp.bfloat16), "mp", axis=0, tiled=True)
        out_total = out_total + jnp.einsum(
            "tc,td->cd", mixed, mix_rows, preferred_element_type=jnp.float32
        )
        mixed_grad = jnp.einsum("td,cd->tc", mix_rows, out_back, preferred_element_type=jnp.float32)
        c_grad = mixed_grad * conv_out
        conv_grad = mixed_grad * c_gate
        later = shifted(conv_grad[: taps - 1], "seq", -1)
        tail = jnp.concatenate([conv_grad, later], axis=0)
        product_grad = jnp.zeros_like(conv_grad)
        tap_rows = []
        for offset in range(taps):
            product_grad = product_grad + local_taps[offset] * tail[offset : offset + block_rows]
            tap_rows.append(
                jnp.sum(
                    conv_grad * extended[taps - 1 - offset : taps - 1 - offset + block_rows], axis=0
                )
            )
        taps_total = taps_total + jnp.stack(tap_rows)
        stacked = jnp.stack([product_grad * x_value, c_grad, product_grad * b_gate]).astype(
            jnp.bfloat16
        )
        in_total = in_total + jnp.einsum(
            "td,ktc->kdc", normed_rows, stacked, preferred_element_type=jnp.float32
        )
        normed_grad = lax.psum_scatter(
            jnp.einsum("ktc,kdc->td", stacked, in_back, preferred_element_type=jnp.float32),
            "mp",
            scatter_dimension=0,
            tiled=True,
        )
        source_grad, gain_part = norm_back(normed_grad, source, scale_mix, gain_mix)
        gain_mix_total = gain_mix_total + gain_part
        input_grads.append(source_grad + middle_grad)
    in_grad, out_grad, pair_out, down_out = (
        lax.psum_scatter(in_total, "seq", scatter_dimension=1, tiled=True),
        lax.psum_scatter(out_total, "seq", scatter_dimension=1, tiled=True),
        lax.psum_scatter(pair_total, "seq", scatter_dimension=1, tiled=True),
        lax.psum_scatter(down_total, "seq", scatter_dimension=1, tiled=True),
    )
    taps_full = lax.dynamic_update_slice_in_dim(
        jnp.zeros((taps, width), jnp.float32), taps_total, model_pos * channels, 1
    )
    gain_mix_grad, gain_mlp_grad, taps_grad = lax.psum(
        (gain_mix_total, gain_mlp_total, taps_full), ("seq", "mp")
    )
    return (
        jnp.stack(outputs),
        jnp.stack(input_grads),
        gain_mix_grad,
        gain_mlp_grad,
        taps_grad,
        in_grad,
        out_grad,
        pair_out,
        down_out,
    )


def solution(mesh):
    placed = (
        P(None, ("seq", "mp"), None),
        P(None, ("seq", "mp"), None),
        P(),
        P(),
        P(),
        P(),
        P(None, "seq", "mp"),
        P("mp", "seq"),
        P(None, "seq", "mp"),
        P("mp", "seq"),
    )
    return jax.shard_map(
        local,
        mesh=mesh,
        in_specs=placed,
        out_specs=(
            P(None, ("seq", "mp"), None),
            P(None, ("seq", "mp"), None),
            P(),
            P(),
            P(),
            P(None, "seq", "mp"),
            P("mp", "seq"),
            P(None, "seq", "mp"),
            P("mp", "seq"),
        ),
        check_vma=False,
    )
```

profile of v0, /device:TPU:0, one launch (start us, length us, event | category | flops | bytes accessed | tf_op | source)
XLA Modules:
  0.0 1761.0 jit_solution(10204969167509031524)
XLA Ops:
  10.0 2.5 fusion.53
  13.9 42.7 %all-gather.15.cloned.1.call-done = bf16[3,2048,256]{2,1,0:T(8,128)(2,1)} async-done(((bf16[3,512,256]{2,1,0:T(8,128)(2,1)}), bf16[3,2048,256]{2,1,0:T(8,128)(2,1)}) %all-gather.15.cloned.1.call-update) | async-done | bytes 3145744 | tf_op jit(solution)/shard_map/all_gather | solution.py:63
  56.6 49.4 %all-gather.13.cloned.1.call-done = bf16[1024,2048]{1,0:T(8,128)(2,1)} async-done(((bf16[128,2048]{1,0:T(8,128)(2,1)}), bf16[1024,2048]{1,0:T(8,128)(2,1)}) %all-gather.13.cloned.1.call-update) | async-done | bytes 4194320 | tf_op jit(solution)/shard_map/all_gather | solution.py:71
  105.9 6.1 fusion.29
  113.3 3.4 collective-permute-start
  116.7 37.3 %all-gather.25.cloned.1.call-done = bf16[1024,2048]{1,0:T(8,128)(2,1)} async-done(((bf16[128,2048]{1,0:T(8,128)(2,1)}), bf16[1024,2048]{1,0:T(8,128)(2,1)}) %all-gather.25.cloned.1.call-update) | async-done | bytes 4194320 | tf_op jit(solution)/shard_map/all_gather | solution.py:71
  154.0 6.2 fusion.32
  160.4 3.4 collective-permute-start.1
  165.7 2.1 multiply_convert_fusion.17
  167.7 13.2 all-gather.17.cloned.1.call-done
  180.9 5.9 fusion.105
  188.2 4.6 fusion.107
  193.7 83.0 %reduce-scatter.13.cloned.1.call-done = f32[128,2048]{1,0:T(8,128)} async-done(((f32[1024,2048]{1,0:T(8,128)}), f32[128,2048]{1,0:T(8,128)}) %reduce-scatter.13.cloned.1.call-update) | async-done | bytes 1048592 | tf_op jit(solution)/shard_map/reduce_scatter | solution.py:88
  276.6 90.1 %reduce-scatter.17.cloned.1.call-done = f32[128,2048]{1,0:T(8,128)} async-done(((f32[1024,2048]{1,0:T(8,128)}), f32[128,2048]{1,0:T(8,128)}) %reduce-scatter.17.cloned.1.call-update) | async-done | bytes 1048592 | tf_op jit(solution)/shard_map/reduce_scatter | solution.py:88
  366.8 1.9 multiply_reduce_fusion.11
  372.4 2.6 fusion.74
  375.2 79.5 %all-gather.21.cloned.1.call-done = bf16[2,2048,1024]{2,1,0:T(8,128)(2,1)} async-done(((bf16[2,512,1024]{2,1,0:T(8,128)(2,1)}), bf16[2,2048,1024]{2,1,0:T(8,128)(2,1)}) %all-gather.21.cloned.1.call-update) | async-done | bytes 8388624 | tf_op jit(solution)/shard_map/all_gather | solution.py:65
  454.6 49.4 %all-gather.19.cloned.1.call-done = bf16[1024,2048]{1,0:T(8,128)(2,1)} async-done(((bf16[128,2048]{1,0:T(8,128)(2,1)}), bf16[1024,2048]{1,0:T(8,128)(2,1)}) %all-gather.19.cloned.1.call-update) | async-done | bytes 4194320 | tf_op jit(solution)/shard_map/all_gather | solution.py:96
  504.0 14.5 fusion.19
  518.5 38.7 %all-gather.23.cloned.1.call-done = bf16[1024,2048]{1,0:T(8,128)(2,1)} async-done(((bf16[1024,512]{1,0:T(8,128)(2,1)}), bf16[1024,2048]{1,0:T(8,128)(2,1)}) %all-gather.23.cloned.1.call-update) | async-done | bytes 4194320 | tf_op jit(solution)/shard_map/all_gather | solution.py:66
  557.1 49.2 %all-gather.29.cloned.1.call-done = bf16[1024,2048]{1,0:T(8,128)(2,1)} async-done(((bf16[128,2048]{1,0:T(8,128)(2,1)}), bf16[1024,2048]{1,0:T(8,128)(2,1)}) %all-gather.29.cloned.1.call-update) | async-done | bytes 4194320 | tf_op jit(solution)/shard_map/all_gather | solution.py:116
  606.3 13.1 fusion.27
  621.4 13.3 convolution_bitcast_fusion.3
  634.8 88.4 %reduce-scatter.21.cloned.1.call-done = f32[128,2048]{1,0:T(8,128)} async-done(((f32[1024,2048]{1,0:T(8,128)}), f32[128,2048]{1,0:T(8,128)}) %reduce-scatter.21.cloned.1.call-update) | async-done | bytes 1048592 | tf_op jit(solution)/shard_map/reduce_scatter | solution.py:130
  723.2 3.0 multiply_reduce_fusion.7
  727.2 44.6 %all-gather.27.cloned.1.call-done = bf16[1024,2048]{1,0:T(8,128)(2,1)} async-done(((bf16[128,2048]{1,0:T(8,128)(2,1)}), bf16[1024,2048]{1,0:T(8,128)(2,1)}) %all-gather.27.cloned.1.call-update) | async-done | bytes 4194320 | tf_op jit(solution)/shard_map/all_gather | solution.py:96
  771.8 14.5 fusion.22
  786.3 33.0 %all-gather.33.cloned.1.call-done = bf16[1024,2048]{1,0:T(8,128)(2,1)} async-done(((bf16[128,2048]{1,0:T(8,128)(2,1)}), bf16[1024,2048]{1,0:T(8,128)(2,1)}) %all-gather.33.cloned.1.call-update) | async-done | bytes 4194320 | tf_op jit(solution)/shard_map/all_gather | solution.py:116
  819.3 13.1 fusion.28
  834.4 13.3 convolution_bitcast_fusion.1
  848.2 10.6 fusion.106
  858.9 10.7 fusion.108
  869.7 66.5 %reduce-scatter.25.cloned.1.call-done = f32[128,2048]{1,0:T(8,128)} async-done(((f32[1024,2048]{1,0:T(8,128)}), f32[128,2048]{1,0:T(8,128)}) %reduce-scatter.25.cloned.1.call-update) | async-done | bytes 1048592 | tf_op jit(solution)/shard_map/reduce_scatter | solution.py:130
  936.2 1.6 multiply_reduce_fusion.6
  937.8 88.6 %reduce-scatter.15.cloned.1.call-done = f32[128,2048]{1,0:T(8,128)} async-done(((f32[1024,2048]{1,0:T(8,128)}), f32[128,2048]{1,0:T(8,128)}) %reduce-scatter.15.cloned.1.call-update) | async-done | bytes 1048592 | tf_op jit(solution)/shard_map/reduce_scatter | solution.py:102
  1026.3 90.1 %reduce-scatter.19.cloned.1.call-done = f32[128,2048]{1,0:T(8,128)} async-done(((f32[1024,2048]{1,0:T(8,128)}), f32[128,2048]{1,0:T(8,128)}) %reduce-scatter.19.cloned.1.call-update) | async-done | bytes 1048592 | tf_op jit(solution)/shard_map/reduce_scatter | solution.py:102
  1116.5 5.2 fusion.99
  1122.5 15.4 fusion.7
  1137.9 16.2 add_bitcast_fusion
  1154.1 13.2 all-gather.31.cloned.1.call-done
  1167.3 3.9 fusion.109
  1175.0 39.7 %all-gather.35.cloned.1.call-done = bf16[1024,2048]{1,0:T(8,128)(2,1)} async-done(((bf16[128,2048]{1,0:T(8,128)(2,1)}), bf16[1024,2048]{1,0:T(8,128)(2,1)}) %all-gather.35.cloned.1.call-update) | async-done | bytes 4194320 | tf_op jit(solution)/shard_map/all_gather | solution.py:139
  1214.7 3.9 fusion.110
  1220.5 4.2 collective-permute-done.3
  1226.0 2.3 copy-done.15
  1228.3 3.6 fusion.3
  1231.9 5.7 add_bitcast_fusion.1
  1238.9 7.6 convolution_bitcast_fusion.2
  1247.7 7.7 convolution_bitcast_fusion
  1257.0 6.8 fusion.112
  1263.8 7.1 convolution_add_fusion
  1272.0 3.6 fusion.111
  1275.8 2.6 convolution_add_fusion.1
  1279.6 90.7 %reduce-scatter.33.cloned.1.call-done = f32[2,512,1024]{1,2,0:T(8,128)} async-done(((f32[2,2048,1024]{1,2,0:T(8,128)}), f32[2,512,1024]{1,2,0:T(8,128)}) %reduce-scatter.33.cloned.1.call-update) | async-done | bytes 4194320 | tf_op jit(solution)/shard_map/reduce_scatter | solution.py:176
  1370.3 5.3 copy.24
  1375.6 67.7 %reduce-scatter.29.cloned.1.call-done = f32[3,512,256]{1,2,0:T(8,128)} async-done(((f32[3,2048,256]{1,2,0:T(8,128)}), f32[3,512,256]{1,2,0:T(8,128)}) %reduce-scatter.29.cloned.1.call-update) | async-done | bytes 1572880 | tf_op jit(solution)/shard_map/reduce_scatter | solution.py:174
  1443.3 3.0 copy.23
  1446.3 88.9 %reduce-scatter.23.cloned.1.call-done = f32[128,2048]{1,0:T(8,128)} async-done(((f32[1024,2048]{1,0:T(8,128)}), f32[128,2048]{1,0:T(8,128)}) %reduce-scatter.23.cloned.1.call-update) | async-done | bytes 1048592 | tf_op jit(solution)/shard_map/reduce_scatter | solution.py:164
  1535.2 90.3 %reduce-scatter.27.cloned.1.call-done = f32[128,2048]{1,0:T(8,128)} async-done(((f32[1024,2048]{1,0:T(8,128)}), f32[128,2048]{1,0:T(8,128)}) %reduce-scatter.27.cloned.1.call-update) | async-done | bytes 1048592 | tf_op jit(solution)/shard_map/reduce_scatter | solution.py:164
  1625.5 2.2 fusion.59
  1627.7 39.2 %all-reduce = (f32[2048]{0:T(1024)}, f32[2048]{0:T(1024)}, f32[3,2048]{1,0:T(4,128)}) all-reduce(f32[2048]{0:T(1024)S(1)} %add.200, f32[2048]{0:T(1024)S(1)} %add.201, f32[3,2048]{1,0:T(4,128)S(1)} %fusion.87), channel_id=1, replica_groups=mesh['seq'=4,'mp'=8] {'seq','mp'}, use_global_device_ids=true, to_apply=%region_18.19 | all-reduce | flops 10240 | bytes 81920 | tf_op jit(solution)/shard_map/psum | solution.py:182
  1666.9 2.1 fusion.58
  1670.6 44.3 %reduce-scatter.35.cloned.1.call-done = f32[1024,512]{1,0:T(8,128)} async-done(((f32[1024,2048]{1,0:T(8,128)}), f32[1024,512]{1,0:T(8,128)}) %reduce-scatter.35.cloned.1.call-update) | async-done | bytes 2097168 | tf_op jit(solution)/shard_map/reduce_scatter | solution.py:177
  1714.8 38.9 %reduce-scatter.31.cloned.1.call-done = f32[256,512]{1,0:T(8,128)} async-done(((f32[256,2048]{1,0:T(8,128)}), f32[256,512]{1,0:T(8,128)}) %reduce-scatter.31.cloned.1.call-update) | async-done | bytes 524304 | tf_op jit(solution)/shard_map/reduce_scatter | solution.py:175
  (209 shorter events, 34.6 us)
Async XLA Ops:
  7.2 49.4 %all-gather.15.cloned.1.call-start = ((), (), s32[]{:S(2)}) async-start(), calls=%async_computation.13 | async-start | bytes 3932160 | tf_op jit(solution)/shard_map/all_gather | solution.py:63
  7.9 98.0 %all-gather.13.cloned.1.call-start = ((), (), s32[]{:S(2)}) async-start(), calls=%async_computation.12 | async-start | bytes 4718592 | tf_op jit(solution)/shard_map/all_gather | solution.py:71
  12.5 141.5 %all-gather.25.cloned.1.call-start = ((), (), s32[]{:S(2)}) async-start(), calls=%async_computation.20 | async-start | bytes 4718592 | tf_op jit(solution)/shard_map/all_gather | solution.py:71
  13.2 167.7 %all-gather.17.cloned.1.call-start = ((), (), s32[]{:S(2)}) async-start(), calls=%async_computation.14 | async-start | bytes 1310720 | tf_op jit(solution)/shard_map/all_gather | solution.py:64
  13.8 262.8 %reduce-scatter.13.cloned.1.call-start = ((), (), s32[]{:S(2)}) async-start(), calls=%async_computation.15 | async-start | bytes 9437184 | tf_op jit(solution)/shard_map/reduce_scatter | solution.py:88
  112.1 53.0 %copy-start.2 = (f32[3,1024,256]{2,1,0:T(8,128)}, f32[3,1024,256]{2,1,0:T(8,128)S(1)}, u32[]{:S(2)}) copy-start(f32[3,1024,256]{2,1,0:T(8,128)S(1)} %fusion.29) | copy-start | bytes 9437188
  113.3 51.4 %collective-permute-start = (f32[2,256]{1,0:T(2,128)S(1)}, f32[2,256]{1,0:T(2,128)S(1)}, u32[]{:S(2)}, u32[]{:S(2)}) collective-permute-start(f32[2,256]{1,0:T(2,128)S(1)} %slice.140), channel_id=1, source_target_pairs={{0,8},{8,16},{16,24},{1,9},{9,17},{17,25},{2,10},{10,18},{18,26},{... | collective-permute-start | bytes 6152 | tf_op jit(solution)/shard_map/ppermute | solution.py:12
  154.0 11.7 copy-start.9
  160.2 4.8 copy-start.4
  160.4 4.7 copy-start.6
  160.4 4.7 collective-permute-start.1
  164.7 22.2 %copy-start.47 = (f32[2,256]{1,0:T(2,128)}, f32[2,256]{1,0:T(2,128)S(1)}, u32[]{:S(2)}) copy-start(f32[2,256]{1,0:T(2,128)S(1)} %collective-permute-done) | copy-start | bytes 6148
  186.9 179.9 %reduce-scatter.17.cloned.1.call-start = ((), (), s32[]{:S(2)}) async-start(), calls=%async_computation.21 | async-start | bytes 9437184 | tf_op jit(solution)/shard_map/reduce_scatter | solution.py:88
  192.8 174.0 %copy-start = (bf16[2,128,2048]{2,1,0:T(8,128)(2,1)S(1)}, bf16[2,128,2048]{2,1,0:T(8,128)(2,1)}, u32[]{:S(2)}) copy-start(bf16[2,128,2048]{2,1,0:T(8,128)(2,1)} %param.10) | copy-start | bytes 3145732
  192.8 175.9 %copy-start.36 = (f32[2048]{0:T(1024)S(1)}, f32[2048]{0:T(1024)}, u32[]{:S(2)}) copy-start(f32[2048]{0:T(1024)} %param.14) | copy-start | bytes 24580
  192.9 261.8 %all-gather.21.cloned.1.call-start = ((), (), s32[]{:S(2)}) async-start(), calls=%async_computation.17 | async-start | bytes 10485760 | tf_op jit(solution)/shard_map/all_gather | solution.py:65
  193.6 176.9 %copy-start.53 = (s32[2]{0:T(128)S(1)}, s32[2]{0:T(128)}, u32[]{:S(2)}) copy-start(s32[2]{0:T(128)} %param.12) | copy-start | bytes 28
  193.6 310.4 %all-gather.19.cloned.1.call-start = ((), (), s32[]{:S(2)}) async-start(), calls=%async_computation.16 | async-start | bytes 4718592 | tf_op jit(solution)/shard_map/all_gather | solution.py:96
  369.7 187.4 %all-gather.23.cloned.1.call-start = ((), (), s32[]{:S(2)}) async-start(), calls=%async_computation.18 | async-start | bytes 5242880 | tf_op jit(solution)/shard_map/all_gather | solution.py:66
  370.4 235.9 %all-gather.29.cloned.1.call-start = ((), (), s32[]{:S(2)}) async-start(), calls=%async_computation.24 | async-start | bytes 4718592 | tf_op jit(solution)/shard_map/all_gather | solution.py:116
  374.9 348.2 %reduce-scatter.21.cloned.1.call-start = ((), (), s32[]{:S(2)}) async-start(), calls=%async_computation.25 | async-start | bytes 9437184 | tf_op jit(solution)/shard_map/reduce_scatter | solution.py:130
  634.7 137.1 %all-gather.27.cloned.1.call-start = ((), (), s32[]{:S(2)}) async-start(), calls=%async_computation.22 | async-start | bytes 4718592 | tf_op jit(solution)/shard_map/all_gather | solution.py:96
  726.2 93.2 %all-gather.33.cloned.1.call-start = ((), (), s32[]{:S(2)}) async-start(), calls=%async_computation.28 | async-start | bytes 4718592 | tf_op jit(solution)/shard_map/all_gather | solution.py:116
  726.9 209.3 %reduce-scatter.25.cloned.1.call-start = ((), (), s32[]{:S(2)}) async-start(), calls=%async_computation.29 | async-start | bytes 9437184 | tf_op jit(solution)/shard_map/reduce_scatter | solution.py:130
  847.7 178.6 %reduce-scatter.15.cloned.1.call-start = ((), (), s32[]{:S(2)}) async-start(), calls=%async_computation.19 | async-start | bytes 9437184 | tf_op jit(solution)/shard_map/reduce_scatter | solution.py:102
  858.8 257.6 %reduce-scatter.19.cloned.1.call-start = ((), (), s32[]{:S(2)}) async-start(), calls=%async_computation.23 | async-start | bytes 9437184 | tf_op jit(solution)/shard_map/reduce_scatter | solution.py:102
  869.6 246.9 %copy-start.19 = (f32[128,2048]{1,0:T(8,128)S(1)}, f32[128,2048]{1,0:T(8,128)}, u32[]{:S(2)}) copy-start(f32[128,2048]{1,0:T(8,128)} %reduce-scatter.21.cloned.1.call-done) | copy-start | bytes 3145732
  869.6 297.7 %all-gather.31.cloned.1.call-start = ((), (), s32[]{:S(2)}) async-start(), calls=%async_computation.26 | async-start | bytes 4718592 | tf_op jit(solution)/shard_map/all_gather | solution.py:139
  1121.7 93.0 %all-gather.35.cloned.1.call-start = ((), (), s32[]{:S(2)}) async-start(), calls=%async_computation.30 | async-start | bytes 4718592 | tf_op jit(solution)/shard_map/all_gather | solution.py:139
  1122.2 15.6 copy-start.61
  1122.2 248.0 %reduce-scatter.33.cloned.1.call-start = ((), (), s32[]{:S(2)}) async-start(), calls=%async_computation.34 | async-start | bytes 20971520 | tf_op jit(solution)/shard_map/reduce_scatter | solution.py:176
  1122.5 15.4 copy-start.55
  1122.5 15.4 copy-start.63
  1154.1 17.2 copy-start.3
  1154.1 17.2 copy-start.48
  1154.1 289.2 %reduce-scatter.29.cloned.1.call-start = ((), (), s32[]{:S(2)}) async-start(), calls=%async_computation.32 | async-start | bytes 7864320 | tf_op jit(solution)/shard_map/reduce_scatter | solution.py:174
  1167.3 4.0 copy-start.23
  1172.5 46.2 %copy-start.46 = (f32[2,256]{1,0:T(2,128)S(1)}, f32[2,256]{1,0:T(2,128)}, u32[]{:S(2)}) copy-start(f32[2,256]{1,0:T(2,128)} %copy-done.45) | copy-start | bytes 6148
  1173.5 47.0 %collective-permute-start.2 = (f32[2,256]{1,0:T(2,128)S(1)}, f32[2,256]{1,0:T(2,128)S(1)}, u32[]{:S(2)}, u32[]{:S(2)}) collective-permute-start(f32[2,256]{1,0:T(2,128)S(1)} %slice.153), channel_id=1, source_target_pairs={{8,0},{16,8},{24,16},{9,1},{17,9},{25,17},{10,2},{18,10},{26,18},{... | collective-permute-start | bytes 6152 | tf_op jit(solution)/shard_map/ppermute | solution.py:12
  1214.7 4.0 copy-start.5
  1214.7 4.0 copy-start.7
  1214.7 4.1 copy-start.22
  1218.6 6.1 copy-start.14
  1218.6 6.1 copy-start.40
  1218.6 6.1 copy-start.42
  1218.6 6.0 copy-start.44
  1219.2 6.8 copy-start.30
  1219.2 5.5 collective-permute-start.3
  1225.5 6.4 copy-start.32
  1225.5 6.4 copy-start.34
  1225.7 6.1 copy-start.25
  1237.6 297.6 %reduce-scatter.23.cloned.1.call-start = ((), (), s32[]{:S(2)}) async-start(), calls=%async_computation.27 | async-start | bytes 9437184 | tf_op jit(solution)/shard_map/reduce_scatter | solution.py:164
  1246.5 379.0 %reduce-scatter.27.cloned.1.call-start = ((), (), s32[]{:S(2)}) async-start(), calls=%async_computation.31 | async-start | bytes 9437184 | tf_op jit(solution)/shard_map/reduce_scatter | solution.py:164
  1255.4 459.4 %reduce-scatter.35.cloned.1.call-start = ((), (), s32[]{:S(2)}) async-start(), calls=%async_computation.35 | async-start | bytes 10485760 | tf_op jit(solution)/shard_map/reduce_scatter | solution.py:177
  1257.0 6.8 copy-start.54
  1257.0 6.8 copy-start.57
  1270.9 4.7 copy-start.12
  1270.9 482.8 %reduce-scatter.31.cloned.1.call-start = ((), (), s32[]{:S(2)}) async-start(), calls=%async_computation.33 | async-start | bytes 2621440 | tf_op jit(solution)/shard_map/reduce_scatter | solution.py:175
  1279.5 346.0 %copy-start.1 = (bf16[2,128,2048]{2,1,0:T(8,128)(2,1)S(1)}, bf16[2,128,2048]{2,1,0:T(8,128)(2,1)}, u32[]{:S(2)}) copy-start(bf16[2,128,2048]{2,1,0:T(8,128)(2,1)} %param.10) | copy-start | bytes 3145732
  1279.5 346.0 %copy-start.37 = (f32[2048]{0:T(1024)S(1)}, f32[2048]{0:T(1024)}, u32[]{:S(2)}) copy-start(f32[2048]{0:T(1024)} %param.13) | copy-start | bytes 24580
  1279.5 346.0 %copy-start.50 = (f32[128]{0:T(128)S(1)}, f32[128]{0:T(128)}, u32[]{:S(2)}) copy-start(f32[128]{0:T(128)} %copy-done.49) | copy-start | bytes 1540
  1279.5 346.0 %copy-start.52 = (f32[128]{0:T(128)S(1)}, f32[128]{0:T(128)}, u32[]{:S(2)}) copy-start(f32[128]{0:T(128)} %copy-done.51) | copy-start | bytes 1540
  1375.6 291.3 %copy-start.17 = (f32[128,2048]{1,0:T(8,128)S(1)}, f32[128,2048]{1,0:T(8,128)}, u32[]{:S(2)}) copy-start(f32[128,2048]{1,0:T(8,128)} %get-tuple-element.44) | copy-start | bytes 3145732
  1375.6 291.3 %copy-start.18 = (f32[128,2048]{1,0:T(8,128)S(1)}, f32[128,2048]{1,0:T(8,128)}, u32[]{:S(2)}) copy-start(f32[128,2048]{1,0:T(8,128)} %get-tuple-element.66) | copy-start | bytes 3145732
  (28 other events, 50.0 us)
Sparse Core Ops, SparseCore 0:
  9.9 46.6 all-gather.14
  58.7 47.1 all-gather.12
  108.1 45.8 all-gather.24
  155.7 25.1 all-gather.16
  187.0 89.5 reduce-scatter.12
  278.8 87.9 reduce-scatter.16
  368.6 85.9 all-gather.20
  456.8 47.1 all-gather.18
  505.8 51.2 all-gather.22
  559.1 47.1 all-gather.28
  634.8 88.3 reduce-scatter.20
  726.3 45.4 all-gather.26
  773.4 45.8 all-gather.32
  847.8 88.3 reduce-scatter.24
  938.3 87.9 reduce-scatter.14
  1028.5 87.9 reduce-scatter.18
  1121.8 45.4 all-gather.30
  1168.7 45.8 all-gather.34
  1217.7 152.4 reduce-scatter.32
  1373.1 70.1 reduce-scatter.28
  1445.6 89.5 reduce-scatter.22
  1537.5 87.9 reduce-scatter.26
  1629.2 85.6 reduce-scatter.34
  1718.5 35.1 reduce-scatter.30
where the time goes:
time: 1770 us; the launch traced here: 1760 us
  waiting for transfers between devices  1430 us (81%)
  matrix products  210 us (12%)
  blocking collectives  39.2 us (2%)
  other arithmetic  32.5 us (2%)
  local copies, waits for them, and re-layouts  25.6 us (1%)
    reduce_scatter x2, waiting for transfers between devices, local(): lax.psum_scatter(jnp.einsum('ktc,kdc->td', stacked, in_back, preferred_el...  179 us
    reduce_scatter x2, waiting for transfers between devices, local(): lax.psum_scatter(jnp.dot(hidden_act, down_full, preferred_element_type=jn...  179 us
    reduce_scatter x2, waiting for transfers between devices, local(): lax.psum_scatter(jnp.dot(mixed, out_full, preferred_element_type=jnp.floa...  173 us
    reduce_scatter x2, waiting for transfers between devices, local(): lax.psum_scatter(jnp.einsum('ktf,kdf->td', pair_grad, pair_back, preferre...  155 us
    all_gather x2, waiting for transfers between devices, local(): lax.all_gather(normed_two.astype(jnp.bfloat16), 'mp', axis=0, tiled=True)  94 us
    reduce_scatter x1, waiting for transfers between devices, local(): lax.psum_scatter(pair_total, 'seq', scatter_dimension=1, tiled=True)  90.7 us
    all_gather x2, waiting for transfers between devices, local(): lax.all_gather(normed.astype(jnp.bfloat16), 'mp', axis=0, tiled=True)  86.7 us
    all_gather x2, waiting for transfers between devices, local(): lax.all_gather(top_grad.astype(jnp.bfloat16), 'mp', axis=0, tiled=True)  82.2 us
  transfers between devices with their start and end apart: 28, of which 26 were waited for; matrix products, arithmetic and copies ran while one was open for 11% of the time, Pallas kernels for 0%

commit v1 on v0

--- a/solution.py
+++ b/solution.py
@@ -10,6 +10,11 @@
     count = lax.axis_size(axis)
     leading, last = (max(0, -steps), min(count, count - steps))
     return lax.ppermute(value, axis, [(source, source + steps) for source in range(leading, last)])
+
+
+def scatter_sum(value, axis, dim):
+    low = value.astype(jnp.bfloat16)
+    return lax.psum_scatter(low, axis, scatter_dimension=dim, tiled=True).astype(jnp.float32)
 
 
 def normalize(values, gain):
@@ -85,11 +90,10 @@
                 + local_taps[offset] * extended[taps - 1 - offset : taps - 1 - offset + block_rows]
             )
         mixed = (c_gate * conv_out).astype(jnp.bfloat16)
-        mix_share = lax.psum_scatter(
+        mix_share = scatter_sum(
             jnp.dot(mixed, out_full, preferred_element_type=jnp.float32),
             "mp",
-            scatter_dimension=0,
-            tiled=True,
+             0,
         )
         middle = source + mix_share
         normed_two, scale_mlp = normalize(middle, gain_mlp)
@@ -99,11 +103,10 @@
         up_part = gated[1]
         activated = jax.nn.silu(gate_part)
         hidden_act = (activated * up_part).astype(jnp.bfloat16)
-        mlp_share = lax.psum_scatter(
+        mlp_share = scatter_sum(
             jnp.dot(hidden_act, down_full, preferred_element_type=jnp.float32),
             "mp",
-            scatter_dimension=0,
-            tiled=True,
+             0,
         )
         outputs.append((mask_rows * (middle + mlp_share)).astype(jnp.bfloat16))
         in_back, out_back, pair_back, down_back = (
@@ -127,11 +130,10 @@
         pair_total = pair_total + jnp.einsum(
             "td,ktf->kdf", mlp_rows, pair_grad, preferred_element_type=jnp.float32
         )
-        normed_two_grad = lax.psum_scatter(
+        normed_two_grad = scatter_sum(
             jnp.einsum("ktf,kdf->td", pair_grad, pair_back, preferred_element_type=jnp.float32),
             "mp",
-            scatter_dimension=0,
-            tiled=True,
+             0,
         )
         middle_grad, gain_part = norm_back(normed_two_grad, middle, scale_mlp, gain_mlp)
         gain_mlp_total = gain_mlp_total + gain_part
@@ -161,20 +163,19 @@
         in_total = in_total + jnp.einsum(
             "td,ktc->kdc", normed_rows, stacked, preferred_element_type=jnp.float32
         )
-        normed_grad = lax.psum_scatter(
+        normed_grad = scatter_sum(
             jnp.einsum("ktc,kdc->td", stacked, in_back, preferred_element_type=jnp.float32),
             "mp",
-            scatter_dimension=0,
-            tiled=True,
+             0,
         )
         source_grad, gain_part = norm_back(normed_grad, source, scale_mix, gain_mix)
         gain_mix_total = gain_mix_total + gain_part
         input_grads.append(source_grad + middle_grad)
     in_grad, out_grad, pair_out, down_out = (
-        lax.psum_scatter(in_total, "seq", scatter_dimension=1, tiled=True),
-        lax.psum_scatter(out_total, "seq", scatter_dimension=1, tiled=True),
-        lax.psum_scatter(pair_total, "seq", scatter_dimension=1, tiled=True),
-        lax.psum_scatter(down_total, "seq", scatter_dimension=1, tiled=True),
+        scatter_sum(in_total, "seq", 1),
+        scatter_sum(out_total, "seq", 1),
+        scatter_sum(pair_total, "seq", 1),
+        scatter_sum(down_total, "seq", 1),
     )
     taps_full = lax.dynamic_update_slice_in_dim(
         jnp.zeros((taps, width), jnp.float32), taps_total, model_pos * channels, 1

time: 1770 us -> 1310 us (0.74)
  waiting for transfers between devices: 1430 us -> 972 us
    reduce_scatter x12, waiting for transfers between devices: 927 us -> 519 us  [scatter_sum(): lax.psum_scatter(low, axis, scatter_dimension=dim, tiled=True)]
    all_gather x2, waiting for transfers between devices: 94 us -> 69.3 us  [local(): lax.all_gather(normed_two.astype(jnp.bfloat16), 'mp', axis=0, tiled=True)]
  transfers between devices with their start and end apart: 28 -> 28, of which waited for: 26 -> 25; matrix products, arithmetic and copies ran while one was open for 11% -> 18% of each run, Pallas kernels for 0% -> 0%
where the time goes in v1:
time: 1310 us; the launch traced here: 1300 us
  waiting for transfers between devices  972 us (74%)
  matrix products  198 us (15%)
  other arithmetic  43.6 us (3%)
  blocking collectives  38.7 us (3%)
  local copies, waits for them, and re-layouts  19 us (1%)
  between operations  15.5 us (1%)
    reduce_scatter x12, waiting for transfers between devices, scatter_sum(): lax.psum_scatter(low, axis, scatter_dimension=dim, tiled=True)  519 us
    all_gather x2, waiting for transfers between devices, local(): lax.all_gather(normed.astype(jnp.bfloat16), 'mp', axis=0, tiled=True)  86.1 us
    all_gather x2, waiting for transfers between devices, local(): lax.all_gather(top_grad.astype(jnp.bfloat16), 'mp', axis=0, tiled=True)  82.3 us
    all_gather x1, waiting for transfers between devices, local(): lax.all_gather(gate_up, 'seq', axis=1, tiled=True)  77.9 us
    all_gather x2, waiting for transfers between devices, local(): lax.all_gather(normed_two.astype(jnp.bfloat16), 'mp', axis=0, tiled=True)  69.3 us
    all_gather x1, waiting for transfers between devices, local(): lax.all_gather(mixer_in, 'seq', axis=1, tiled=True)  43.2 us
    psum x1, blocking collectives, local(): lax.psum((gain_mix_total, gain_mlp_total, taps_full), ('seq', 'mp'))  38.7 us
    all_gather x1, waiting for transfers between devices, local(): lax.all_gather(mlp_down, 'seq', axis=1, tiled=True)  38.6 us
  transfers between devices with their start and end apart: 28, of which 25 were waited for; matrix products, arithmetic and copies ran while one was open for 18% of the time, Pallas kernels for 0%

profile of v1, /device:TPU:0, one launch (start us, length us, event | category | flops | bytes accessed | tf_op | source)
XLA Modules:
  0.0 1298.1 jit_solution(5095437056916648835)
XLA Ops:
  9.5 2.5 fusion.76
  13.3 43.2 %all-gather.15.cloned.1.call-done = bf16[3,2048,256]{2,1,0:T(8,128)(2,1)} async-done(((bf16[3,512,256]{2,1,0:T(8,128)(2,1)}), bf16[3,2048,256]{2,1,0:T(8,128)(2,1)}) %all-gather.15.cloned.1.call-update) | async-done | bytes 3145744 | tf_op jit(solution)/shard_map/all_gather | solution.py:68
  56.6 49.4 %all-gather.13.cloned.1.call-done = bf16[1024,2048]{1,0:T(8,128)(2,1)} async-done(((bf16[128,2048]{1,0:T(8,128)(2,1)}), bf16[1024,2048]{1,0:T(8,128)(2,1)}) %all-gather.13.cloned.1.call-update) | async-done | bytes 4194320 | tf_op jit(solution)/shard_map/all_gather | solution.py:76
  105.9 6.1 fusion.32
  113.9 3.4 collective-permute-start
  117.2 36.8 %all-gather.25.cloned.1.call-done = bf16[1024,2048]{1,0:T(8,128)(2,1)} async-done(((bf16[128,2048]{1,0:T(8,128)(2,1)}), bf16[1024,2048]{1,0:T(8,128)(2,1)}) %all-gather.25.cloned.1.call-update) | async-done | bytes 4194320 | tf_op jit(solution)/shard_map/all_gather | solution.py:76
  154.0 6.1 fusion.35
  160.3 3.4 collective-permute-start.1
  165.6 3.3 multiply_convert_fusion.17
  168.9 12.0 all-gather.17.cloned.1.call-done
  180.9 4.6 convolution_convert_fusion.1
  185.6 3.3 convolution_convert_fusion
  189.8 45.9 %reduce-scatter.13.cloned.1.call-done = bf16[128,2048]{1,0:T(8,128)(2,1)} async-done(((bf16[1024,2048]{1,0:T(8,128)(2,1)}), bf16[128,2048]{1,0:T(8,128)(2,1)}) %reduce-scatter.13.cloned.1.call-update) | async-done | bytes 524304 | tf_op jit(solution)/shard_map/reduce_scatter | solution.py:17
  235.7 50.3 %reduce-scatter.17.cloned.1.call-done = bf16[128,2048]{1,0:T(8,128)(2,1)} async-done(((bf16[1024,2048]{1,0:T(8,128)(2,1)}), bf16[128,2048]{1,0:T(8,128)(2,1)}) %reduce-scatter.17.cloned.1.call-update) | async-done | bytes 524304 | tf_op jit(solution)/shard_map/reduce_scatter | solution.py:17
  287.7 2.5 multiply_convert_fusion.16
  295.7 77.9 %all-gather.21.cloned.1.call-done = bf16[2,2048,1024]{2,1,0:T(8,128)(2,1)} async-done(((bf16[2,512,1024]{2,1,0:T(8,128)(2,1)}), bf16[2,2048,1024]{2,1,0:T(8,128)(2,1)}) %all-gather.21.cloned.1.call-update) | async-done | bytes 8388624 | tf_op jit(solution)/shard_map/all_gather | solution.py:70
  373.7 49.4 %all-gather.19.cloned.1.call-done = bf16[1024,2048]{1,0:T(8,128)(2,1)} async-done(((bf16[128,2048]{1,0:T(8,128)(2,1)}), bf16[1024,2048]{1,0:T(8,128)(2,1)}) %all-gather.19.cloned.1.call-update) | async-done | bytes 4194320 | tf_op jit(solution)/shard_map/all_gather | solution.py:100
  423.0 14.5 %fusion.18 = f32[2,1024,1024]{2,1,0:T(8,128)} fusion(bf16[2,2048,1024]{2,1,0:T(8,128)(2,1)} %all-gather.21.cloned.1.call-done, bf16[1024,2048]{1,0:T(8,128)(2,1)} %all-gather.19.cloned.1.call-done), kind=kOutput, calls=%fused_computation.43 | convolution fusion | flops 8589934592 | bytes 20971520 | tf_op jit(solution)/shard_map/td,kdf->ktf/dot_general | solution.py:101
  437.6 38.6 %all-gather.23.cloned.1.call-done = bf16[1024,2048]{1,0:T(8,128)(2,1)} async-done(((bf16[1024,512]{1,0:T(8,128)(2,1)}), bf16[1024,2048]{1,0:T(8,128)(2,1)}) %all-gather.23.cloned.1.call-update) | async-done | bytes 4194320 | tf_op jit(solution)/shard_map/all_gather | solution.py:71
  476.2 49.2 %all-gather.29.cloned.1.call-done = bf16[1024,2048]{1,0:T(8,128)(2,1)} async-done(((bf16[128,2048]{1,0:T(8,128)(2,1)}), bf16[1024,2048]{1,0:T(8,128)(2,1)}) %all-gather.29.cloned.1.call-update) | async-done | bytes 4194320 | tf_op jit(solution)/shard_map/all_gather | solution.py:119
  525.4 13.1 %fusion.30 = (bf16[1,1024,1024]{2,1,0:T(8,128)(2,1)S(1)}, bf16[1,1024,1024]{2,1,0:T(8,128)(2,1)S(1)}, bf16[1024,1024]{1,0:T(8,128)(2,1)}) fusion(f32[2,1024,1024]{2,1,0:T(8,128)} %fusion.18, bf16[1024,2048]{1,0:T(8,128)(2,1)} %all-gather.29.cloned.1.call-done, bf16[1024,2048]{1,0:T(8,128)(2,1)} %all-gather.23.cloned.1.call-done), kind=kOutput, calls=%fused_computation.51 | convolution fusion | flops 4310695936 | bytes 23068672 | tf_op jit(solution)/shard_map/td,fd->tf/dot_general | solution.py:123
  540.5 12.6 bitcast_convert_fusion.3
  553.5 20.0 %all-gather.27.cloned.1.call-done = bf16[1024,2048]{1,0:T(8,128)(2,1)} async-done(((bf16[128,2048]{1,0:T(8,128)(2,1)}), bf16[1024,2048]{1,0:T(8,128)(2,1)}) %all-gather.27.cloned.1.call-update) | async-done | bytes 4194320 | tf_op jit(solution)/shard_map/all_gather | solution.py:100
  573.4 14.5 %fusion.21 = f32[2,1024,1024]{2,1,0:T(8,128)} fusion(bf16[2,2048,1024]{2,1,0:T(8,128)(2,1)} %all-gather.21.cloned.1.call-done, bf16[1024,2048]{1,0:T(8,128)(2,1)} %all-gather.27.cloned.1.call-done), kind=kOutput, calls=%fused_computation.44 | convolution fusion | flops 8589934592 | bytes 20971520 | tf_op jit(solution)/shard_map/td,kdf->ktf/dot_general | solution.py:101
  587.9 33.1 %all-gather.33.cloned.1.call-done = bf16[1024,2048]{1,0:T(8,128)(2,1)} async-done(((bf16[128,2048]{1,0:T(8,128)(2,1)}), bf16[1024,2048]{1,0:T(8,128)(2,1)}) %all-gather.33.cloned.1.call-update) | async-done | bytes 4194320 | tf_op jit(solution)/shard_map/all_gather | solution.py:119
  621.0 13.1 %fusion.31 = (bf16[1,1024,1024]{2,1,0:T(8,128)(2,1)S(1)}, bf16[1,1024,1024]{2,1,0:T(8,128)(2,1)S(1)}, bf16[1024,1024]{1,0:T(8,128)(2,1)}) fusion(f32[2,1024,1024]{2,1,0:T(8,128)} %fusion.21, bf16[1024,2048]{1,0:T(8,128)(2,1)} %all-gather.33.cloned.1.call-done, bf16[1024,2048]{1,0:T(8,128)(2,1)} %all-gather.23.cloned.1.call-done), kind=kOutput, calls=%fused_computation.52 | convolution fusion | flops 4310695936 | bytes 23068672 | tf_op jit(solution)/shard_map/td,fd->tf/dot_general | solution.py:123
  636.2 12.7 bitcast_convert_fusion.1
  649.3 9.3 convolution_convert_fusion.2
  658.7 9.4 convolution_convert_fusion.3
  668.2 4.2 reduce-scatter.21.cloned.1.call-done
  672.4 50.3 %reduce-scatter.25.cloned.1.call-done = bf16[128,2048]{1,0:T(8,128)(2,1)} async-done(((bf16[1024,2048]{1,0:T(8,128)(2,1)}), bf16[128,2048]{1,0:T(8,128)(2,1)}) %reduce-scatter.25.cloned.1.call-update) | async-done | bytes 524304 | tf_op jit(solution)/shard_map/reduce_scatter | solution.py:17
  722.7 2.1 fusion.74
  724.9 48.2 %reduce-scatter.19.cloned.1.call-done = bf16[128,2048]{1,0:T(8,128)(2,1)} async-done(((bf16[1024,2048]{1,0:T(8,128)(2,1)}), bf16[128,2048]{1,0:T(8,128)(2,1)}) %reduce-scatter.19.cloned.1.call-update) | async-done | bytes 524304 | tf_op jit(solution)/shard_map/reduce_scatter | solution.py:17
  773.0 50.3 %reduce-scatter.15.cloned.1.call-done = bf16[128,2048]{1,0:T(8,128)(2,1)} async-done(((bf16[1024,2048]{1,0:T(8,128)(2,1)}), bf16[128,2048]{1,0:T(8,128)(2,1)}) %reduce-scatter.15.cloned.1.call-update) | async-done | bytes 524304 | tf_op jit(solution)/shard_map/reduce_scatter | solution.py:17
  823.4 4.7 fusion.114
  828.7 7.2 fusion.123
  835.9 6.1 add_convert_fusion.1
  843.7 15.1 %fusion.8 = f32[2,1024,2048]{2,1,0:T(8,128)} fusion(bf16[1024,2048]{1,0:T(8,128)(2,1)} %all-gather.19.cloned.1.call-done, bf16[1,1024,1024]{2,1,0:T(8,128)(2,1)} %copy-done.54, bf16[1,1024,1024]{2,1,0:T(8,128)(2,1)S(1)} %copy-done.53), kind=kOutput, calls=%fused_computation.21 | convolution fusion | flops 8592031744 | bytes 25165824 | tf_op jit(solution)/shard_map/td,ktf->kdf/dot_general | solution.py:130
  858.8 15.6 %fusion = bf16[2,2048,1024]{1,2,0:T(8,128)(2,1)} fusion(f32[2,1024,2048]{2,1,0:T(8,128)} %fusion.8, bf16[1024,2048]{1,0:T(8,128)(2,1)S(1)} %copy-done.47, bf16[1,1024,1024]{2,1,0:T(8,128)(2,1)} %copy-done.57, bf16[1,1024,1024]{2,1,0:T(8,128)(2,1)S(1)} %copy-done.56), kind=kOutput, calls=%fused_computation.1 | convolution fusion | flops 8600420352 | bytes 33554432 | tf_op jit(solution)/shard_map/td,ktf->kdf/dot_general | solution.py:130
  875.7 3.5 fusion.120
  879.2 2.9 multiply_reduce_fusion.4
  883.8 37.1 %all-gather.35.cloned.1.call-done = bf16[1024,2048]{1,0:T(8,128)(2,1)} async-done(((bf16[128,2048]{1,0:T(8,128)(2,1)}), bf16[1024,2048]{1,0:T(8,128)(2,1)}) %all-gather.35.cloned.1.call-update) | async-done | bytes 4194320 | tf_op jit(solution)/shard_map/all_gather | solution.py:141
  920.9 3.9 fusion.121
  924.8 2.6 multiply_reduce_fusion.1
  931.3 2.3 fusion.27
  934.2 2.3 fusion.96
  938.2 2.0 fusion.101
  940.2 3.6 fusion.4
  943.9 5.1 fusion.24
  949.3 7.6 bitcast_convert_fusion.2
  957.9 6.9 bitcast_convert_fusion
  964.9 10.9 reduce-scatter.35.cloned.1.call-done
  975.9 2.8 convert_element_type.225
  979.8 85.6 %reduce-scatter.33.cloned.1.call-done = bf16[2,512,1024]{1,2,0:T(8,128)(2,1)} async-done(((bf16[2,2048,1024]{1,2,0:T(8,128)(2,1)}), bf16[2,512,1024]{1,2,0:T(8,128)(2,1)}) %reduce-scatter.33.cloned.1.call-update) | async-done | bytes 2097168 | tf_op jit(solution)/shard_map/reduce_scatter | solution.py:17
  1065.5 4.1 copy.24
  1069.6 27.1 %reduce-scatter.31.cloned.1.call-done = bf16[256,512]{1,0:T(8,128)(2,1)} async-done(((bf16[256,2048]{1,0:T(8,128)(2,1)}), bf16[256,512]{1,0:T(8,128)(2,1)}) %reduce-scatter.31.cloned.1.call-update) | async-done | bytes 262160 | tf_op jit(solution)/shard_map/reduce_scatter | solution.py:17
  1096.7 1.8 convert_element_type.220
  1098.5 45.4 %reduce-scatter.29.cloned.1.call-done = bf16[3,512,256]{1,2,0:T(8,128)(2,1)} async-done(((bf16[3,2048,256]{1,2,0:T(8,128)(2,1)}), bf16[3,512,256]{1,2,0:T(8,128)(2,1)}) %reduce-scatter.29.cloned.1.call-update) | async-done | bytes 786448 | tf_op jit(solution)/shard_map/reduce_scatter | solution.py:17
  1143.9 2.5 copy.23
  1146.5 49.9 %reduce-scatter.23.cloned.1.call-done = bf16[128,2048]{1,0:T(8,128)(2,1)} async-done(((bf16[1024,2048]{1,0:T(8,128)(2,1)}), bf16[128,2048]{1,0:T(8,128)(2,1)}) %reduce-scatter.23.cloned.1.call-update) | async-done | bytes 524304 | tf_op jit(solution)/shard_map/reduce_scatter | solution.py:17
  1196.4 50.4 %reduce-scatter.27.cloned.1.call-done = bf16[128,2048]{1,0:T(8,128)(2,1)} async-done(((bf16[1024,2048]{1,0:T(8,128)(2,1)}), bf16[128,2048]{1,0:T(8,128)(2,1)}) %reduce-scatter.27.cloned.1.call-update) | async-done | bytes 524304 | tf_op jit(solution)/shard_map/reduce_scatter | solution.py:17
  1246.8 2.0 fusion.78
  1248.8 1.8 fusion.70
  1252.1 38.7 %all-reduce = (f32[2048]{0:T(1024)}, f32[2048]{0:T(1024)}, f32[3,2048]{1,0:T(4,128)}) all-reduce(f32[2048]{0:T(1024)S(1)} %add.196, f32[2048]{0:T(1024)S(1)} %add.197, f32[3,2048]{1,0:T(4,128)S(1)} %fusion.102), channel_id=1, replica_groups=mesh['seq'=4,'mp'=8] {'seq','mp'}, use_global_device_ids=true, to_apply=%region_18.19 | all-reduce | flops 10240 | bytes 81920 | tf_op jit(solution)/shard_map/psum | solution.py:183
  (198 shorter events, 35.3 us)
Async XLA Ops:
  7.2 49.4 %all-gather.15.cloned.1.call-start = ((), (), s32[]{:S(2)}) async-start(), calls=%async_computation.13 | async-start | bytes 3932160 | tf_op jit(solution)/shard_map/all_gather | solution.py:68
  7.9 98.0 %all-gather.13.cloned.1.call-start = ((), (), s32[]{:S(2)}) async-start(), calls=%async_computation.12 | async-start | bytes 4718592 | tf_op jit(solution)/shard_map/all_gather | solution.py:76
  9.5 96.5 %copy-start.37 = (f32[128]{0:T(128)}, f32[128]{0:T(128)S(1)}, u32[]{:S(2)}) copy-start(f32[128]{0:T(128)S(1)} %get-tuple-element.88) | copy-start | bytes 1540
  9.5 96.5 %copy-start.39 = (f32[128]{0:T(128)}, f32[128]{0:T(128)S(1)}, u32[]{:S(2)}) copy-start(f32[128]{0:T(128)S(1)} %get-tuple-element.89) | copy-start | bytes 1540
  12.0 142.0 %all-gather.25.cloned.1.call-start = ((), (), s32[]{:S(2)}) async-start(), calls=%async_computation.20 | async-start | bytes 4718592 | tf_op jit(solution)/shard_map/all_gather | solution.py:76
  12.7 168.2 %all-gather.17.cloned.1.call-start = ((), (), s32[]{:S(2)}) async-start(), calls=%async_computation.14 | async-start | bytes 1310720 | tf_op jit(solution)/shard_map/all_gather | solution.py:69
  13.3 222.4 %reduce-scatter.13.cloned.1.call-start = ((), (), s32[]{:S(2)}) async-start(), calls=%async_computation.15 | async-start | bytes 4718592 | tf_op jit(solution)/shard_map/reduce_scatter | solution.py:17
  113.8 51.2 %copy-start.5 = (f32[1024,256]{1,0:T(8,128)}, f32[1024,256]{1,0:T(8,128)S(1)}, u32[]{:S(2)}) copy-start(f32[1024,256]{1,0:T(8,128)S(1)} %fusion.89) | copy-start | bytes 3145732
  113.9 50.7 %collective-permute-start = (f32[2,256]{1,0:T(2,128)S(1)}, f32[2,256]{1,0:T(2,128)S(1)}, u32[]{:S(2)}, u32[]{:S(2)}) collective-permute-start(f32[2,256]{1,0:T(2,128)S(1)} %slice.140), channel_id=1, source_target_pairs={{0,8},{8,16},{16,24},{1,9},{9,17},{17,25},{2,10},{10,18},{18,26},{... | collective-permute-start | bytes 6152 | tf_op jit(solution)/shard_map/ppermute | solution.py:12
  160.1 4.8 copy-start.2
  160.3 25.2 %copy-start.3 = (f32[1024,256]{1,0:T(8,128)}, f32[1024,256]{1,0:T(8,128)S(1)}, u32[]{:S(2)}) copy-start(f32[1024,256]{1,0:T(8,128)S(1)} %fusion.91) | copy-start | bytes 3145732
  160.3 4.7 collective-permute-start.1
  164.6 24.4 %copy-start.43 = (f32[2,256]{1,0:T(2,128)}, f32[2,256]{1,0:T(2,128)S(1)}, u32[]{:S(2)}) copy-start(f32[2,256]{1,0:T(2,128)S(1)} %collective-permute-done) | copy-start | bytes 6148
  168.9 16.7 %copy-start.20 = (bf16[1024,256]{1,0:T(8,128)(2,1)}, bf16[1024,256]{1,0:T(8,128)(2,1)S(1)}, u32[]{:S(2)}) copy-start(bf16[1024,256]{1,0:T(8,128)(2,1)S(1)} %get-tuple-element.53) | copy-start | bytes 1572868
  168.9 16.7 %copy-start.18 = (bf16[1024,256]{1,0:T(8,128)(2,1)}, bf16[1024,256]{1,0:T(8,128)(2,1)S(1)}, u32[]{:S(2)}) copy-start(bf16[1024,256]{1,0:T(8,128)(2,1)S(1)} %get-tuple-element.82) | copy-start | bytes 1572868
  180.9 4.7 copy-start.16
  185.5 100.5 %reduce-scatter.17.cloned.1.call-start = ((), (), s32[]{:S(2)}) async-start(), calls=%async_computation.21 | async-start | bytes 4718592 | tf_op jit(solution)/shard_map/reduce_scatter | solution.py:17
  188.9 97.1 %copy-start = (bf16[2,128,2048]{2,1,0:T(8,128)(2,1)S(1)}, bf16[2,128,2048]{2,1,0:T(8,128)(2,1)}, u32[]{:S(2)}) copy-start(bf16[2,128,2048]{2,1,0:T(8,128)(2,1)} %param.10) | copy-start | bytes 3145732
  188.9 98.8 %copy-start.29 = (f32[2048]{0:T(1024)S(1)}, f32[2048]{0:T(1024)}, u32[]{:S(2)}) copy-start(f32[2048]{0:T(1024)} %param.14) | copy-start | bytes 24580
  189.0 102.1 %copy-start.45 = (s32[2]{0:T(128)S(1)}, s32[2]{0:T(128)}, u32[]{:S(2)}) copy-start(s32[2]{0:T(128)} %param.12) | copy-start | bytes 28
  189.0 104.0 %copy-start.12 = (bf16[2,128,2048]{2,1,0:T(8,128)(2,1)S(1)}, bf16[2,128,2048]{2,1,0:T(8,128)(2,1)}, u32[]{:S(2)}) copy-start(bf16[2,128,2048]{2,1,0:T(8,128)(2,1)} %param.11) | copy-start | bytes 3145732
  189.0 184.7 %all-gather.21.cloned.1.call-start = ((), (), s32[]{:S(2)}) async-start(), calls=%async_computation.17 | async-start | bytes 10485760 | tf_op jit(solution)/shard_map/all_gather | solution.py:70
  189.7 233.3 %all-gather.19.cloned.1.call-start = ((), (), s32[]{:S(2)}) async-start(), calls=%async_computation.16 | async-start | bytes 4718592 | tf_op jit(solution)/shard_map/all_gather | solution.py:100
  290.3 185.9 %all-gather.23.cloned.1.call-start = ((), (), s32[]{:S(2)}) async-start(), calls=%async_computation.18 | async-start | bytes 5242880 | tf_op jit(solution)/shard_map/all_gather | solution.py:71
  291.0 234.4 %all-gather.29.cloned.1.call-start = ((), (), s32[]{:S(2)}) async-start(), calls=%async_computation.24 | async-start | bytes 4718592 | tf_op jit(solution)/shard_map/all_gather | solution.py:119
  294.2 279.2 %all-gather.27.cloned.1.call-start = ((), (), s32[]{:S(2)}) async-start(), calls=%async_computation.22 | async-start | bytes 4718592 | tf_op jit(solution)/shard_map/all_gather | solution.py:100
  295.0 326.1 %all-gather.33.cloned.1.call-start = ((), (), s32[]{:S(2)}) async-start(), calls=%async_computation.28 | async-start | bytes 4718592 | tf_op jit(solution)/shard_map/all_gather | solution.py:119
  295.5 376.9 %reduce-scatter.21.cloned.1.call-start = ((), (), s32[]{:S(2)}) async-start(), calls=%async_computation.25 | async-start | bytes 4718592 | tf_op jit(solution)/shard_map/reduce_scatter | solution.py:17
  553.2 169.5 %reduce-scatter.25.cloned.1.call-start = ((), (), s32[]{:S(2)}) async-start(), calls=%async_computation.29 | async-start | bytes 4718592 | tf_op jit(solution)/shard_map/reduce_scatter | solution.py:17
  648.9 124.2 %reduce-scatter.19.cloned.1.call-start = ((), (), s32[]{:S(2)}) async-start(), calls=%async_computation.23 | async-start | bytes 4718592 | tf_op jit(solution)/shard_map/reduce_scatter | solution.py:17
  658.7 164.7 %reduce-scatter.15.cloned.1.call-start = ((), (), s32[]{:S(2)}) async-start(), calls=%async_computation.19 | async-start | bytes 4718592 | tf_op jit(solution)/shard_map/reduce_scatter | solution.py:17
  668.1 54.6 %copy-start.7 = (bf16[128,2048]{1,0:T(8,128)(2,1)S(1)}, bf16[128,2048]{1,0:T(8,128)(2,1)}, u32[]{:S(2)}) copy-start(bf16[128,2048]{1,0:T(8,128)(2,1)} %reduce-scatter.13.cloned.1.call-done) | copy-start | bytes 1572868
  668.1 54.6 %copy-start.8 = (bf16[128,2048]{1,0:T(8,128)(2,1)S(1)}, bf16[128,2048]{1,0:T(8,128)(2,1)}, u32[]{:S(2)}) copy-start(bf16[128,2048]{1,0:T(8,128)(2,1)} %reduce-scatter.17.cloned.1.call-done) | copy-start | bytes 1572868
  668.1 206.4 %all-gather.31.cloned.1.call-start = ((), (), s32[]{:S(2)}) async-start(), calls=%async_computation.26 | async-start | bytes 4718592 | tf_op jit(solution)/shard_map/all_gather | solution.py:141
  828.1 92.8 %all-gather.35.cloned.1.call-start = ((), (), s32[]{:S(2)}) async-start(), calls=%async_computation.30 | async-start | bytes 4718592 | tf_op jit(solution)/shard_map/all_gather | solution.py:141
  828.7 7.3 copy-start.51
  828.7 147.2 %reduce-scatter.35.cloned.1.call-start = ((), (), s32[]{:S(2)}) async-start(), calls=%async_computation.35 | async-start | bytes 5242880 | tf_op jit(solution)/shard_map/reduce_scatter | solution.py:17
  828.7 7.2 copy-start.48
  842.1 223.4 %reduce-scatter.33.cloned.1.call-start = ((), (), s32[]{:S(2)}) async-start(), calls=%async_computation.34 | async-start | bytes 10485760 | tf_op jit(solution)/shard_map/reduce_scatter | solution.py:17
  843.7 15.1 %copy-start.47 = (bf16[1024,2048]{1,0:T(8,128)(2,1)S(1)}, bf16[1024,2048]{1,0:T(8,128)(2,1)}, u32[]{:S(2)}) copy-start(bf16[1024,2048]{1,0:T(8,128)(2,1)} %all-gather.27.cloned.1.call-done) | copy-start | bytes 12582916
  843.7 15.1 %copy-start.56 = (bf16[1,1024,1024]{2,1,0:T(8,128)(2,1)S(1)}, bf16[1,1024,1024]{2,1,0:T(8,128)(2,1)}, u32[]{:S(2)}) copy-start(bf16[1,1024,1024]{2,1,0:T(8,128)(2,1)} %copy-done.55) | copy-start | bytes 6291460
  874.5 4.7 copy-start.6
  874.5 4.7 copy-start.44
  874.5 222.2 %reduce-scatter.31.cloned.1.call-start = ((), (), s32[]{:S(2)}) async-start(), calls=%async_computation.33 | async-start | bytes 1310720 | tf_op jit(solution)/shard_map/reduce_scatter | solution.py:17
  882.1 42.7 %copy-start.4 = (f32[1024,256]{1,0:T(8,128)S(1)}, f32[1024,256]{1,0:T(8,128)}, u32[]{:S(2)}) copy-start(f32[1024,256]{1,0:T(8,128)} %copy-done.3) | copy-start | bytes 3145732
  882.1 42.7 %copy-start.42 = (f32[2,256]{1,0:T(2,128)S(1)}, f32[2,256]{1,0:T(2,128)}, u32[]{:S(2)}) copy-start(f32[2,256]{1,0:T(2,128)} %copy-done.41) | copy-start | bytes 6148
  882.1 51.5 %collective-permute-start.2 = (f32[2,256]{1,0:T(2,128)S(1)}, f32[2,256]{1,0:T(2,128)S(1)}, u32[]{:S(2)}, u32[]{:S(2)}) collective-permute-start(f32[2,256]{1,0:T(2,128)S(1)} %slice.153), channel_id=1, source_target_pairs={{8,0},{16,8},{24,16},{9,1},{17,9},{25,17},{10,2},{18,10},{26,18},{... | collective-permute-start | bytes 6152 | tf_op jit(solution)/shard_map/ppermute | solution.py:12
  920.9 3.9 copy-start.15
  924.7 5.2 copy-start.21
  924.7 5.2 copy-start.49
  927.4 3.8 copy-start.50
  928.4 5.7 collective-permute-start.3
  933.6 210.3 %reduce-scatter.29.cloned.1.call-start = ((), (), s32[]{:S(2)}) async-start(), calls=%async_computation.32 | async-start | bytes 3932160 | tf_op jit(solution)/shard_map/reduce_scatter | solution.py:17
  936.4 7.4 copy-start.25
  936.4 7.4 copy-start.28
  949.0 247.4 %reduce-scatter.23.cloned.1.call-start = ((), (), s32[]{:S(2)}) async-start(), calls=%async_computation.27 | async-start | bytes 4718592 | tf_op jit(solution)/shard_map/reduce_scatter | solution.py:17
  956.9 289.9 %reduce-scatter.27.cloned.1.call-start = ((), (), s32[]{:S(2)}) async-start(), calls=%async_computation.31 | async-start | bytes 4718592 | tf_op jit(solution)/shard_map/reduce_scatter | solution.py:17
  964.9 13.8 %copy-start.22 = (bf16[1,128,2048]{2,1,0:T(8,128)(2,1)S(1)}, bf16[1,128,2048]{2,1,0:T(8,128)(2,1)}, u32[]{:S(2)}) copy-start(bf16[1,128,2048]{2,1,0:T(8,128)(2,1)} %get-tuple-element.65) | copy-start | bytes 1572868
  964.9 13.8 %copy-start.23 = (bf16[1,128,2048]{2,1,0:T(8,128)(2,1)S(1)}, bf16[1,128,2048]{2,1,0:T(8,128)(2,1)}, u32[]{:S(2)}) copy-start(bf16[1,128,2048]{2,1,0:T(8,128)(2,1)} %get-tuple-element.66) | copy-start | bytes 1572868
  979.8 267.0 %copy-start.30 = (f32[2048]{0:T(1024)S(1)}, f32[2048]{0:T(1024)}, u32[]{:S(2)}) copy-start(f32[2048]{0:T(1024)} %param.13) | copy-start | bytes 24580
  979.8 267.0 %copy-start.38 = (f32[128]{0:T(128)S(1)}, f32[128]{0:T(128)}, u32[]{:S(2)}) copy-start(f32[128]{0:T(128)} %copy-done.37) | copy-start | bytes 1540
  979.8 267.0 %copy-start.40 = (f32[128]{0:T(128)S(1)}, f32[128]{0:T(128)}, u32[]{:S(2)}) copy-start(f32[128]{0:T(128)} %copy-done.39) | copy-start | bytes 1540
  1069.6 179.2 %copy-start.13 = (f32[128,2048]{1,0:T(8,128)S(1)}, f32[128,2048]{1,0:T(8,128)}, u32[]{:S(2)}) copy-start(f32[128,2048]{1,0:T(8,128)} %get-tuple-element.48) | copy-start | bytes 3145732
  1069.6 179.2 %copy-start.14 = (f32[128,2048]{1,0:T(8,128)S(1)}, f32[128,2048]{1,0:T(8,128)}, u32[]{:S(2)}) copy-start(f32[128,2048]{1,0:T(8,128)} %get-tuple-element.64) | copy-start | bytes 3145732
  (22 other events, 45.6 us)
Sparse Core Ops, SparseCore 0:
  9.9 46.6 all-gather.14
  58.7 47.1 all-gather.12
  108.1 45.8 all-gather.24
  155.7 25.1 all-gather.16
  185.7 50.0 reduce-scatter.12
  237.9 48.1 reduce-scatter.16
  287.9 85.7 all-gather.20
  375.8 47.1 all-gather.18
  424.9 51.2 all-gather.22
  478.2 47.1 all-gather.28
  527.6 45.8 all-gather.26
  574.9 46.0 all-gather.32
  623.9 48.4 reduce-scatter.20
  674.5 48.1 reduce-scatter.24
  724.9 48.1 reduce-scatter.18
  775.2 48.1 reduce-scatter.14
  828.2 45.2 all-gather.30
  875.0 45.8 all-gather.34
  924.4 51.4 reduce-scatter.34
  979.1 86.3 reduce-scatter.32
  1068.9 27.6 reduce-scatter.30
  1099.9 43.9 reduce-scatter.28
  1146.3 49.9 reduce-scatter.22
  1198.6 48.1 reduce-scatter.26

commit v2 on v1

v2 whole, which is shorter than its diff:
```python
import functools

import jax
import jax.numpy as jnp
from jax import lax
from jax.experimental import pallas as pl
from jax.experimental.pallas import tpu as pltpu
from jax.sharding import PartitionSpec as P

EPS = 1e-05
MESH = pl.DeviceIdType.MESH
BF = jnp.bfloat16
F32 = jnp.float32
HALVES = 2
VMEM_LIMIT = 60 * 2**20


def nn(a, b):
    return lax.dot_general(a, b, (((1,), (0,)), ((), ())), preferred_element_type=F32)


def nt(a, b):
    return lax.dot_general(a, b, (((1,), (1,)), ((), ())), preferred_element_type=F32)


def tn(a, b):
    return lax.dot_general(a, b, (((0,), (0,)), ((), ())), preferred_element_type=F32)


class Place:
    def __init__(self, seqs, models):
        self.seqs, self.chips = seqs, models // 2
        self.s = lax.axis_index("seq")
        self.m = lax.axis_index("mp")
        self.z = self.m // 2
        self.c = self.m % 2
        self.sibling = {"mp": self.m + 1 - 2 * self.c}
        self.above = {"mp": self.m + 2}
        self.below = {"mp": self.m - 2}
        self.has_above = self.z < self.chips - 1
        self.has_below = self.z > 0

    def peer(self, step):
        return {"seq": lax.rem(self.s + step, self.seqs)}

    def enter(self):
        barrier = pltpu.get_barrier_semaphore()

        def greet(where):
            pl.semaphore_signal(barrier, inc=1, device_id=where, device_id_type=MESH)

        greet(self.sibling)
        for step in range(1, self.seqs):
            greet(self.peer(step))
        pl.when(self.has_above)(lambda: greet(self.above))
        pl.when(self.has_below)(lambda: greet(self.below))
        chips = self.chips
        lines = (self.z + chips - 1) // chips + (2 * chips - 2 - self.z) // chips
        pl.semaphore_wait(barrier, self.seqs + lines)


def remote(src, dst, send, recv, where):
    return pltpu.make_async_remote_copy(
        src_ref=src, dst_ref=dst, send_sem=send, recv_sem=recv, device_id=where, device_id_type=MESH
    )


class Gather:
    def __init__(self, place, rows, own, sems):
        self.p, self.rows, self.own = place, rows, own
        self.share = rows.shape[0] // (2 * place.chips)
        self.piece = self.share // HALVES
        self.send, self.recv = sems

    def at(self, chip, core, half):
        return self.rows.at[pl.ds((chip * 2 + core) * self.share + half * self.piece, self.piece)]

    def copy(self, kind, chip, half, own=False):
        p = self.p
        where = (p.above, p.below, p.sibling)[kind]
        dst = self.at(chip, p.c, half)
        src = self.own.at[pl.ds(half * self.piece, self.piece)] if own and self.own is not None else dst
        return remote(src, dst, self.send.at[kind, chip, half], self.recv.at[kind // 2, chip, half], where)

    def start(self):
        p = self.p
        for half in range(HALVES):
            pl.when(p.has_above)(lambda h=half: self.copy(0, p.z, h, True).start())
            pl.when(p.has_below)(lambda h=half: self.copy(1, p.z, h, True).start())
        for half in range(HALVES):
            self.copy(2, p.z, half, True).start()

    def round(self, k):
        p = self.p
        for half in range(HALVES):

            @pl.when(p.z >= k)
            def _(half=half):
                chip = p.z - k
                self.copy(0, chip, half).wait_recv()
                pl.when(p.has_above)(lambda: self.copy(0, chip, half).start())
                self.copy(2, chip, half).start()

            @pl.when(p.z + k <= p.chips - 1)
            def _(half=half):
                chip = p.z + k
                self.copy(1, chip, half).wait_recv()
                pl.when(p.has_below)(lambda: self.copy(1, chip, half).start())
                self.copy(2, chip, half).start()

    def rounds(self):
        return [functools.partial(self.round, k) for k in range(1, self.p.chips)]

    def arrived(self):
        p = self.p
        for chip in range(p.chips):
            for half in range(HALVES):
                dst = self.at(chip, 1 - p.c, half)
                remote(dst, dst, self.send.at[2, chip, half], self.recv.at[1, chip, half], p.sibling).wait_recv()

    def drain(self):
        p = self.p
        for chip in range(p.chips):
            for half in range(HALVES):
                pl.when(p.has_above & (chip <= p.z))(lambda ch=chip, h=half: self.copy(0, ch, h).wait_send())
                pl.when(p.has_below & (chip >= p.z))(lambda ch=chip, h=half: self.copy(1, ch, h).wait_send())
                self.copy(2, chip, half).wait_send()


class Scatter:
    def __init__(self, place, part, from_core, from_line, sems):
        self.p, self.part, self.from_core, self.from_line = place, part, from_core, from_line
        self.share = from_core.shape[1]
        self.piece = self.share // HALVES
        self.core_send, self.core_recv, self.line_send, self.line_recv = sems

    def rows(self, chip, core):
        return self.part.at[pl.ds((chip * 2 + core) * self.share, self.share)]

    def core_copy(self, chip):
        p = self.p
        return remote(
            self.rows(chip, 1 - p.c), self.from_core.at[chip], self.core_send.at[chip], self.core_recv.at[chip], p.sibling
        )

    def give(self, chip):
        self.core_copy(chip).start()

    def mine(self, chip, half):
        return self.part.at[pl.ds((chip * 2 + self.p.c) * self.share + half * self.piece, self.piece)]

    def line_copy(self, down, chip, slot, half):
        p = self.p
        dst = self.from_line.at[slot, pl.ds(half * self.piece, self.piece)]
        return remote(
            self.mine(chip, half),
            dst,
            self.line_send.at[down, chip, half],
            self.line_recv.at[slot, half],
            p.below if down else p.above,
        )

    def total(self, chip, half, slots):
        span = pl.ds(half * self.piece, self.piece)
        value = self.mine(chip, half)[...].astype(F32) + self.from_core[chip, span].astype(F32)
        for slot in slots:
            value = value + self.from_line[slot, span].astype(F32)
        return value

    def hop(self, down, chip, slot, has_source):
        self.core_copy(chip).wait_recv()
        for half in range(HALVES):

            @pl.when(has_source)
            def _(half=half):
                self.line_copy(down, chip, chip, half).wait_recv()
                self.mine(chip, half)[...] = self.total(chip, half, [chip]).astype(BF)

            @pl.when(jnp.logical_not(has_source))
            def _(half=half):
                self.mine(chip, half)[...] = self.total(chip, half, []).astype(BF)

            self.line_copy(down, chip, slot, half).start()

    def round(self, r):
        p = self.p
        last = p.chips - 1

        @pl.when((p.z <= r) & p.has_above)
        def _():
            chip = last - r + p.z
            self.hop(0, chip, chip, p.has_below)

        @pl.when((last - p.z <= r) & p.has_below)
        def _():
            chip = r - last + p.z
            self.hop(1, chip, p.chips if r == last - 1 else chip, p.has_above)

    def rounds(self):
        return [functools.partial(self.round, r) for r in range(self.p.chips - 1)]

    def finish(self, store):
        p = self.p
        self.core_copy(p.z).wait_recv()
        for half in range(HALVES):
            pl.when(p.has_below)(lambda h=half: self.line_copy(0, p.z, p.z, h).wait_recv())
            pl.when(p.has_above)(lambda h=half: self.line_copy(1, p.z, p.chips, h).wait_recv())
            for up in (False, True):
                for low in (False, True):

                    @pl.when((p.has_above == up) & (p.has_below == low))
                    def _(half=half, up=up, low=low):
                        slots = ([p.z] if low else []) + ([p.chips] if up else [])
                        store(half * self.piece, self.piece, self.total(p.z, half, slots))

    def drain(self):
        p = self.p
        for chip in range(p.chips):
            self.core_copy(chip).wait_send()
            for half in range(HALVES):
                pl.when(p.has_above & (chip > p.z))(lambda ch=chip, h=half: self.line_copy(0, ch, ch, h).wait_send())
                pl.when(p.has_below & (chip < p.z))(lambda ch=chip, h=half: self.line_copy(1, ch, ch, h).wait_send())


def gather_sems(count, chips):
    return [pltpu.SemaphoreType.DMA((count, 3, chips, HALVES)), pltpu.SemaphoreType.DMA((count, 2, chips, HALVES))]


def scatter_sems(count, chips):
    return [
        pltpu.SemaphoreType.DMA((count, chips)),
        pltpu.SemaphoreType.DMA((count, chips)),
        pltpu.SemaphoreType.DMA((count, 2, chips, HALVES)),
        pltpu.SemaphoreType.DMA((count, chips + 1, HALVES)),
    ]


def picks(sems, index):
    return [sem.at[index] for sem in sems]


def far_first(place):
    low, high = 0, place.chips - 1
    order = []
    for _ in range(place.chips):
        left = place.z - low >= high - place.z
        order.append(jnp.where(left, low, high))
        low, high = jnp.where(left, low + 1, low), jnp.where(left, high, high - 1)
    return order


def weave(*lists):
    for step in range(max(len(steps) for steps in lists)):
        for steps in lists:
            if step < len(steps):
                steps[step]()


class Shards:
    def __init__(self, place, shard, full, dim, sems):
        self.p, self.shard, self.full, self.dim = place, shard, full, dim
        self.send, self.recv, self.local = sems

    def at(self, owner):
        size = self.shard.shape[self.dim]
        span = pl.ds(pl.multiple_of(owner * size, size), size)
        return self.full.at[(slice(None),) * self.dim + (span,)]

    def copy(self, step):
        p = self.p
        return remote(self.shard, self.at(p.s), self.send.at[step - 1], self.recv.at[step - 1], p.peer(step))

    def local_copy(self):
        return pltpu.make_async_copy(self.shard, self.at(self.p.s), self.local)

    def start(self):
        for step in range(1, self.p.seqs):
            self.copy(step).start()
        self.local_copy().start()

    def arrived(self):
        self.local_copy().wait()
        for step in range(1, self.p.seqs):
            self.copy(step).wait_recv()

    def drain(self):
        for step in range(1, self.p.seqs):
            self.copy(step).wait_send()


def mixer_forward_kernel(
    seqs,
    models,
    normed_ref,
    top_ref,
    taps_ref,
    in_ref,
    out_ref,
    pair_ref,
    down_ref,
    normed_rows,
    top_rows,
    in_rows,
    out_rows,
    pair_rows,
    down_rows,
    gates_out,
    product_out,
    mixed_out,
    mix_out,
    in_full,
    out_full,
    rows,
    gates,
    product,
    mixed,
    part,
    from_core,
    from_line,
    total,
    w_send,
    w_recv,
    w_local,
    halo_send,
    halo_recv,
    keep,
    *sems,
):
    p = Place(seqs, models)
    chips = p.chips
    g_sems, s_sems = sems[:2], sems[2:]
    slots, block = rows.shape[0], rows.shape[1]
    tile = block // chips
    share = tile // 2
    channels = in_full.shape[2]
    p.enter()

    firsts = [Gather(p, rows.at[slot], normed_ref.at[slot], picks(g_sems, slot)) for slot in range(slots)]
    tops = [Gather(p, top_rows.at[slot], top_ref.at[slot], picks(g_sems, slots + slot)) for slot in range(slots)]
    sums = [
        Scatter(p, part.at[slot], from_core.at[slot], from_line.at[slot], picks(s_sems, slot)) for slot in range(slots)
    ]
    weights = [
        Shards(p, shard, full, dim, (w_send.at[i], w_recv.at[i], w_local.at[i]))
        for i, (shard, full, dim) in enumerate(
            ((in_ref, in_full, 1), (out_ref, out_full, 1), (pair_ref, pair_rows, 1), (down_ref, down_rows, 1))
        )
    ]

    def own(slot, which, source):
        span = pl.ds(p.m * share, share)
        return pltpu.make_async_copy(source.at[slot], which.at[slot, span], keep.at[slot + (slots if which is top_rows else 0)])

    for slot in range(slots):
        own(slot, rows, normed_ref).start()
        own(slot, top_rows, top_ref).start()

    def halo(slot):
        return remote(
            product.at[slot, pl.ds(block, 8)],
            product.at[slot, pl.ds(0, 8)],
            halo_send.at[slot],
            halo_recv.at[slot],
            p.peer(1),
        )

    has_later, has_earlier = p.s < seqs - 1, p.s > 0
    for slot in range(slots):

        @pl.when(jnp.logical_not(has_earlier))
        def _(slot=slot):
            product[slot, pl.ds(0, 8)] = jnp.zeros((8, channels), F32)

    def project(slot):
        @pl.loop(0, chips)
        def _(i):
            span = pl.ds(i * tile, tile)
            source = rows[slot, span]
            b_gate = nn(source, in_full[0])
            x_value = nn(source, in_full[2])
            gates[slot, 0, span] = b_gate
            gates[slot, 1, span] = nn(source, in_full[1])
            gates[slot, 2, span] = x_value
            product[slot, pl.ds(8 + i * tile, tile)] = b_gate * x_value

        pl.when(has_later)(lambda: halo(slot).start())

    def convolve(slot):
        pl.when(has_earlier)(lambda: halo(slot).wait_recv())
        for i in range(chips):
            conv = 0.0
            for offset in range(taps_ref.shape[0]):
                conv = conv + taps_ref[offset : offset + 1] * product[slot, pl.ds(8 + i * tile - offset, tile)]
            mixed[slot, pl.ds(i * tile, tile)] = (gates[slot, 1, pl.ds(i * tile, tile)] * conv).astype(BF)

    def project_out(slot):
        for chip in far_first(p):
            span = pl.ds(chip * tile, tile)
            part[slot, span] = nn(mixed[slot, span], out_full[...]).astype(BF)
            sums[slot].give(chip)

    def finish(slot):
        def store(first, size, value):
            total[slot, pl.ds(first, size)] = value

        sums[slot].finish(store)

    firsts[0].start()
    weights[0].start()
    weights[1].start()
    steps = firsts[0].rounds()
    for step in steps[:-1]:
        step()
    firsts[1].start()
    steps[-1]()
    own(0, rows, normed_ref).wait()
    firsts[0].arrived()
    weights[0].arrived()
    weights[1].arrived()
    weights[2].start()
    weights[3].start()
    project(0)
    steps = firsts[1].rounds()
    steps[0]()
    convolve(0)
    project_out(0)
    weave(sums[0].rounds(), steps[1:])
    tops[0].start()
    own(1, rows, normed_ref).wait()
    firsts[1].arrived()
    project(1)
    steps = tops[0].rounds()
    steps[0]()
    convolve(1)
    project_out(1)
    finish(0)
    weave(sums[1].rounds(), steps[1:])
    tops[1].start()
    finish(1)
    stores = [
        pltpu.make_async_copy(src, dst, keep.at[2 * slots + i])
        for i, (src, dst) in enumerate(
            (
                (rows, normed_rows),
                (in_full, in_rows),
                (out_full, out_rows),
                (gates, gates_out),
                (product, product_out),
                (mixed, mixed_out),
                (total, mix_out),
            )
        )
    ]
    for store in stores:
        store.start()
    weave(tops[1].rounds())
    for slot in range(slots):
        own(slot, top_rows, top_ref).wait()
        tops[slot].arrived()
    weights[2].arrived()
    weights[3].arrived()
    for store in stores:
        store.wait()
    for thing in firsts + tops + sums + weights:
        thing.drain()
    for slot in range(slots):
        pl.when(has_later)(lambda slot=slot: halo(slot).wait_send())


def mixer_forward(seqs, models, normed, top, taps, mixer_in, mixer_out, gate_up, mlp_down):
    slots, share, width = normed.shape
    chips = models // 2
    block = share * models
    channels = mixer_in.shape[2]
    units = gate_up.shape[2]
    hbm = pl.BlockSpec(memory_space=pltpu.HBM)
    shape = jax.ShapeDtypeStruct
    return pl.pallas_call(
        functools.partial(mixer_forward_kernel, seqs, models),
        out_shape=[
            shape((slots, block, width), BF),
            shape((slots, block, width), BF),
            shape((3, width, channels), BF),
            shape((channels, width), BF),
            shape((2, width, units), BF),
            shape((units, width), BF),
            shape((slots, 3, block, channels), F32),
            shape((slots, block + 8, channels), F32),
            shape((slots, block, channels), BF),
            shape((slots, share, width), F32),
        ],
        in_specs=[hbm, hbm, pl.BlockSpec(memory_space=pltpu.VMEM)] + [hbm] * 4,
        out_specs=[hbm] * 10,
        scratch_shapes=[
            pltpu.VMEM((3, width, channels), BF),
            pltpu.VMEM((channels, width), BF),
            pltpu.VMEM((slots, block, width), BF),
            pltpu.VMEM((slots, 3, block, channels), F32),
            pltpu.VMEM((slots, block + 8, channels), F32),
            pltpu.VMEM((slots, block, channels), BF),
            pltpu.VMEM((slots, block, width), BF),
            pltpu.VMEM((slots, chips, share, width), BF),
            pltpu.VMEM((slots, chips + 1, share, width), BF),
            pltpu.VMEM((slots, share, width), F32),
            pltpu.SemaphoreType.DMA((4, seqs - 1)),
            pltpu.SemaphoreType.DMA((4, seqs - 1)),
            pltpu.SemaphoreType.DMA((4,)),
            pltpu.SemaphoreType.DMA((slots,)),
            pltpu.SemaphoreType.DMA((slots,)),
            pltpu.SemaphoreType.DMA((2 * slots + 7,)),
            *gather_sems(2 * slots, chips),
            *scatter_sems(slots, chips),
        ],
        compiler_params=pltpu.CompilerParams(collective_id=1, has_side_effects=True, vmem_limit_bytes=VMEM_LIMIT),
    )(normed, top, taps, mixer_in, mixer_out, gate_up, mlp_down)


def shifted(value, axis, steps):
    count = lax.axis_size(axis)
    leading, last = (max(0, -steps), min(count, count - steps))
    return lax.ppermute(value, axis, [(source, source + steps) for source in range(leading, last)])


def scatter_sum(value, axis, dim):
    low = value.astype(BF)
    return lax.psum_scatter(low, axis, scatter_dimension=dim, tiled=True).astype(F32)


def normalize(values, gain):
    scale = lax.rsqrt(jnp.mean(values * values, axis=-1, keepdims=True) + EPS)
    return (values * scale * gain, scale)


def norm_back(grad, values, scale, gain):
    unit = values * scale
    scaled = grad * gain
    gain_grad = jnp.sum(grad * unit, axis=(0, 1))
    input_grad = scale * (scaled - unit * jnp.mean(scaled * unit, axis=-1, keepdims=True))
    return (input_grad, gain_grad)


def local(
    hidden,
    cotangent,
    lengths,
    gain_mix,
    gain_mlp,
    conv_weight,
    mixer_in,
    mixer_out,
    gate_up,
    mlp_down,
):
    seqs, models = lax.axis_size("seq"), lax.axis_size("mp")
    seq_pos = lax.axis_index("seq")
    model_pos = lax.axis_index("mp")
    slots, share, width = hidden.shape
    block_rows = share * models
    channels = mixer_in.shape[2]
    taps = conv_weight.shape[0]
    local_taps = lax.dynamic_slice_in_dim(conv_weight, model_pos * channels, channels, 1)
    share_start = (seq_pos * models + model_pos) * share
    share_pos = share_start + jnp.arange(share, dtype=jnp.int32)
    mask = (share_pos[None, :] < lengths[:, None]).astype(F32)[:, :, None]
    source = hidden.astype(F32)
    top_grad = cotangent.astype(F32) * mask
    normed, scale_mix = normalize(source, gain_mix)
    (
        normed_rows,
        top_rows,
        in_full,
        out_full,
        pair_full,
        down_full,
        gates,
        extended,
        mixed,
        mix_share,
    ) = mixer_forward(
        seqs,
        models,
        normed.astype(BF),
        top_grad.astype(BF),
        local_taps,
        mixer_in,
        mixer_out,
        gate_up,
        mlp_down,
    )
    middle = source + mix_share
    normed_two, scale_mlp = normalize(middle, gain_mlp)
    normed_two = normed_two.astype(BF)
    acts, pair_grads, mlp_rows, outputs, middle_grads, mixed_rows = [], [], [], [], [], []
    stackeds, input_parts, tap_totals = [], [], []
    for slot in range(slots):
        rows = lax.all_gather(normed_two[slot], "mp", axis=0, tiled=True)
        mlp_rows.append(rows)
        gated = jnp.einsum("td,kdf->ktf", rows, pair_full, preferred_element_type=F32)
        gate_part, up_part = gated[0], gated[1]
        activated = jax.nn.silu(gate_part)
        act = (activated * up_part).astype(BF)
        acts.append(act)
        outputs.append(scatter_sum(jnp.dot(act, down_full, preferred_element_type=F32), "mp", 0))
        act_grad = jnp.einsum("td,fd->tf", top_rows[slot], down_full, preferred_element_type=F32)
        sigma = jax.nn.sigmoid(gate_part)
        gate_grad = (act_grad * up_part * sigma * (1.0 + gate_part * (1.0 - sigma))).astype(BF)
        pair_grad = jnp.stack([gate_grad, (act_grad * activated).astype(BF)])
        pair_grads.append(pair_grad)
        middle_grads.append(
            scatter_sum(jnp.einsum("ktf,kdf->td", pair_grad, pair_full, preferred_element_type=F32), "mp", 0)
        )
    output = (mask * (middle + jnp.stack(outputs))).astype(BF)
    middle_grad, gain_mlp_grad = norm_back(jnp.stack(middle_grads), middle, scale_mlp, gain_mlp)
    middle_grad = middle_grad + top_grad
    act, pair_grad, rows = jnp.stack(acts), jnp.stack(pair_grads), jnp.stack(mlp_rows)
    down_total = jnp.einsum("stf,std->fd", act, top_rows, preferred_element_type=F32)
    pair_total = jnp.einsum("std,sktf->kdf", rows, pair_grad, preferred_element_type=F32)
    low_grad = middle_grad.astype(BF)
    for slot in range(slots):
        mix_rows = lax.all_gather(low_grad[slot], "mp", axis=0, tiled=True)
        mixed_rows.append(mix_rows)
        mixed_grad = jnp.einsum("td,cd->tc", mix_rows, out_full, preferred_element_type=F32)
        ext = extended[slot]
        conv_out = 0.0
        for offset in range(taps):
            conv_out = conv_out + local_taps[offset] * ext[8 - offset : 8 - offset + block_rows]
        b_gate, c_gate, x_value = gates[slot, 0], gates[slot, 1], gates[slot, 2]
        c_grad = mixed_grad * conv_out
        conv_grad = mixed_grad * c_gate
        later = shifted(conv_grad[: taps - 1], "seq", -1)
        tail = jnp.concatenate([conv_grad, later], axis=0)
        product_grad = jnp.zeros_like(conv_grad)
        tap_rows = []
        for offset in range(taps):
            product_grad = product_grad + local_taps[offset] * tail[offset : offset + block_rows]
            tap_rows.append(jnp.sum(conv_grad * ext[8 - offset : 8 - offset + block_rows], axis=0))
        tap_totals.append(jnp.stack(tap_rows))
        stacked = jnp.stack([product_grad * x_value, c_grad, product_grad * b_gate]).astype(BF)
        stackeds.append(stacked)
        input_parts.append(
            scatter_sum(jnp.einsum("ktc,kdc->td", stacked, in_full, preferred_element_type=F32), "mp", 0)
        )
    out_total = jnp.einsum("stc,std->cd", mixed, jnp.stack(mixed_rows), preferred_element_type=F32)
    in_total = jnp.einsum("std,sktc->kdc", normed_rows, jnp.stack(stackeds), preferred_element_type=F32)
    source_grad, gain_mix_grad = norm_back(jnp.stack(input_parts), source, scale_mix, gain_mix)
    taps_full = lax.dynamic_update_slice_in_dim(
        jnp.zeros((taps, width), F32), tap_totals[0] + tap_totals[1], model_pos * channels, 1
    )
    gain_mix_grad, gain_mlp_grad, taps_grad = lax.psum((gain_mix_grad, gain_mlp_grad, taps_full), ("seq", "mp"))
    return (
        output,
        source_grad + middle_grad,
        gain_mix_grad,
        gain_mlp_grad,
        taps_grad,
        scatter_sum(in_total, "seq", 1),
        scatter_sum(out_total, "seq", 1),
        scatter_sum(pair_total, "seq", 1),
        scatter_sum(down_total, "seq", 1),
    )


def solution(mesh):
    placed = (
        P(None, ("seq", "mp"), None),
        P(None, ("seq", "mp"), None),
        P(),
        P(),
        P(),
        P(),
        P(None, "seq", "mp"),
        P("mp", "seq"),
        P(None, "seq", "mp"),
        P("mp", "seq"),
    )
    return jax.shard_map(
        local,
        mesh=mesh,
        in_specs=placed,
        out_specs=(
            P(None, ("seq", "mp"), None),
            P(None, ("seq", "mp"), None),
            P(),
            P(),
            P(),
            P(None, "seq", "mp"),
            P("mp", "seq"),
            P(None, "seq", "mp"),
            P("mp", "seq"),
        ),
        check_vma=False,
    )
```

time: 1310 us -> 1080 us (0.82)
  waiting for transfers between devices: 972 us -> 592 us
  Pallas kernels: 0 us -> 191 us
  matrix products: 198 us -> 168 us
    all_gather x12 -> x4, waiting for transfers between devices: 447 us -> 225 us  [the longest x2 181 us: local(): rows = lax.all_gather(normed_two[slot], 'mp', axis=0, tiled=True)]
    pallas_call x0 -> x1, Pallas kernels: none -> 191 us  [mixer_forward(): pl.pallas_call(functools.partial(mixer_forward_kernel, seqs, models), out...]
    reduce_scatter x12 -> x10, waiting for transfers between devices: 519 us -> 361 us  [scatter_sum(): lax.psum_scatter(low, axis, scatter_dimension=dim, tiled=True).astype(F32)]
    dot_general x24 -> x16, matrix products: 198 us -> 168 us  [the longest x2 25.4 us: local(): jnp.einsum('td,kdf->ktf', rows, pair_full, preferred_element_type=F32)]
  transfers between devices with their start and end apart: 28 -> 16, of which waited for: 25 -> 14; matrix products, arithmetic and copies ran while one was open for 18% -> 18% of each run, Pallas kernels for 0% -> 0%
where the time goes in v2:
time: 1080 us; the launch traced here: 1070 us
  waiting for transfers between devices  592 us (55%)
  Pallas kernels  191 us (18%)
  matrix products  168 us (16%)
  blocking collectives  40.5 us (4%)
  other arithmetic  37.1 us (3%)
  local copies, waits for them, and re-layouts  20.4 us (2%)
  between operations  14.7 us (1%)
    reduce_scatter x10, waiting for transfers between devices, scatter_sum(): lax.psum_scatter(low, axis, scatter_dimension=dim, tiled=True).astype(F32)  361 us
    pallas_call x1, Pallas kernels, mixer_forward(): pl.pallas_call(functools.partial(mixer_forward_kernel, seqs, models), out...  191 us
    all_gather x2, waiting for transfers between devices, local(): rows = lax.all_gather(normed_two[slot], 'mp', axis=0, tiled=True)  181 us
    all_gather x2, waiting for transfers between devices, local(): mix_rows = lax.all_gather(low_grad[slot], 'mp', axis=0, tiled=True)  44 us
    psum x1, blocking collectives, local(): lax.psum((gain_mix_grad, gain_mlp_grad, taps_full), ('seq', 'mp'))  40.5 us
    dot_general x2, matrix products, local(): jnp.einsum('td,kdf->ktf', rows, pair_full, preferred_element_type=F32)  25.4 us
    dot_general x2, matrix products, local(): jnp.einsum('ktf,kdf->td', pair_grad, pair_full, preferred_element_type=F32)  25.3 us
    dot_general x2, matrix products, local(): jnp.dot(act, down_full, preferred_element_type=F32)  23.2 us
  transfers between devices with their start and end apart: 16, of which 14 were waited for; matrix products, arithmetic and copies ran while one was open for 18% of the time, Pallas kernels for 0%

profile of v2, /device:TPU:0, one launch (start us, length us, event | category | flops | bytes accessed | tf_op | source)
XLA Modules:
  0.0 1068.4 jit_solution(359182552246786480)
XLA Ops:
  7.2 1.5 fusion.96
  8.8 0.7 compare_convert_fusion
  9.5 1.3 constant_dynamic-slice_fusion.1.taps_ref
  10.8 3.3 fusion.93
  14.0 190.7 %shard_map.169 = (bf16[2,1024,2048]{2,1,0:T(8,128)(2,1)}, bf16[2,1024,2048]{2,1,0:T(8,128)(2,1)}, bf16[3,2048,256]{2,1,0:T(8,128)(2,1)}, bf16[256,2048]{1,0:T(8,...) custom-call(bf16[2,128,2048]{2,1,0:T(8,128)(2,1)} %get-tuple-element, ...), custom_call_target="tpu_custom_call" | custom-call | tf_op jit(solution)/shard_map/pallas_call | solution.py:478
  204.8 1.9 multiply_reduce_fusion
  207.0 1.0 fusion.157
  208.1 0.7 all-gather.9.cloned.1.call-update
  209.3 171.8 %all-gather.11.cloned.1.call-done = bf16[1,1024,2048]{2,1,0:T(8,128)(2,1)} async-done(((bf16[1,128,2048]{2,1,0:T(8,128)(2,1)}), bf16[1,1024,2048]{2,1,0:T(8,128)(2,1)}) %all-gather.11.cloned.1.call-update) | async-done | bytes 4194320 | tf_op jit(solution)/shard_map/all_gather | solution.py:596
  381.1 12.7 %fusion.53 = f32[2,1024,1024]{1,2,0:T(8,128)S(1)} fusion(bf16[2,2048,1024]{2,1,0:T(8,128)(2,1)} %get-tuple-element.20, bf16[1,1024,2048]{2,1,0:T(8,128)(2,1)} %all-gather.11.cloned.1.call-done), kind=kOutput, calls=%fused_computation.73 | convolution fusion | flops 8589934592 | bytes 20971520 | tf_op jit(solution)/shard_map/td,kdf->ktf/dot_general | solution.py:598
  393.8 11.1 %fusion.103 = (bf16[1,1024,1024]{1,2,0:T(8,128)(2,1)S(1)}, bf16[1,1024,1024]{1,2,0:T(8,128)(2,1)S(1)}) fusion(f32[2,1024,1024]{1,2,0:T(8,128)S(1)} %fusion.53, bf16[1024,2048]{1,0:T(8,128)(2,1)S(1)} %copy-done.18, bf16[2,1024,2048]{2,1,0:T(8,128)(2,1)} %get-tuple-element.22), kind=kOutput, calls=%fused_computation.121 | convolution fusion | flops 4308598784 | bytes 20971520 | tf_op jit(solution)/shard_map/td,fd->tf/dot_general | solution.py:604
  404.9 1.3 copy-done.5
  406.2 0.7 copy-done.6
  406.9 12.6 %bitcast_convert_fusion.4 = bf16[1024,2048]{1,0:T(8,128)(2,1)} fusion(bf16[2,2048,1024]{2,1,0:T(8,128)(2,1)} %get-tuple-element.20, bf16[1,1024,1024]{1,2,0:T(8,128)(2,1)S(1)} %get-tuple-element.65, bf16[1,1024,1024]{1,2,0:T(8,128)(2,1)S(1)} %get-tuple-element.64), kind=kOutput, calls=%fused_computation.18 | convolution fusion | flops 8594128896 | bytes 16777216 | tf_op jit(solution)/shard_map/ktf,kdf->td/dot_general | solution.py:610
  419.7 9.4 all-gather.9.cloned.1.call-done
  429.1 12.7 %fusion.50 = f32[2,1024,1024]{1,2,0:T(8,128)S(1)} fusion(bf16[2,2048,1024]{2,1,0:T(8,128)(2,1)} %get-tuple-element.20, bf16[1,1024,2048]{2,1,0:T(8,128)(2,1)} %all-gather.9.cloned.1.call-done), kind=kOutput, calls=%fused_computation.72 | convolution fusion | flops 8589934592 | bytes 20971520 | tf_op jit(solution)/shard_map/td,kdf->ktf/dot_general | solution.py:598
  441.9 11.1 %fusion.102 = (bf16[1,1024,1024]{1,2,0:T(8,128)(2,1)S(1)}, bf16[1,1024,1024]{1,2,0:T(8,128)(2,1)S(1)}) fusion(f32[2,1024,1024]{1,2,0:T(8,128)S(1)} %fusion.50, bf16[1024,2048]{1,0:T(8,128)(2,1)S(1)} %copy-done.19, bf16[2,1024,2048]{2,1,0:T(8,128)(2,1)} %get-tuple-element.22), kind=kOutput, calls=%fused_computation.120 | convolution fusion | flops 4308598784 | bytes 20971520 | tf_op jit(solution)/shard_map/td,fd->tf/dot_general | solution.py:604
  453.0 1.3 copy-done.7
  454.3 0.8 copy-done.9
  455.0 12.7 %bitcast_convert_fusion.5 = bf16[1024,2048]{1,0:T(8,128)(2,1)} fusion(bf16[2,2048,1024]{2,1,0:T(8,128)(2,1)} %get-tuple-element.20, bf16[1,1024,1024]{1,2,0:T(8,128)(2,1)S(1)} %get-tuple-element.63, bf16[1,1024,1024]{1,2,0:T(8,128)(2,1)S(1)} %get-tuple-element.62), kind=kOutput, calls=%fused_computation.19 | convolution fusion | flops 8594128896 | bytes 16777216 | tf_op jit(solution)/shard_map/ktf,kdf->td/dot_general | solution.py:610
  468.1 12.7 %reduce-scatter.17.cloned.1.call-done = bf16[128,2048]{1,0:T(8,128)(2,1)} async-done(((bf16[1024,2048]{1,0:T(8,128)(2,1)}), bf16[128,2048]{1,0:T(8,128)(2,1)}) %reduce-scatter.17.cloned.1.call-update) | async-done | bytes 524304 | tf_op jit(solution)/shard_map/reduce_scatter | solution.py:526
  480.8 50.3 %reduce-scatter.15.cloned.1.call-done = bf16[128,2048]{1,0:T(8,128)(2,1)} async-done(((bf16[1024,2048]{1,0:T(8,128)(2,1)}), bf16[128,2048]{1,0:T(8,128)(2,1)}) %reduce-scatter.15.cloned.1.call-update) | async-done | bytes 524304 | tf_op jit(solution)/shard_map/reduce_scatter | solution.py:526
  531.1 1.8 fusion.92
  532.9 1.9 fusion.142
  534.8 1.0 fusion.156
  536.0 0.5 all-gather.13.cloned.1.call-update
  536.5 5.0 multiply_convert_fusion
  541.5 5.3 multiply_convert_fusion.1
  546.9 10.5 bitcast_convert_fusion.1
  557.4 2.8 fusion.79
  560.4 0.6 copy-done.10
  561.4 1.9 copy-done.20
  563.2 1.3 copy-done.21
  564.5 19.4 %fusion = bf16[2,2048,1024]{1,2,0:T(8,128)(2,1)} fusion(bf16[1,1024,2048]{2,1,0:T(8,128)(2,1)S(1)} %copy-done.20, bf16[1,1024,2048]{2,1,0:T(8,128)(2,1)S(1)} %copy-done.21, bf16[1,2,1024,1024]{2,3,1,0:T(8,128)(2,1)S(1)} %fusion.79, bf16[1,2,1024,1024]{2,3,1,0:T(8,128)(2,1)S(1)} %fusion.80), kind=kOutput, calls=%fused_computation.1 | convolution fusion | flops 17192452096 | bytes 25165824 | tf_op jit(solution)/shard_map/std,sktf->kdf/dot_general | solution.py:617
  584.4 0.9 constant_dynamic-slice_fusion
  585.3 44.0 %all-gather.13.cloned.1.call-done = bf16[1,1024,2048]{2,1,0:T(8,128)(2,1)} async-done(((bf16[1,128,2048]{2,1,0:T(8,128)(2,1)}), bf16[1,1024,2048]{2,1,0:T(8,128)(2,1)}) %all-gather.13.cloned.1.call-update) | async-done | bytes 4194320 | tf_op jit(solution)/shard_map/all_gather | solution.py:620
  629.3 7.2 fusion.81
  636.6 4.3 fusion.18
  640.9 6.8 fusion.131
  647.7 1.3 collective-permute-start.1
  649.0 1.3 collective-permute-start
  650.3 2.9 collective-permute-done.1
  653.2 1.9 collective-permute-done
  655.2 0.8 fusion.141
  656.9 8.5 fusion.71
  665.6 7.6 bitcast_convert_fusion.3
  673.3 1.0 copy-done.12
  674.3 7.6 bitcast_convert_fusion.2
  682.0 11.5 %convolution_convert_fusion = bf16[1024,2048]{1,0:T(8,128)(2,1)} fusion(bf16[1024,2048]{1,0:T(8,128)(2,1)} %get-tuple-element.21, f32[2,1024,1024]{1,2,0:T(8,128)} %copy-done.3), kind=kOutput, calls=%fused_computation.70 | convolution fusion | flops 4303355904 | bytes 16777216 | tf_op jit(solution)/shard_map/dot_general | solution.py:603
  693.8 11.7 %convolution_convert_fusion.1 = bf16[1024,2048]{1,0:T(8,128)(2,1)} fusion(bf16[1024,2048]{1,0:T(8,128)(2,1)} %get-tuple-element.21, f32[2,1024,1024]{1,2,0:T(8,128)} %copy-done.4), kind=kOutput, calls=%fused_computation.71 | convolution fusion | flops 4303355904 | bytes 16777216 | tf_op jit(solution)/shard_map/dot_general | solution.py:603
  705.5 3.0 convert_element_type.153
  708.5 65.6 %reduce-scatter.27.cloned.1.call-done = bf16[2,512,1024]{1,2,0:T(8,128)(2,1)} async-done(((bf16[2,2048,1024]{1,2,0:T(8,128)(2,1)}), bf16[2,512,1024]{1,2,0:T(8,128)(2,1)}) %reduce-scatter.27.cloned.1.call-update) | async-done | bytes 2097168 | tf_op jit(solution)/shard_map/reduce_scatter | solution.py:526
  774.1 4.1 copy.31
  778.2 27.1 %reduce-scatter.25.cloned.1.call-done = bf16[256,512]{1,0:T(8,128)(2,1)} async-done(((bf16[256,2048]{1,0:T(8,128)(2,1)}), bf16[256,512]{1,0:T(8,128)(2,1)}) %reduce-scatter.25.cloned.1.call-update) | async-done | bytes 262160 | tf_op jit(solution)/shard_map/reduce_scatter | solution.py:526
  805.3 1.8 convert_element_type.146
  807.1 45.3 %reduce-scatter.23.cloned.1.call-done = bf16[3,512,256]{1,2,0:T(8,128)(2,1)} async-done(((bf16[3,2048,256]{1,2,0:T(8,128)(2,1)}), bf16[3,512,256]{1,2,0:T(8,128)(2,1)}) %reduce-scatter.23.cloned.1.call-update) | async-done | bytes 786448 | tf_op jit(solution)/shard_map/reduce_scatter | solution.py:526
  852.4 2.5 copy.30
  854.9 49.9 %reduce-scatter.19.cloned.1.call-done = bf16[128,2048]{1,0:T(8,128)(2,1)} async-done(((bf16[1024,2048]{1,0:T(8,128)(2,1)}), bf16[128,2048]{1,0:T(8,128)(2,1)}) %reduce-scatter.19.cloned.1.call-update) | async-done | bytes 524304 | tf_op jit(solution)/shard_map/reduce_scatter | solution.py:526
  904.8 50.4 %reduce-scatter.21.cloned.1.call-done = bf16[128,2048]{1,0:T(8,128)(2,1)} async-done(((bf16[1024,2048]{1,0:T(8,128)(2,1)}), bf16[128,2048]{1,0:T(8,128)(2,1)}) %reduce-scatter.21.cloned.1.call-update) | async-done | bytes 524304 | tf_op jit(solution)/shard_map/reduce_scatter | solution.py:526
  955.3 1.9 fusion.95
  957.2 40.5 %all-reduce = (f32[2048]{0:T(1024)}, f32[2048]{0:T(1024)}, f32[3,2048]{1,0:T(4,128)}) all-reduce(f32[2048]{0:T(1024)S(1)} %get-tuple-element.49, f32[2048]{0:T(1024)S(1)} %get-tuple-element.44, f32[3,2048]{1,0:T(4,128)S(1)} %fusion.143), channel_id=1, replica_groups=mesh['seq'=4,'mp'=8] {'seq','mp'}, use_global_device_ids=true, to_apply=%region_11.12 | all-reduce | flops 10240 | bytes 81920 | tf_op jit(solution)/shard_map/psum | solution.py:649
  997.7 9.2 reduce-scatter.13.cloned.1.call-done
  1006.9 50.4 %reduce-scatter.11.cloned.1.call-done = bf16[128,2048]{1,0:T(8,128)(2,1)} async-done(((bf16[1024,2048]{1,0:T(8,128)(2,1)}), bf16[128,2048]{1,0:T(8,128)(2,1)}) %reduce-scatter.11.cloned.1.call-update) | async-done | bytes 524304 | tf_op jit(solution)/shard_map/reduce_scatter | solution.py:526
  1057.3 4.3 fusion.88
  (99 shorter events, 4.2 us)
Async XLA Ops:
  7.2 373.9 %all-gather.11.cloned.1.call-start = ((), (), s32[]{:S(2)}) async-start(), calls=%async_computation.21 | async-start | bytes 4718592 | tf_op jit(solution)/shard_map/all_gather | solution.py:596
  8.8 196.0 %copy-start.16 = (f32[2,128]{1,0:T(2,128)}, f32[2,128]{1,0:T(2,128)S(1)}, u32[]{:S(2)}) copy-start(f32[2,128]{1,0:T(2,128)S(1)} %add_rsqrt_fusion.1) | copy-start | bytes 3076
  14.0 190.8 %copy-start = (bf16[2,128,2048]{2,1,0:T(8,128)(2,1)S(1)}, bf16[2,128,2048]{2,1,0:T(8,128)(2,1)}, u32[]{:S(2)}) copy-start(bf16[2,128,2048]{2,1,0:T(8,128)(2,1)} %param.10) | copy-start | bytes 3145732
  204.8 2.0 copy-start.14
  208.1 221.0 %all-gather.9.cloned.1.call-start = ((), (), s32[]{:S(2)}) async-start(), calls=%async_computation.20 | async-start | bytes 4718592 | tf_op jit(solution)/shard_map/all_gather | solution.py:596
  208.8 271.9 %reduce-scatter.17.cloned.1.call-start = ((), (), s32[]{:S(2)}) async-start(), calls=%async_computation.13 | async-start | bytes 4718592 | tf_op jit(solution)/shard_map/reduce_scatter | solution.py:526
  381.1 12.7 %copy-start.18 = (bf16[1024,2048]{1,0:T(8,128)(2,1)S(1)}, bf16[1024,2048]{1,0:T(8,128)(2,1)}, u32[]{:S(2)}) copy-start(bf16[1024,2048]{1,0:T(8,128)(2,1)} %get-tuple-element.21) | copy-start | bytes 12582916
  393.8 11.1 %copy-start.3 = (f32[2,1024,1024]{1,2,0:T(8,128)}, f32[2,1024,1024]{1,2,0:T(8,128)S(1)}, u32[]{:S(2)}) copy-start(f32[2,1024,1024]{1,2,0:T(8,128)S(1)} %fusion.53) | copy-start | bytes 25165828
  404.9 1.3 copy-start.5
  404.9 2.0 copy-start.6
  419.5 111.6 %reduce-scatter.15.cloned.1.call-start = ((), (), s32[]{:S(2)}) async-start(), calls=%async_computation.12 | async-start | bytes 4718592 | tf_op jit(solution)/shard_map/reduce_scatter | solution.py:526
  429.1 12.7 %copy-start.19 = (bf16[1024,2048]{1,0:T(8,128)(2,1)S(1)}, bf16[1024,2048]{1,0:T(8,128)(2,1)}, u32[]{:S(2)}) copy-start(bf16[1024,2048]{1,0:T(8,128)(2,1)} %get-tuple-element.21) | copy-start | bytes 12582916
  441.9 11.1 %copy-start.4 = (f32[2,1024,1024]{1,2,0:T(8,128)}, f32[2,1024,1024]{1,2,0:T(8,128)S(1)}, u32[]{:S(2)}) copy-start(f32[2,1024,1024]{1,2,0:T(8,128)S(1)} %fusion.50) | copy-start | bytes 25165828
  453.0 1.3 copy-start.7
  453.0 2.1 copy-start.9
  467.8 65.2 %copy-start.2 = (bf16[2,128,2048]{2,1,0:T(8,128)(2,1)S(1)}, bf16[2,128,2048]{2,1,0:T(8,128)(2,1)}, u32[]{:S(2)}) copy-start(bf16[2,128,2048]{2,1,0:T(8,128)(2,1)} %param.11) | copy-start | bytes 3145732
  467.8 117.5 %all-gather.15.cloned.1.call-start = ((), (), s32[]{:S(2)}) async-start(), calls=%async_computation.23 | async-start | bytes 4718592 | tf_op jit(solution)/shard_map/all_gather | solution.py:620
  535.9 93.4 %all-gather.13.cloned.1.call-start = ((), (), s32[]{:S(2)}) async-start(), calls=%async_computation.22 | async-start | bytes 4718592 | tf_op jit(solution)/shard_map/all_gather | solution.py:620
  536.5 169.0 %reduce-scatter.29.cloned.1.call-start = ((), (), s32[]{:S(2)}) async-start(), calls=%async_computation.19 | async-start | bytes 5242880 | tf_op jit(solution)/shard_map/reduce_scatter | solution.py:526
  536.5 10.3 slice-start.4
  541.5 5.3 slice-start.5
  557.4 216.7 %reduce-scatter.27.cloned.1.call-start = ((), (), s32[]{:S(2)}) async-start(), calls=%async_computation.18 | async-start | bytes 10485760 | tf_op jit(solution)/shard_map/reduce_scatter | solution.py:526
  557.4 2.9 copy-start.8
  557.4 3.6 copy-start.10
  561.0 2.2 copy-start.20
  561.0 3.5 copy-start.21
  583.9 221.4 %reduce-scatter.25.cloned.1.call-start = ((), (), s32[]{:S(2)}) async-start(), calls=%async_computation.17 | async-start | bytes 1310720 | tf_op jit(solution)/shard_map/reduce_scatter | solution.py:526
  629.3 7.3 copy-start.23
  636.5 215.9 %reduce-scatter.23.cloned.1.call-start = ((), (), s32[]{:S(2)}) async-start(), calls=%async_computation.16 | async-start | bytes 3932160 | tf_op jit(solution)/shard_map/reduce_scatter | solution.py:526
  636.5 4.4 copy-start.22
  636.6 18.6 %slice-start = ((s8[6291456]{0:T(1024)(128)(4,1)}), s8[4194304]{0:T(1024)(128)(4,1)S(1)}, s32[]{:S(2)}) async-start(s8[6291456]{0:T(1024)(128)(4,1)} %bitcast.289), calls=%async_computation.24 | async-start | bytes 8388608
  636.6 20.4 %slice-start.2 = ((s8[8388608]{0:T(1024)(128)(4,1)}), s8[4194304]{0:T(1024)(128)(4,1)S(1)}, s32[]{:S(2)}) async-start(s8[8388608]{0:T(1024)(128)(4,1)} %bitcast.317), calls=%async_computation.26 | async-start | bytes 8388608
  640.9 14.3 %slice-start.1 = ((s8[6291456]{0:T(1024)(128)(4,1)}), s8[2097152]{0:T(1024)(128)(4,1)S(1)}, s32[]{:S(2)}) async-start(s8[6291456]{0:T(1024)(128)(4,1)} %bitcast.289), calls=%async_computation.25 | async-start | bytes 4194304
  640.9 16.0 %slice-start.3 = ((s8[8388608]{0:T(1024)(128)(4,1)}), s8[4194304]{0:T(1024)(128)(4,1)S(1)}, s32[]{:S(2)}) async-start(s8[8388608]{0:T(1024)(128)(4,1)} %bitcast.317), calls=%async_computation.27 | async-start | bytes 8388608
  647.7 8.7 copy-start.24
  647.7 8.7 copy-start.25
  647.7 5.5 collective-permute-start.1
  649.0 6.1 collective-permute-start
  655.9 0.8 copy-start.11
  656.0 1.0 copy-start.13
  665.4 239.4 %reduce-scatter.19.cloned.1.call-start = ((), (), s32[]{:S(2)}) async-start(), calls=%async_computation.14 | async-start | bytes 4718592 | tf_op jit(solution)/shard_map/reduce_scatter | solution.py:526
  673.2 1.0 copy-start.12
  673.3 282.0 %reduce-scatter.21.cloned.1.call-start = ((), (), s32[]{:S(2)}) async-start(), calls=%async_computation.15 | async-start | bytes 4718592 | tf_op jit(solution)/shard_map/reduce_scatter | solution.py:526
  681.9 325.0 %reduce-scatter.13.cloned.1.call-start = ((), (), s32[]{:S(2)}) async-start(), calls=%async_computation.11 | async-start | bytes 4718592 | tf_op jit(solution)/shard_map/reduce_scatter | solution.py:526
  693.5 363.8 %reduce-scatter.11.cloned.1.call-start = ((), (), s32[]{:S(2)}) async-start(), calls=%async_computation.10 | async-start | bytes 4718592 | tf_op jit(solution)/shard_map/reduce_scatter | solution.py:526
  708.5 246.8 %copy-start.1 = (bf16[2,128,2048]{2,1,0:T(8,128)(2,1)S(1)}, bf16[2,128,2048]{2,1,0:T(8,128)(2,1)}, u32[]{:S(2)}) copy-start(bf16[2,128,2048]{2,1,0:T(8,128)(2,1)} %param.10) | copy-start | bytes 3145732
  708.5 246.8 %copy-start.15 = (f32[2048]{0:T(1024)S(1)}, f32[2048]{0:T(1024)}, u32[]{:S(2)}) copy-start(f32[2048]{0:T(1024)} %param.13) | copy-start | bytes 24580
  708.5 246.8 %copy-start.17 = (f32[2,128]{1,0:T(2,128)S(1)}, f32[2,128]{1,0:T(2,128)}, u32[]{:S(2)}) copy-start(f32[2,128]{1,0:T(2,128)} %copy-done.16) | copy-start | bytes 3076
Sparse Core Ops, SparseCore 0:
  208.2 172.8 all-gather.10
  383.2 45.8 all-gather.8
  432.0 48.7 reduce-scatter.16
  482.9 48.1 reduce-scatter.14
  536.0 45.2 all-gather.14
  583.4 45.8 all-gather.12
  632.8 51.4 reduce-scatter.28
  687.7 86.3 reduce-scatter.26
  777.5 27.7 reduce-scatter.24
  808.4 43.9 reduce-scatter.22
  854.8 49.9 reduce-scatter.18
  907.1 48.1 reduce-scatter.20
  957.7 49.1 reduce-scatter.12
  1009.1 48.1 reduce-scatter.10

commit v3 on v2

--- a/solution.py
+++ b/solution.py
@@ -12,7 +12,7 @@
 BF = jnp.bfloat16
 F32 = jnp.float32
 HALVES = 2
-VMEM_LIMIT = 60 * 2**20
+VMEM_LIMIT = 63 * 2**20
 
 
 def nn(a, b):
@@ -515,15 +515,623 @@
     )(normed, top, taps, mixer_in, mixer_out, gate_up, mlp_down)
 
 
-def shifted(value, axis, steps):
-    count = lax.axis_size(axis)
-    leading, last = (max(0, -steps), min(count, count - steps))
-    return lax.ppermute(value, axis, [(source, source + steps) for source in range(leading, last)])
-
-
-def scatter_sum(value, axis, dim):
-    low = value.astype(BF)
-    return lax.psum_scatter(low, axis, scatter_dimension=dim, tiled=True).astype(F32)
+def mlp_kernel(
+    seqs,
+    models,
+    normed_ref,
+    top_rows,
+    pair_ref,
+    down_ref,
+    grad_out,
+    mlp_part,
+    pair_grad,
+    down_grad,
+    pair,
+    down,
+    rows,
+    top_tile,
+    top_cols,
+    acts,
+    stage,
+    part,
+    from_core,
+    from_line,
+    total,
+    load,
+    tile_sem,
+    cols_sem,
+    stage_sem,
+    keep,
+    *sems,
+):
+    p = Place(seqs, models)
+    chips = p.chips
+    g_sems, s_sems = sems[:2], sems[2:]
+    slots, block, width = rows.shape
+    units = down.shape[0]
+    tile = block // chips
+    share = tile // 2
+    unit_block = min(512, units)
+    wide_block = 512
+    columns = top_cols.shape[-1]
+    loads = [pltpu.make_async_copy(pair_ref, pair, load.at[0]), pltpu.make_async_copy(down_ref, down, load.at[1])]
+    for thing in loads:
+        thing.start()
+    p.enter()
+    gathers = [Gather(p, rows.at[slot], normed_ref.at[slot], picks(g_sems, slot)) for slot in range(slots)]
+    sums = [
+        Scatter(p, part.at[slot], from_core.at[slot], from_line.at[slot], picks(s_sems, slot)) for slot in range(slots)
+    ]
+
+    def own(slot):
+        return pltpu.make_async_copy(
+            normed_ref.at[slot], rows.at[slot, pl.ds(p.m * share, share)], load.at[2 + slot]
+        )
+
+    order = far_first(p)
+    tiles = [(slot, chip) for slot in range(slots) for chip in order]
+
+    def fetch(index):
+        slot, chip = tiles[index]
+        return pltpu.make_async_copy(
+            top_rows.at[slot, pl.ds(chip * tile, tile)], top_tile.at[index % 2], tile_sem.at[index % 2]
+        )
+
+    def put(index):
+        slot, chip = tiles[index]
+        return pltpu.make_async_copy(
+            stage.at[index % 2], mlp_part.at[slot, pl.ds(chip * tile, tile)], stage_sem.at[index % 2]
+        )
+
+    def work(index):
+        slot, chip = tiles[index]
+        buf = index % 2
+        span = pl.ds(chip * tile, tile)
+        fetch(index).wait()
+        if index + 1 < len(tiles):
+            fetch(index + 1).start()
+        if index >= 2:
+            put(index - 2).wait()
+
+        @pl.loop(0, units // unit_block)
+        def _(i):
+            cut = pl.ds(pl.multiple_of(i * unit_block, unit_block), unit_block)
+            source = rows[slot, span]
+            gate = nn(source, pair[0, :, cut])
+            up = nn(source, pair[1, :, cut])
+            act_grad = nt(top_tile[buf], down[cut])
+            sigma = jax.nn.sigmoid(gate)
+            silu = gate * sigma
+            acts[0, slot, span, cut] = (silu * up).astype(BF)
+            acts[1, slot, span, cut] = (act_grad * up * sigma * (1.0 + gate * (1.0 - sigma))).astype(BF)
+            acts[2, slot, span, cut] = (act_grad * silu).astype(BF)
+
+        @pl.loop(0, width // wide_block)
+        def _(i):
+            cut = pl.ds(pl.multiple_of(i * wide_block, wide_block), wide_block)
+            value = nt(acts[1, slot, span], pair[0, cut]) + nt(acts[2, slot, span], pair[1, cut])
+            part[slot, span, cut] = value.astype(BF)
+            stage[buf, :, cut] = nn(acts[0, slot, span], down[:, cut]).astype(BF)
+
+        sums[slot].give(chip)
+        put(index).start()
+
+    def finish(slot):
+        def store(first, size, value):
+            total[slot, pl.ds(first, size)] = value
+
+        sums[slot].finish(store)
+
+    def pair_step(index):
+        k, first = divmod(index, width // wide_block)
+        cut = pl.ds(first * wide_block, wide_block)
+        value = 0.0
+        for slot in range(slots):
+            value = value + tn(rows[slot, :, cut], acts[1 + k, slot])
+        pair[k, cut] = value.astype(BF)
+        pltpu.make_async_copy(pair.at[k, cut], pair_grad.at[k, cut], keep.at[index]).start()
+
+    pair_steps = 2 * (width // wide_block)
+
+    def fetch_columns(index):
+        return pltpu.make_async_copy(
+            top_rows.at[:, :, pl.ds(index * columns, columns)], top_cols.at[index % 2], cols_sem.at[index % 2]
+        )
+
+    def down_step(index):
+        fetch_columns(index).wait()
+        for first in range(0, units, unit_block):
+            cut = pl.ds(first, unit_block)
+            value = 0.0
+            for slot in range(slots):
+                value = value + tn(acts[0, slot, :, cut], top_cols[index % 2, slot])
+            down[cut, pl.ds(index * columns, columns)] = value.astype(BF)
+        if index + 2 < width // columns:
+            fetch_columns(index + 2).start()
+
+    for slot in range(slots):
+        own(slot).start()
+    fetch(0).start()
+    gathers[0].start()
+    steps = gathers[0].rounds()
+    for step in steps[:-1]:
+        step()
+    gathers[1].start()
+    steps[-1]()
+    own(0).wait()
+    gathers[0].arrived()
+    for thing in loads:
+        thing.wait()
+    next_rows = gathers[1].rounds()
+    hops = sums[0].rounds()
+    for index in range(chips):
+        work(index)
+        if index < len(hops):
+            hops[index]()
+            next_rows[index]()
+    own(1).wait()
+    gathers[1].arrived()
+    hops = sums[1].rounds()
+    for index in range(chips):
+        work(chips + index)
+        if index == 0:
+            finish(0)
+        if index < len(hops):
+            hops[index]()
+    fetch_columns(0).start()
+    fetch_columns(1).start()
+    for index in range(pair_steps):
+        pair_step(index)
+    for index in range(width // columns):
+        down_step(index)
+    finish(1)
+    last = [
+        pltpu.make_async_copy(down, down_grad, keep.at[pair_steps]),
+        pltpu.make_async_copy(total, grad_out, keep.at[pair_steps + 1]),
+    ]
+    for thing in last:
+        thing.start()
+    for index in range(pair_steps):
+        k, first = divmod(index, width // wide_block)
+        cut = pl.ds(first * wide_block, wide_block)
+        pltpu.make_async_copy(pair.at[k, cut], pair_grad.at[k, cut], keep.at[index]).wait()
+    for index in range(len(tiles) - 2, len(tiles)):
+        put(index).wait()
+    for thing in last:
+        thing.wait()
+    for thing in gathers + sums:
+        thing.drain()
+
+
+def mlp(seqs, models, normed, top_rows, pair_full, down_full):
+    slots, share, width = normed.shape
+    chips = models // 2
+    block = share * models
+    units = down_full.shape[0]
+    hbm = pl.BlockSpec(memory_space=pltpu.HBM)
+    shape = jax.ShapeDtypeStruct
+    return pl.pallas_call(
+        functools.partial(mlp_kernel, seqs, models),
+        out_shape=[
+            shape((slots, share, width), F32),
+            shape((slots, block, width), BF),
+            shape((2, width, units), BF),
+            shape((units, width), BF),
+        ],
+        in_specs=[hbm] * 4,
+        out_specs=[hbm] * 4,
+        scratch_shapes=[
+            pltpu.VMEM((2, width, units), BF),
+            pltpu.VMEM((units, width), BF),
+            pltpu.VMEM((slots, block, width), BF),
+            pltpu.VMEM((2, block // chips, width), BF),
+            pltpu.VMEM((2, slots, block, 256), BF),
+            pltpu.VMEM((3, slots, block, units), BF),
+            pltpu.VMEM((2, block // chips, width), BF),
+            pltpu.VMEM((slots, block, width), BF),
+            pltpu.VMEM((slots, chips, share, width), BF),
+            pltpu.VMEM((slots, chips + 1, share, width), BF),
+            pltpu.VMEM((slots, share, width), F32),
+            pltpu.SemaphoreType.DMA((2 + slots,)),
+            pltpu.SemaphoreType.DMA((2,)),
+            pltpu.SemaphoreType.DMA((2,)),
+            pltpu.SemaphoreType.DMA((2,)),
+            pltpu.SemaphoreType.DMA((2 * (width // 512) + 2,)),
+            *gather_sems(slots, chips),
+            *scatter_sems(slots, chips),
+        ],
+        compiler_params=pltpu.CompilerParams(collective_id=2, has_side_effects=True, vmem_limit_bytes=VMEM_LIMIT),
+    )(normed, top_rows, pair_full, down_full)
+
+
+class Spread:
+    def __init__(self, place, partial, got, sems):
+        self.p, self.partial, self.got = place, partial, got
+        self.send, self.recv, self.local = sems
+
+    def block(self, owner):
+        size = self.partial.shape[1] // self.p.seqs
+        return self.partial.at[:, pl.ds(pl.multiple_of(owner * size, size), size)]
+
+    def copy(self, step):
+        p = self.p
+        return remote(
+            self.block(lax.rem(p.s + step, p.seqs)),
+            self.got.at[step],
+            self.send.at[step - 1],
+            self.recv.at[step - 1],
+            p.peer(step),
+        )
+
+    def local_copy(self):
+        return pltpu.make_async_copy(self.block(self.p.s), self.got.at[0], self.local)
+
+    def start(self):
+        for step in range(1, self.p.seqs):
+            self.copy(step).start()
+        self.local_copy().start()
+
+    def finish(self):
+        self.local_copy().wait()
+        for step in range(1, self.p.seqs):
+            self.copy(step).wait()
+
+
+def mixer_backward_kernel(
+    seqs,
+    models,
+    low_ref,
+    mlp_part,
+    taps_ref,
+    in_ref,
+    out_ref,
+    normed_rows,
+    gates_ref,
+    product_ref,
+    mixed_ref,
+    pair_grad,
+    down_grad,
+    mlp_out,
+    grad_out,
+    taps_out,
+    in_got,
+    out_got,
+    pair_got,
+    down_got,
+    in_full,
+    out_full,
+    rows,
+    columns,
+    gates,
+    product,
+    mixed,
+    conv_grad,
+    stacked,
+    part,
+    from_core,
+    from_line,
+    mlp_total,
+    grad_total,
+    load,
+    cols_sem,
+    w_send,
+    w_recv,
+    w_local,
+    halo_send,
+    halo_recv,
+    free,
+    *sems,
+):
+    p = Place(seqs, models)
+    chips = p.chips
+    g_sems, s_sems = sems[:2], sems[2:]
+    slots, block, width = rows.shape
+    channels = out_full.shape[0]
+    taps = taps_ref.shape[0]
+    tile = block // chips
+    share = tile // 2
+    wide_block = 512
+    cols = columns.shape[-1]
+    loads = [
+        pltpu.make_async_copy(src, dst, load.at[i])
+        for i, (src, dst) in enumerate(
+            [(mlp_part.at[slot], part.at[slot]) for slot in range(slots)]
+            + [
+                (low_ref.at[slot], rows.at[slot, pl.ds(p.m * share, share)])
+                for slot in range(slots)
+            ]
+            + [
+                (in_ref, in_full),
+                (out_ref, out_full),
+                (gates_ref, gates),
+                (product_ref, product),
+                (mixed_ref, mixed),
+            ]
+        )
+    ]
+    for thing in loads:
+        thing.start()
+    p.enter()
+    gathers = [Gather(p, rows.at[slot], low_ref.at[slot], picks(g_sems, slot)) for slot in range(slots)]
+
+    def scatter(slot, index):
+        return Scatter(p, part.at[slot], from_core.at[slot], from_line.at[slot], picks(s_sems, index))
+
+    mlp_sums = [scatter(slot, slot) for slot in range(slots)]
+    sums = [scatter(slot, slots + slot) for slot in range(slots)]
+    spreads = [
+        Spread(p, partial, got, (w_send.at[i], w_recv.at[i], w_local.at[i]))
+        for i, (partial, got) in enumerate(
+            ((pair_grad, pair_got), (down_grad, down_got), (in_full, in_got), (out_full, out_got))
+        )
+    ]
+    has_later, has_earlier = p.s < seqs - 1, p.s > 0
+    order = far_first(p)
+
+    def halo(slot):
+        return remote(
+            conv_grad.at[slot, pl.ds(0, 8)],
+            conv_grad.at[slot, pl.ds(block, 8)],
+            halo_send.at[slot],
+            halo_recv.at[slot],
+            p.peer(seqs - 1),
+        )
+
+    for slot in range(slots):
+
+        @pl.when(jnp.logical_not(has_later))
+        def _(slot=slot):
+            conv_grad[slot, pl.ds(block, 8)] = jnp.zeros((8, channels), F32)
+
+    taps_out[...] = jnp.zeros_like(taps_out)
+
+    def first_pass(slot):
+        for i in range(chips):
+            span = pl.ds(i * tile, tile)
+            mixed_grad = nt(rows[slot, span], out_full[...])
+            grad = mixed_grad * gates[slot, 1, span]
+            conv_grad[slot, span] = grad
+            conv = 0.0
+            for offset in range(taps):
+                earlier = product[slot, pl.ds(8 + i * tile - offset, tile)]
+                conv = conv + taps_ref[offset : offset + 1] * earlier
+                taps_out[offset : offset + 1] += jnp.sum(grad * earlier, axis=0, keepdims=True)
+            stacked[slot, span, pl.ds(channels, channels)] = (mixed_grad * conv).astype(BF)
+            if i == 0:
+                pl.when(has_earlier)(lambda: halo(slot).start())
+
+    def second_pass(slot):
+        pl.when(has_later)(lambda: halo(slot).wait_recv())
+        for i in range(chips):
+            span = pl.ds(i * tile, tile)
+            grad = 0.0
+            for offset in range(taps):
+                grad = grad + taps_ref[offset : offset + 1] * conv_grad[slot, pl.ds(i * tile + offset, tile)]
+            stacked[slot, span, pl.ds(0, channels)] = (grad * gates[slot, 2, span]).astype(BF)
+            stacked[slot, span, pl.ds(2 * channels, channels)] = (grad * gates[slot, 0, span]).astype(BF)
+
+    def third_pass(slot):
+        for chip in order:
+            span = pl.ds(chip * tile, tile)
+
+            @pl.loop(0, width // wide_block)
+            def _(i):
+                cut = pl.ds(pl.multiple_of(i * wide_block, wide_block), wide_block)
+                value = 0.0
+                for k in range(3):
+                    value = value + nt(stacked[slot, span, pl.ds(k * channels, channels)], in_full[k, cut])
+                part[slot, span, cut] = value.astype(BF)
+
+            sums[slot].give(chip)
+
+    def finish(what, total, slot):
+        def store(first, size, value):
+            total[slot, pl.ds(first, size)] = value
+
+        what[slot].finish(store)
+
+    def neighbours(act):
+        act(p.sibling)
+        pl.when(p.has_above)(lambda: act(p.above))
+        pl.when(p.has_below)(lambda: act(p.below))
+
+    def give_free(slot):
+        mlp_sums[slot].drain()
+        neighbours(
+            lambda where: pl.semaphore_signal(free.at[slot], inc=1, device_id=where, device_id_type=MESH)
+        )
+
+    def take_free(slot):
+        lines = (p.z + chips - 1) // chips + (2 * chips - 2 - p.z) // chips
+        pl.semaphore_wait(free.at[slot], 1 + lines)
+
+    def fetch_columns(index):
+        return pltpu.make_async_copy(
+            normed_rows.at[:, :, pl.ds(index * cols, cols)], columns.at[index % 2], cols_sem.at[index % 2]
+        )
+
+    steps_in = width // cols
+
+    def in_step(index):
+        fetch_columns(index).wait()
+        value = 0.0
+        for slot in range(slots):
+            value = value + tn(columns[index % 2, slot], stacked[slot])
+        for k in range(3):
+            in_full[k, pl.ds(index * cols, cols)] = value[:, k * channels : (k + 1) * channels].astype(BF)
+        if index + 2 < steps_in:
+            fetch_columns(index + 2).start()
+
+    def out_step():
+        for first in range(0, width, wide_block):
+            cut = pl.ds(first, wide_block)
+            value = 0.0
+            for slot in range(slots):
+                value = value + tn(mixed[slot], rows[slot, :, cut])
+            out_full[:, cut] = value.astype(BF)
+
+    spreads[0].start()
+    spreads[1].start()
+    gathers[0].start()
+    loads[0].wait()
+    for chip in order:
+        mlp_sums[0].give(chip)
+    hops, next_rows = mlp_sums[0].rounds(), gathers[0].rounds()
+    weave(hops[:-1], next_rows[:-1])
+    gathers[1].start()
+    weave(hops[-1:], next_rows[-1:])
+    loads[1].wait()
+    for chip in order:
+        mlp_sums[1].give(chip)
+    loads[2].wait()
+    for thing in loads[2 + slots :]:
+        thing.wait()
+    gathers[0].arrived()
+    fetch_columns(0).start()
+    fetch_columns(1).start()
+    mlp_hops, next_rows, hops = mlp_sums[1].rounds(), gathers[1].rounds(), sums[0].rounds()
+    first_pass(0)
+    finish(mlp_sums, mlp_total, 0)
+    give_free(0)
+    weave(mlp_hops[:1], next_rows[:1])
+    second_pass(0)
+    take_free(0)
+    third_pass(0)
+    weave(mlp_hops[1:], next_rows[1:], hops[:1])
+    loads[3].wait()
+    gathers[1].arrived()
+    first_pass(1)
+    finish(mlp_sums, mlp_total, 1)
+    give_free(1)
+    hops[1]()
+    second_pass(1)
+    take_free(1)
+    weave(hops[2:])
+    third_pass(1)
+    hops = sums[1].rounds()
+    hops[0]()
+    out_step()
+    spreads[3].start()
+    for index in range(steps_in):
+        in_step(index)
+    spreads[2].start()
+    weave(hops[1:])
+    finish(sums, grad_total, 0)
+    finish(sums, grad_total, 1)
+    last = [
+        pltpu.make_async_copy(mlp_total, mlp_out, load.at[0]),
+        pltpu.make_async_copy(grad_total, grad_out, load.at[1]),
+    ]
+    for thing in last:
+        thing.start()
+    for thing in spreads:
+        thing.finish()
+    for thing in last:
+        thing.wait()
+    for thing in gathers + sums:
+        thing.drain()
+    for slot in range(slots):
+        pl.when(has_earlier)(lambda slot=slot: halo(slot).wait_send())
+
+
+def mixer_backward(
+    seqs, models, low, mlp_part, taps, in_full, out_full, normed_rows, gates, product, mixed, pair_grad, down_grad
+):
+    slots, share, width = low.shape
+    chips = models // 2
+    block = share * models
+    channels = out_full.shape[0]
+    units = down_grad.shape[0]
+    hbm = pl.BlockSpec(memory_space=pltpu.HBM)
+    vmem = pl.BlockSpec(memory_space=pltpu.VMEM)
+    shape = jax.ShapeDtypeStruct
+    return pl.pallas_call(
+        functools.partial(mixer_backward_kernel, seqs, models),
+        out_shape=[
+            shape((slots, share, width), F32),
+            shape((slots, share, width), F32),
+            shape((8, channels), F32),
+            shape((seqs, 3, width // seqs, channels), BF),
+            shape((seqs, channels, width // seqs), BF),
+            shape((seqs, 2, width // seqs, units), BF),
+            shape((seqs, units, width // seqs), BF),
+        ],
+        in_specs=[hbm, hbm, vmem] + [hbm] * 8,
+        out_specs=[hbm, hbm, vmem] + [hbm] * 4,
+        scratch_shapes=[
+            pltpu.VMEM((3, width, channels), BF),
+            pltpu.VMEM((channels, width), BF),
+            pltpu.VMEM((slots, block, width), BF),
+            pltpu.VMEM((2, slots, block, 256), BF),
+            pltpu.VMEM((slots, 3, block, channels), F32),
+            pltpu.VMEM((slots, block + 8, channels), F32),
+            pltpu.VMEM((slots, block, channels), BF),
+            pltpu.VMEM((slots, block + 8, channels), F32),
+            pltpu.VMEM((slots, block, 3 * channels), BF),
+            pltpu.VMEM((slots, block, width), BF),
+            pltpu.VMEM((slots, chips, share, width), BF),
+            pltpu.VMEM((slots, chips + 1, share, width), BF),
+            pltpu.VMEM((slots, share, width), F32),
+            pltpu.VMEM((slots, share, width), F32),
+            pltpu.SemaphoreType.DMA((2 * slots + 5,)),
+            pltpu.SemaphoreType.DMA((2,)),
+            pltpu.SemaphoreType.DMA((4, seqs - 1)),
+            pltpu.SemaphoreType.DMA((4, seqs - 1)),
+            pltpu.SemaphoreType.DMA((4,)),
+            pltpu.SemaphoreType.DMA((slots,)),
+            pltpu.SemaphoreType.DMA((slots,)),
+            pltpu.SemaphoreType.REGULAR((slots,)),
+            *gather_sems(slots, chips),
+            *scatter_sems(2 * slots, chips),
+        ],
+        compiler_params=pltpu.CompilerParams(collective_id=3, has_side_effects=True, vmem_limit_bytes=VMEM_LIMIT),
+    )(low, mlp_part, taps, in_full, out_full, normed_rows, gates, product, mixed, pair_grad, down_grad)
+
+
+def small_sum_kernel(seqs, models, value_ref, out_ref, by_model, by_seq, send, recv, seq_send, seq_recv):
+    s, m = lax.axis_index("seq"), lax.axis_index("mp")
+    along = [{"mp": lax.rem(m + step, models)} for step in range(1, models)]
+    across = [{"seq": lax.rem(s + step, seqs)} for step in range(1, seqs)]
+    barrier = pltpu.get_barrier_semaphore()
+    for where in along + across:
+        pl.semaphore_signal(barrier, inc=1, device_id=where, device_id_type=MESH)
+    pl.semaphore_wait(barrier, models + seqs - 2)
+    by_model[m] = value_ref[...]
+    copies = [
+        remote(value_ref, by_model.at[m], send.at[i], recv.at[i], where) for i, where in enumerate(along)
+    ]
+    for thing in copies:
+        thing.start()
+    for thing in copies:
+        thing.wait()
+    by_seq[s] = functools.reduce(lambda a, b: a + b, [by_model[i] for i in range(models)])
+    copies = [
+        remote(by_seq.at[s], by_seq.at[s], seq_send.at[i], seq_recv.at[i], where) for i, where in enumerate(across)
+    ]
+    for thing in copies:
+        thing.start()
+    for thing in copies:
+        thing.wait()
+    out_ref[...] = functools.reduce(lambda a, b: a + b, [by_seq[i] for i in range(seqs)])
+
+
+def small_sum(seqs, models, value):
+    vmem = pl.BlockSpec(memory_space=pltpu.VMEM)
+    return pl.pallas_call(
+        functools.partial(small_sum_kernel, seqs, models),
+        out_shape=jax.ShapeDtypeStruct(value.shape, F32),
+        in_specs=[vmem],
+        out_specs=vmem,
+        scratch_shapes=[
+            pltpu.VMEM((models, *value.shape), F32),
+            pltpu.VMEM((seqs, *value.shape), F32),
+            pltpu.SemaphoreType.DMA((models - 1,)),
+            pltpu.SemaphoreType.DMA((models - 1,)),
+            pltpu.SemaphoreType.DMA((seqs - 1,)),
+            pltpu.SemaphoreType.DMA((seqs - 1,)),
+        ],
+        compiler_params=pltpu.CompilerParams(collective_id=4, has_side_effects=True),
+    )(value)
 
 
 def normalize(values, gain):
@@ -555,7 +1163,6 @@
     seq_pos = lax.axis_index("seq")
     model_pos = lax.axis_index("mp")
     slots, share, width = hidden.shape
-    block_rows = share * models
     channels = mixer_in.shape[2]
     taps = conv_weight.shape[0]
     local_taps = lax.dynamic_slice_in_dim(conv_weight, model_pos * channels, channels, 1)
@@ -573,7 +1180,7 @@
         pair_full,
         down_full,
         gates,
-        extended,
+        product,
         mixed,
         mix_share,
     ) = mixer_forward(
@@ -589,74 +1196,46 @@
     )
     middle = source + mix_share
     normed_two, scale_mlp = normalize(middle, gain_mlp)
-    normed_two = normed_two.astype(BF)
-    acts, pair_grads, mlp_rows, outputs, middle_grads, mixed_rows = [], [], [], [], [], []
-    stackeds, input_parts, tap_totals = [], [], []
-    for slot in range(slots):
-        rows = lax.all_gather(normed_two[slot], "mp", axis=0, tiled=True)
-        mlp_rows.append(rows)
-        gated = jnp.einsum("td,kdf->ktf", rows, pair_full, preferred_element_type=F32)
-        gate_part, up_part = gated[0], gated[1]
-        activated = jax.nn.silu(gate_part)
-        act = (activated * up_part).astype(BF)
-        acts.append(act)
-        outputs.append(scatter_sum(jnp.dot(act, down_full, preferred_element_type=F32), "mp", 0))
-        act_grad = jnp.einsum("td,fd->tf", top_rows[slot], down_full, preferred_element_type=F32)
-        sigma = jax.nn.sigmoid(gate_part)
-        gate_grad = (act_grad * up_part * sigma * (1.0 + gate_part * (1.0 - sigma))).astype(BF)
-        pair_grad = jnp.stack([gate_grad, (act_grad * activated).astype(BF)])
-        pair_grads.append(pair_grad)
-        middle_grads.append(
-            scatter_sum(jnp.einsum("ktf,kdf->td", pair_grad, pair_full, preferred_element_type=F32), "mp", 0)
-        )
-    output = (mask * (middle + jnp.stack(outputs))).astype(BF)
-    middle_grad, gain_mlp_grad = norm_back(jnp.stack(middle_grads), middle, scale_mlp, gain_mlp)
+    middle_grad, mlp_part, pair_total, down_total = mlp(
+        seqs, models, normed_two.astype(BF), top_rows, pair_full, down_full
+    )
+    middle_grad, gain_mlp_grad = norm_back(middle_grad, middle, scale_mlp, gain_mlp)
     middle_grad = middle_grad + top_grad
-    act, pair_grad, rows = jnp.stack(acts), jnp.stack(pair_grads), jnp.stack(mlp_rows)
-    down_total = jnp.einsum("stf,std->fd", act, top_rows, preferred_element_type=F32)
-    pair_total = jnp.einsum("std,sktf->kdf", rows, pair_grad, preferred_element_type=F32)
-    low_grad = middle_grad.astype(BF)
-    for slot in range(slots):
-        mix_rows = lax.all_gather(low_grad[slot], "mp", axis=0, tiled=True)
-        mixed_rows.append(mix_rows)
-        mixed_grad = jnp.einsum("td,cd->tc", mix_rows, out_full, preferred_element_type=F32)
-        ext = extended[slot]
-        conv_out = 0.0
-        for offset in range(taps):
-            conv_out = conv_out + local_taps[offset] * ext[8 - offset : 8 - offset + block_rows]
-        b_gate, c_gate, x_value = gates[slot, 0], gates[slot, 1], gates[slot, 2]
-        c_grad = mixed_grad * conv_out
-        conv_grad = mixed_grad * c_gate
-        later = shifted(conv_grad[: taps - 1], "seq", -1)
-        tail = jnp.concatenate([conv_grad, later], axis=0)
-        product_grad = jnp.zeros_like(conv_grad)
-        tap_rows = []
-        for offset in range(taps):
-            product_grad = product_grad + local_taps[offset] * tail[offset : offset + block_rows]
-            tap_rows.append(jnp.sum(conv_grad * ext[8 - offset : 8 - offset + block_rows], axis=0))
-        tap_totals.append(jnp.stack(tap_rows))
-        stacked = jnp.stack([product_grad * x_value, c_grad, product_grad * b_gate]).astype(BF)
-        stackeds.append(stacked)
-        input_parts.append(
-            scatter_sum(jnp.einsum("ktc,kdc->td", stacked, in_full, preferred_element_type=F32), "mp", 0)
-        )
-    out_total = jnp.einsum("stc,std->cd", mixed, jnp.stack(mixed_rows), preferred_element_type=F32)
-    in_total = jnp.einsum("std,sktc->kdc", normed_rows, jnp.stack(stackeds), preferred_element_type=F32)
-    source_grad, gain_mix_grad = norm_back(jnp.stack(input_parts), source, scale_mix, gain_mix)
-    taps_full = lax.dynamic_update_slice_in_dim(
-        jnp.zeros((taps, width), F32), tap_totals[0] + tap_totals[1], model_pos * channels, 1
+    mlp_share, source_grad, taps_part, in_got, out_got, pair_got, down_got = mixer_backward(
+        seqs,
+        models,
+        middle_grad.astype(BF),
+        mlp_part,
+        local_taps,
+        in_full,
+        out_full,
+        normed_rows,
+        gates,
+        product,
+        mixed,
+        pair_total,
+        down_total,
     )
-    gain_mix_grad, gain_mlp_grad, taps_grad = lax.psum((gain_mix_grad, gain_mlp_grad, taps_full), ("seq", "mp"))
+    output = (mask * (middle + mlp_share)).astype(BF)
+    source_grad, gain_mix_grad = norm_back(source_grad, source, scale_mix, gain_mix)
+    small = jnp.zeros((8, width), F32)
+    small = lax.dynamic_update_slice(small, taps_part[:taps], (2, model_pos * channels))
+    small = small.at[0].set(gain_mix_grad).at[1].set(gain_mlp_grad)
+    small = small_sum(seqs, models, small)
+
+    def total(got):
+        return jnp.sum(got.astype(F32), axis=0)
+
     return (
         output,
         source_grad + middle_grad,
-        gain_mix_grad,
-        gain_mlp_grad,
-        taps_grad,
-        scatter_sum(in_total, "seq", 1),
-        scatter_sum(out_total, "seq", 1),
-        scatter_sum(pair_total, "seq", 1),
-        scatter_sum(down_total, "seq", 1),
+        small[0],
+        small[1],
+        small[2 : 2 + taps],
+        total(in_got),
+        total(out_got),
+        total(pair_got),
+        total(down_got),
     )
 
 

time: 1080 us -> 804 us (0.74)
  waiting for transfers between devices: 592 us -> 0 us
  Pallas kernels: 191 us -> 748 us
  matrix products: 168 us -> 0 us
  blocking collectives: 40.5 us -> 0 us
  between operations: 14.7 us -> 1.21 us
  local copies, waits for them, and re-layouts: 20.4 us -> 8.19 us
    pallas_call x0 -> x3, Pallas kernels: none -> 558 us  [the longest x1 282 us: mlp(): pl.pallas_call(functools.partial(mlp_kernel, seqs, models), out_shape=[sh...]
    reduce_scatter x10 -> x0, waiting for transfers between devices: 361 us -> none  [scatter_sum(): lax.psum_scatter(low, axis, scatter_dimension=dim, tiled=True).astype(F32)]
    all_gather x4 -> x0, waiting for transfers between devices: 225 us -> none  [the longest x2 181 us: local(): rows = lax.all_gather(normed_two[slot], 'mp', axis=0, tiled=True)]
    dot_general x16 -> x0, matrix products: 168 us -> none  [the longest x2 25.4 us: local(): jnp.einsum('td,kdf->ktf', rows, pair_full, preferred_element_type=F32)]
    psum x1 -> x0, blocking collectives: 40.5 us -> none  [local(): lax.psum((gain_mix_grad, gain_mlp_grad, taps_full), ('seq', 'mp'))]
    convert_element_type x6 -> x2, other arithmetic: 17.2 us -> 4.11 us  [the longest x1 2.9 us: local(): middle_grad.astype(BF)]
    reduce_sum x0 -> x4, other arithmetic: none -> 12.5 us  [total(): return jnp.sum(got.astype(F32), axis=0)]
    unnamed x66 -> x28, local copies, waits for them, and re-layouts: 16.1 us -> 3.77 us
  transfers between devices with their start and end apart: 16 -> 0, of which waited for: 14 -> 0; matrix products, arithmetic and copies ran while one was open for 18% -> 0% of each run, Pallas kernels for 0% -> 0%
where the time goes in v3:
time: 804 us; the launch traced here: 794 us
  Pallas kernels  748 us (93%)
  other arithmetic  36 us (4%)
  local copies, waits for them, and re-layouts  8.19 us (1%)
    pallas_call x1, Pallas kernels, mlp(): pl.pallas_call(functools.partial(mlp_kernel, seqs, models), out_shape=[sh...  282 us
    pallas_call x1, Pallas kernels, mixer_backward(): pl.pallas_call(functools.partial(mixer_backward_kernel, seqs, models), ou...  248 us
    pallas_call x1, Pallas kernels, mixer_forward(): pl.pallas_call(functools.partial(mixer_forward_kernel, seqs, models), out...  191 us
    pallas_call x1, Pallas kernels, small_sum(): pl.pallas_call(functools.partial(small_sum_kernel, seqs, models), out_sha...  26.9 us

profile of v3, /device:TPU:0, one launch (start us, length us, event | category | flops | bytes accessed | tf_op | source)
XLA Modules:
  0.0 793.7 jit_solution(566529520138589846)
XLA Ops:
  0.6 0.0 copy-start
  0.7 0.7 copy-done
  1.4 0.6 constant_dynamic-slice_fusion.taps_ref
  2.0 0.7 compare_convert_fusion
  2.7 1.5 fusion.10
  4.2 3.3 fusion.4
  7.5 190.7 %shard_map.169 = (bf16[2,1024,2048]{2,1,0:T(8,128)(2,1)}, bf16[2,1024,2048]{2,1,0:T(8,128)(2,1)}, bf16[3,2048,256]{2,1,0:T(8,128)(2,1)}, bf16[256,2048]{1,0:T(8,...) custom-call(bf16[2,128,2048]{2,1,0:T(8,128)(2,1)} %get-tuple-element, ...), custom_call_target="tpu_custom_call" | custom-call | tf_op jit(solution)/shard_map/pallas_call | solution.py:478
  198.2 0.0 copy-start.11
  198.2 2.2 multiply_reduce_fusion.2
  200.4 0.0 copy-start.2
  200.4 1.3 copy-done.2
  201.7 0.0 copy-done.11
  201.7 1.2 multiply_convert_fusion.1.normed_ref
  202.9 282.4 %shard_map.170 = (f32[2,128,2048]{2,1,0:T(8,128)}, bf16[2,1024,2048]{2,1,0:T(8,128)(2,1)}, bf16[2,2048,1024]{2,1,0:T(8,128)(2,1)}, bf16[1024,2048]{1,0:T(8,128)(2,1)}) custom-call(bf16[2,128,2048]{2,1,0:T(8,128)(2,1)} %multiply_convert_fusion.1.normed_ref, bf16[2,1024,2048]{2,1,0:T(8,128)(2,1)} %get-tuple-element.55.top_rows, ...), custom_call_target="tpu_custom_call" | custom-call | tf_op jit(solution)/shard_map/pallas_call | solution.py:713
  485.3 0.0 copy-start.3
  485.4 0.0 copy-start.6
  485.4 2.9 multiply_reduce_fusion
  488.3 0.0 copy-done.3
  488.3 0.5 copy-done.6
  488.8 2.9 fusion.12.low_ref
  491.7 248.3 %shard_map.171 = (f32[2,128,2048]{2,1,0:T(8,128)}, f32[2,128,2048]{2,1,0:T(8,128)}, f32[8,256]{1,0:T(8,128)}, bf16[4,3,512,256]{3,2,1,0:T(8,128)(2,1)}, bf16[4,2...) custom-call(bf16[2,128,2048]{2,1,0:T(8,128)(2,1)} %fusion.12.low_ref, ...), custom_call_target="tpu_custom_call" | custom-call | tf_op jit(solution)/shard_map/pallas_call | solution.py:1048
  740.0 0.0 copy-start.13
  740.0 0.0 copy-start.5
  740.0 0.0 copy-start.12
  740.0 8.0 %convert_reduce_fusion = f32[2,512,1024]{2,1,0:T(8,128)} fusion(bf16[4,2,512,1024]{3,2,1,0:T(8,128)(2,1)} %get-tuple-element.73), kind=kLoop, calls=%fused_computation | loop fusion | flops 7340032 | bytes 12582912 | tf_op jit(solution)/shard_map/reduce_sum | solution.py:1227
  748.0 0.0 copy-start.4
  748.0 0.0 copy-done.13
  748.0 0.4 dynamic_update_slice.3
  748.5 0.0 copy-done.5
  748.5 0.0 copy-done.12
  748.5 2.4 fusion.9
  750.9 0.2 scatter.6
  751.1 0.2 scatter.9.value_ref
  751.3 0.0 copy-start.10
  751.3 0.6 copy-done.10
  751.9 26.9 %shard_map.172 = f32[8,2048]{1,0:T(8,128)} custom-call(f32[8,2048]{1,0:T(8,128)} %copy-done.10), custom_call_target="tpu_custom_call" | custom-call | tf_op jit(solution)/shard_map/pallas_call | solution.py:1120
  778.8 1.5 slice.45
  780.3 1.5 fusion.13
  781.8 0.0 copy-done.4
  781.8 0.0 copy-start.7
  781.8 6.4 fusion.8
  788.2 0.0 copy-done.7
  788.2 0.0 copy-start.8
  788.2 2.0 convert_reduce_fusion.1
  790.2 0.0 copy-start.1
  790.2 0.5 copy-done.8
  790.7 0.0 copy-start.9
  790.7 1.6 convert_reduce_fusion.2
  792.3 0.0 copy-done.9
  792.3 1.0 convert_reduce_fusion.3
  793.3 0.0 copy-done.1
  (7 shorter events, 0.0 us)
Async XLA Ops:
  0.6 0.8 copy-start
  198.2 3.6 copy-start.11
  200.4 1.3 copy-start.2
  485.3 2.9 copy-start.3
  485.4 3.5 copy-start.6
  740.0 8.0 %copy-start.13 = (f32[8,256]{1,0:T(8,128)S(1)}, f32[8,256]{1,0:T(8,128)}, u32[]{:S(2)}) copy-start(f32[8,256]{1,0:T(8,128)} %get-tuple-element.70) | copy-start | bytes 24580
  740.0 8.5 %copy-start.5 = (bf16[2,128,2048]{2,1,0:T(8,128)(2,1)S(1)}, bf16[2,128,2048]{2,1,0:T(8,128)(2,1)}, u32[]{:S(2)}) copy-start(bf16[2,128,2048]{2,1,0:T(8,128)(2,1)} %param.14) | copy-start | bytes 3145732
  740.0 8.5 %copy-start.12 = (f32[2048]{0:T(1024)S(1)}, f32[2048]{0:T(1024)}, u32[]{:S(2)}) copy-start(f32[2048]{0:T(1024)} %param.17) | copy-start | bytes 24580
  748.0 33.8 %copy-start.4 = (f32[2,128,2048]{2,1,0:T(8,128)S(1)}, f32[2,128,2048]{2,1,0:T(8,128)}, u32[]{:S(2)}) copy-start(f32[2,128,2048]{2,1,0:T(8,128)} %copy-done.2) | copy-start | bytes 6291460
  751.3 0.6 copy-start.10
  781.8 6.4 copy-start.7
  788.2 2.5 copy-start.8
  790.2 3.1 copy-start.1
  790.7 1.6 copy-start.9

commit v4 on v3

--- a/solution.py
+++ b/solution.py
@@ -111,12 +111,15 @@
     def rounds(self):
         return [functools.partial(self.round, k) for k in range(1, self.p.chips)]
 
+    def other_core(self, chip):
+        p = self.p
+        for half in range(HALVES):
+            dst = self.at(chip, 1 - p.c, half)
+            remote(dst, dst, self.send.at[2, chip, half], self.recv.at[1, chip, half], p.sibling).wait_recv()
+
     def arrived(self):
-        p = self.p
-        for chip in range(p.chips):
-            for half in range(HALVES):
-                dst = self.at(chip, 1 - p.c, half)
-                remote(dst, dst, self.send.at[2, chip, half], self.recv.at[1, chip, half], p.sibling).wait_recv()
+        for chip in range(self.p.chips):
+            self.other_core(chip)
 
     def drain(self):
         p = self.p
@@ -417,9 +420,8 @@
     firsts[0].arrived()
     weights[0].arrived()
     weights[1].arrived()
-    weights[2].start()
+    project(0)
     weights[3].start()
-    project(0)
     steps = firsts[1].rounds()
     steps[0]()
     convolve(0)
@@ -429,6 +431,7 @@
     own(1, rows, normed_ref).wait()
     firsts[1].arrived()
     project(1)
+    weights[2].start()
     steps = tops[0].rounds()
     steps[0]()
     convolve(1)
@@ -568,7 +571,7 @@
             normed_ref.at[slot], rows.at[slot, pl.ds(p.m * share, share)], load.at[2 + slot]
         )
 
-    order = far_first(p)
+    order = far_first(p)[::-1]
     tiles = [(slot, chip) for slot in range(slots) for chip in order]
 
     def fetch(index):
@@ -653,37 +656,37 @@
         own(slot).start()
     fetch(0).start()
     gathers[0].start()
-    steps = gathers[0].rounds()
-    for step in steps[:-1]:
-        step()
-    gathers[1].start()
-    steps[-1]()
     own(0).wait()
-    gathers[0].arrived()
+    own(1).wait()
     for thing in loads:
         thing.wait()
-    next_rows = gathers[1].rounds()
+    for index in range(chips):
+        if index:
+            gathers[0].round(index)
+        if index == chips - 2:
+            gathers[1].start()
+        gathers[0].other_core(order[index])
+        work(index)
     hops = sums[0].rounds()
     for index in range(chips):
-        work(index)
         if index < len(hops):
             hops[index]()
-            next_rows[index]()
-    own(1).wait()
-    gathers[1].arrived()
+        if index:
+            gathers[1].round(index)
+        gathers[1].other_core(order[index])
+        work(chips + index)
     hops = sums[1].rounds()
-    for index in range(chips):
-        work(chips + index)
-        if index == 0:
-            finish(0)
-        if index < len(hops):
-            hops[index]()
+    hops[0]()
+    finish(0)
     fetch_columns(0).start()
     fetch_columns(1).start()
-    for index in range(pair_steps):
-        pair_step(index)
-    for index in range(width // columns):
-        down_step(index)
+    work_steps = [functools.partial(pair_step, index) for index in range(pair_steps)]
+    work_steps += [functools.partial(down_step, index) for index in range(width // columns)]
+    spaced = len(work_steps) // len(hops)
+    for index, step in enumerate(work_steps):
+        step()
+        if (index + 1) % spaced == 0 and (index + 1) // spaced < len(hops):
+            hops[(index + 1) // spaced]()
     finish(1)
     last = [
         pltpu.make_async_copy(down, down_grad, keep.at[pair_steps]),
@@ -757,14 +760,14 @@
         p = self.p
         return remote(
             self.block(lax.rem(p.s + step, p.seqs)),
-            self.got.at[step],
+            self.got(step),
             self.send.at[step - 1],
             self.recv.at[step - 1],
             p.peer(step),
         )
 
     def local_copy(self):
-        return pltpu.make_async_copy(self.block(self.p.s), self.got.at[0], self.local)
+        return pltpu.make_async_copy(self.block(self.p.s), self.got(0), self.local)
 
     def start(self):
         for step in range(1, self.p.seqs):
@@ -862,7 +865,13 @@
     spreads = [
         Spread(p, partial, got, (w_send.at[i], w_recv.at[i], w_local.at[i]))
         for i, (partial, got) in enumerate(
-            ((pair_grad, pair_got), (down_grad, down_got), (in_full, in_got), (out_full, out_got))
+            (
+                (pair_grad.at[pl.ds(0, 1)], lambda step: pair_got.at[step, pl.ds(0, 1)]),
+                (down_grad, lambda step: down_got.at[step]),
+                (in_full, lambda step: in_got.at[step]),
+                (out_full, lambda step: out_got.at[step]),
+                (pair_grad.at[pl.ds(1, 1)], lambda step: pair_got.at[step, pl.ds(1, 1)]),
+            )
         )
     ]
     has_later, has_earlier = p.s < seqs - 1, p.s > 0
@@ -970,7 +979,6 @@
                 value = value + tn(mixed[slot], rows[slot, :, cut])
             out_full[:, cut] = value.astype(BF)
 
-    spreads[0].start()
     spreads[1].start()
     gathers[0].start()
     loads[0].wait()
@@ -991,6 +999,7 @@
     fetch_columns(1).start()
     mlp_hops, next_rows, hops = mlp_sums[1].rounds(), gathers[1].rounds(), sums[0].rounds()
     first_pass(0)
+    spreads[0].start()
     finish(mlp_sums, mlp_total, 0)
     give_free(0)
     weave(mlp_hops[:1], next_rows[:1])
@@ -1001,6 +1010,7 @@
     loads[3].wait()
     gathers[1].arrived()
     first_pass(1)
+    spreads[4].start()
     finish(mlp_sums, mlp_total, 1)
     give_free(1)
     hops[1]()
@@ -1075,9 +1085,9 @@
             pltpu.VMEM((slots, share, width), F32),
             pltpu.SemaphoreType.DMA((2 * slots + 5,)),
             pltpu.SemaphoreType.DMA((2,)),
-            pltpu.SemaphoreType.DMA((4, seqs - 1)),
-            pltpu.SemaphoreType.DMA((4, seqs - 1)),
-            pltpu.SemaphoreType.DMA((4,)),
+            pltpu.SemaphoreType.DMA((5, seqs - 1)),
+            pltpu.SemaphoreType.DMA((5, seqs - 1)),
+            pltpu.SemaphoreType.DMA((5,)),
             pltpu.SemaphoreType.DMA((slots,)),
             pltpu.SemaphoreType.DMA((slots,)),
             pltpu.SemaphoreType.REGULAR((slots,)),
@@ -1090,15 +1100,21 @@
 
 def small_sum_kernel(seqs, models, value_ref, out_ref, by_model, by_seq, send, recv, seq_send, seq_recv):
     s, m = lax.axis_index("seq"), lax.axis_index("mp")
-    along = [{"mp": lax.rem(m + step, models)} for step in range(1, models)]
-    across = [{"seq": lax.rem(s + step, seqs)} for step in range(1, seqs)]
+    cols = by_seq.shape[-1]
+    along = [lax.rem(m + step, models) for step in range(1, models)]
+    across = [lax.rem(s + step, seqs) for step in range(1, seqs)]
+
+    def span(owner):
+        return pl.ds(pl.multiple_of(owner * cols, cols), cols)
+
     barrier = pltpu.get_barrier_semaphore()
-    for where in along + across:
+    for where in [{"mp": peer} for peer in along] + [{"seq": peer} for peer in across]:
         pl.semaphore_signal(barrier, inc=1, device_id=where, device_id_type=MESH)
     pl.semaphore_wait(barrier, models + seqs - 2)
-    by_model[m] = value_ref[...]
+    by_model[m] = value_ref[:, span(m)]
     copies = [
-        remote(value_ref, by_model.at[m], send.at[i], recv.at[i], where) for i, where in enumerate(along)
+        remote(value_ref.at[:, span(peer)], by_model.at[m], send.at[0, i], recv.at[0, i], {"mp": peer})
+        for i, peer in enumerate(along)
     ]
     for thing in copies:
         thing.start()
@@ -1106,27 +1122,38 @@
         thing.wait()
     by_seq[s] = functools.reduce(lambda a, b: a + b, [by_model[i] for i in range(models)])
     copies = [
-        remote(by_seq.at[s], by_seq.at[s], seq_send.at[i], seq_recv.at[i], where) for i, where in enumerate(across)
+        remote(by_seq.at[s], by_seq.at[s], seq_send.at[i], seq_recv.at[i], {"seq": peer})
+        for i, peer in enumerate(across)
     ]
     for thing in copies:
         thing.start()
     for thing in copies:
         thing.wait()
-    out_ref[...] = functools.reduce(lambda a, b: a + b, [by_seq[i] for i in range(seqs)])
+    out_ref[:, span(m)] = functools.reduce(lambda a, b: a + b, [by_seq[i] for i in range(seqs)])
+    copies = [
+        remote(out_ref.at[:, span(m)], out_ref.at[:, span(m)], send.at[1, i], recv.at[1, i], {"mp": peer})
+        for i, peer in enumerate(along)
+    ]
+    for thing in copies:
+        thing.start()
+    for thing in copies:
+        thing.wait()
 
 
 def small_sum(seqs, models, value):
     vmem = pl.BlockSpec(memory_space=pltpu.VMEM)
+    height, width = value.shape
+    cols = width // models
     return pl.pallas_call(
         functools.partial(small_sum_kernel, seqs, models),
         out_shape=jax.ShapeDtypeStruct(value.shape, F32),
         in_specs=[vmem],
         out_specs=vmem,
         scratch_shapes=[
-            pltpu.VMEM((models, *value.shape), F32),
-            pltpu.VMEM((seqs, *value.shape), F32),
-            pltpu.SemaphoreType.DMA((models - 1,)),
-            pltpu.SemaphoreType.DMA((models - 1,)),
+            pltpu.VMEM((models, height, cols), F32),
+            pltpu.VMEM((seqs, height, cols), F32),
+            pltpu.SemaphoreType.DMA((2, models - 1)),
+            pltpu.SemaphoreType.DMA((2, models - 1)),
             pltpu.SemaphoreType.DMA((seqs - 1,)),
             pltpu.SemaphoreType.DMA((seqs - 1,)),
         ],

time: 804 us -> 601 us (0.75)
  Pallas kernels: 748 us -> 547 us
    pallas_call x1, Pallas kernels: 282 us -> 149 us  [mlp(): pl.pallas_call(functools.partial(mlp_kernel, seqs, models), out_shape=[sh...]
    pallas_call x1, Pallas kernels: 248 us -> 190 us  [mixer_backward(): pl.pallas_call(functools.partial(mixer_backward_kernel, seqs, models), ou...]
    pallas_call x1, Pallas kernels: 26.9 us -> 13.8 us  [small_sum(): pl.pallas_call(functools.partial(small_sum_kernel, seqs, models), out_sha...]
where the time goes in v4:
time: 601 us; the launch traced here: 592 us
  Pallas kernels  547 us (91%)
  other arithmetic  36 us (6%)
  local copies, waits for them, and re-layouts  8.19 us (1%)
    pallas_call x1, Pallas kernels, mixer_forward(): pl.pallas_call(functools.partial(mixer_forward_kernel, seqs, models), out...  195 us
    pallas_call x1, Pallas kernels, mixer_backward(): pl.pallas_call(functools.partial(mixer_backward_kernel, seqs, models), ou...  190 us
    pallas_call x1, Pallas kernels, mlp(): pl.pallas_call(functools.partial(mlp_kernel, seqs, models), out_shape=[sh...  149 us
    pallas_call x1, Pallas kernels, small_sum(): pl.pallas_call(functools.partial(small_sum_kernel, seqs, models), out_sha...  13.8 us
    reduce_sum x4, other arithmetic, total(): return jnp.sum(got.astype(F32), axis=0)  12.5 us

profile of v4, /device:TPU:0, one launch (start us, length us, event | category | flops | bytes accessed | tf_op | source)
XLA Modules:
  0.0 592.4 jit_solution(5597301011488734192)
XLA Ops:
  0.6 0.0 copy-start
  0.7 0.7 copy-done
  1.4 0.6 constant_dynamic-slice_fusion.taps_ref
  2.0 0.7 compare_convert_fusion
  2.7 1.5 fusion.10
  4.2 3.3 fusion.4
  7.5 194.6 %shard_map.169 = (bf16[2,1024,2048]{2,1,0:T(8,128)(2,1)}, bf16[2,1024,2048]{2,1,0:T(8,128)(2,1)}, bf16[3,2048,256]{2,1,0:T(8,128)(2,1)}, bf16[256,2048]{1,0:T(8,...) custom-call(bf16[2,128,2048]{2,1,0:T(8,128)(2,1)} %get-tuple-element, ...), custom_call_target="tpu_custom_call" | custom-call | tf_op jit(solution)/shard_map/pallas_call | solution.py:481
  202.1 0.0 copy-start.11
  202.1 2.2 multiply_reduce_fusion.2
  204.4 0.0 copy-start.2
  204.4 1.3 copy-done.2
  205.7 0.0 copy-done.11
  205.7 1.2 multiply_convert_fusion.1.normed_ref
  206.9 149.2 %shard_map.170 = (f32[2,128,2048]{2,1,0:T(8,128)}, bf16[2,1024,2048]{2,1,0:T(8,128)(2,1)}, bf16[2,2048,1024]{2,1,0:T(8,128)(2,1)}, bf16[1024,2048]{1,0:T(8,128)(2,1)}) custom-call(bf16[2,128,2048]{2,1,0:T(8,128)(2,1)} %multiply_convert_fusion.1.normed_ref, bf16[2,1024,2048]{2,1,0:T(8,128)(2,1)} %get-tuple-element.55.top_rows, ...), custom_call_target="tpu_custom_call" | custom-call | tf_op jit(solution)/shard_map/pallas_call | solution.py:716
  356.1 0.0 copy-start.3
  356.1 0.0 copy-start.6
  356.1 2.9 multiply_reduce_fusion
  359.1 0.0 copy-done.3
  359.1 0.5 copy-done.6
  359.6 2.9 fusion.12.low_ref
  362.5 189.5 %shard_map.171 = (f32[2,128,2048]{2,1,0:T(8,128)}, f32[2,128,2048]{2,1,0:T(8,128)}, f32[8,256]{1,0:T(8,128)}, bf16[4,3,512,256]{3,2,1,0:T(8,128)(2,1)}, bf16[4,2...) custom-call(bf16[2,128,2048]{2,1,0:T(8,128)(2,1)} %fusion.12.low_ref, ...), custom_call_target="tpu_custom_call" | custom-call | tf_op jit(solution)/shard_map/pallas_call | solution.py:1058
  552.0 0.0 copy-start.13
  552.0 0.0 copy-start.5
  552.0 0.0 copy-start.12
  552.0 8.0 %convert_reduce_fusion = f32[2,512,1024]{2,1,0:T(8,128)} fusion(bf16[4,2,512,1024]{3,2,1,0:T(8,128)(2,1)} %get-tuple-element.73), kind=kLoop, calls=%fused_computation | loop fusion | flops 7340032 | bytes 12582912 | tf_op jit(solution)/shard_map/reduce_sum | solution.py:1254
  560.0 0.0 copy-start.4
  560.0 0.0 copy-done.13
  560.0 0.4 dynamic_update_slice.3
  560.5 0.0 copy-done.5
  560.5 0.0 copy-done.12
  560.5 2.4 fusion.9
  562.9 0.2 scatter.6
  563.1 0.2 scatter.9.value_ref
  563.3 0.0 copy-start.10
  563.3 0.6 copy-done.10
  563.9 13.8 %shard_map.172 = f32[8,2048]{1,0:T(8,128)} custom-call(f32[8,2048]{1,0:T(8,128)} %copy-done.10), custom_call_target="tpu_custom_call" | custom-call | tf_op jit(solution)/shard_map/pallas_call | solution.py:1147
  577.7 1.5 slice.45
  579.1 1.5 fusion.13
  580.7 0.0 copy-done.4
  580.7 0.0 copy-start.7
  580.7 6.4 %fusion.8 = (f32[2,128,2048]{2,1,0:T(8,128)}, bf16[2,128,2048]{2,1,0:T(8,128)(2,1)}) fusion(bf16[2,128,2048]{2,1,0:T(8,128)(2,1)S(1)} %copy-done.5, f32[2,128,2048]{2,1,0:T(8,128)} %get-tuple-element.69, f32[2,128]{1,0:T(2,128)S(1)} %broadcast_multiply_fusion, f32[2048]{0:T(1024)S(1)} %copy-done.12, f32[2,128]{1,0:T(2,128)S(1)} %add_rsqrt_fusion.1, ...), kind=kLoop, calls=%fused_computation.14 | loop fusion | flops 9437184 | bytes 13652992 | tf_op jit(solution)/shard_map/add | solution.py:1258
  587.0 0.0 copy-done.7
  587.0 0.0 copy-start.8
  587.0 2.0 convert_reduce_fusion.1
  589.0 0.0 copy-start.1
  589.0 0.5 copy-done.8
  589.5 0.0 copy-start.9
  589.5 1.6 convert_reduce_fusion.2
  591.2 0.0 copy-done.9
  591.2 1.0 convert_reduce_fusion.3
  592.1 0.0 copy-done.1
  (7 shorter events, 0.0 us)
Async XLA Ops:
  0.6 0.8 copy-start
  202.1 3.6 copy-start.11
  204.4 1.3 copy-start.2
  356.1 2.9 copy-start.3
  356.1 3.5 copy-start.6
  552.0 8.0 %copy-start.13 = (f32[8,256]{1,0:T(8,128)S(1)}, f32[8,256]{1,0:T(8,128)}, u32[]{:S(2)}) copy-start(f32[8,256]{1,0:T(8,128)} %get-tuple-element.70) | copy-start | bytes 24580
  552.0 8.5 %copy-start.5 = (bf16[2,128,2048]{2,1,0:T(8,128)(2,1)S(1)}, bf16[2,128,2048]{2,1,0:T(8,128)(2,1)}, u32[]{:S(2)}) copy-start(bf16[2,128,2048]{2,1,0:T(8,128)(2,1)} %param.14) | copy-start | bytes 3145732
  552.0 8.5 %copy-start.12 = (f32[2048]{0:T(1024)S(1)}, f32[2048]{0:T(1024)}, u32[]{:S(2)}) copy-start(f32[2048]{0:T(1024)} %param.17) | copy-start | bytes 24580
  560.0 20.7 %copy-start.4 = (f32[2,128,2048]{2,1,0:T(8,128)S(1)}, f32[2,128,2048]{2,1,0:T(8,128)}, u32[]{:S(2)}) copy-start(f32[2,128,2048]{2,1,0:T(8,128)} %copy-done.2) | copy-start | bytes 6291460
  563.3 0.6 copy-start.10
  580.7 6.4 %copy-start.7 = (bf16[4,1024,512]{2,1,0:T(8,128)(2,1)S(1)}, bf16[4,1024,512]{2,1,0:T(8,128)(2,1)}, u32[]{:S(2)}) copy-start(bf16[4,1024,512]{2,1,0:T(8,128)(2,1)} %get-tuple-element.74) | copy-start | bytes 12582916
  587.0 2.5 copy-start.8
  589.0 3.1 copy-start.1
  589.5 1.6 copy-start.9

commit v5 on v4

--- a/solution.py
+++ b/solution.py
@@ -259,42 +259,69 @@
                 steps[step]()
 
 
-class Shards:
-    def __init__(self, place, shard, full, dim, sems):
-        self.p, self.shard, self.full, self.dim = place, shard, full, dim
+class Relay:
+    def __init__(self, place, shard, full, first, size, sems):
+        self.p, self.shard, self.full, self.first, self.size = place, shard, full, first, size
         self.send, self.recv, self.local = sems
-
-    def at(self, owner):
-        size = self.shard.shape[self.dim]
-        span = pl.ds(pl.multiple_of(owner * size, size), size)
-        return self.full.at[(slice(None),) * self.dim + (span,)]
-
-    def copy(self, step):
-        p = self.p
-        return remote(self.shard, self.at(p.s), self.send.at[step - 1], self.recv.at[step - 1], p.peer(step))
+        s = place.s
+        self.square = place.seqs == 4
+        if self.square:
+            self.near = (s + 1 - 2 * lax.rem(s, 2), lax.rem(s + 2, 4))
+
+    def half(self, index):
+        return self.first + index * (self.size // 2), self.size // 2
+
+    def direct(self, index, where):
+        return remote(
+            self.shard(self.first, self.size),
+            self.full(self.p.s, self.first, self.size),
+            self.send.at[index],
+            self.recv.at[index],
+            where,
+        )
+
+    def handed(self, index):
+        view = self.full(self.near[index], *self.half(index))
+        return remote(view, view, self.send.at[2 + index], self.recv.at[2 + index], {"seq": self.near[1 - index]})
 
     def local_copy(self):
-        return pltpu.make_async_copy(self.shard, self.at(self.p.s), self.local)
+        return pltpu.make_async_copy(
+            self.shard(self.first, self.size), self.full(self.p.s, self.first, self.size), self.local
+        )
+
+    def copies(self):
+        if self.square:
+            return [self.direct(index, {"seq": self.near[index]}) for index in range(2)]
+        return [self.direct(step - 1, self.p.peer(step)) for step in range(1, self.p.seqs)]
 
     def start(self):
-        for step in range(1, self.p.seqs):
-            self.copy(step).start()
+        for thing in self.copies():
+            thing.start()
         self.local_copy().start()
+
+    def forward(self):
+        if self.square:
+            for thing in self.copies():
+                thing.wait_recv()
+            for index in range(2):
+                self.handed(index).start()
 
     def arrived(self):
         self.local_copy().wait()
-        for step in range(1, self.p.seqs):
-            self.copy(step).wait_recv()
+        for thing in [self.handed(index) for index in range(2)] if self.square else self.copies():
+            thing.wait_recv()
 
     def drain(self):
-        for step in range(1, self.p.seqs):
-            self.copy(step).wait_send()
-
-
-def mixer_forward_kernel(
+        for thing in self.copies() + ([self.handed(index) for index in range(2)] if self.square else []):
+            thing.wait_send()
+
+
+def forward_kernel(
     seqs,
     models,
     normed_ref,
+    source_ref,
+    gain_ref,
     top_ref,
     taps_ref,
     in_ref,
@@ -305,18 +332,28 @@
     top_rows,
     in_rows,
     out_rows,
-    pair_rows,
-    down_rows,
     gates_out,
     product_out,
     mixed_out,
-    mix_out,
+    middle_out,
+    grad_out,
+    mlp_part,
+    act_rows,
+    pair_grad,
+    down_grad,
     in_full,
     out_full,
     rows,
     gates,
+    ends,
     product,
     mixed,
+    pair,
+    down,
+    top_tile,
+    acts,
+    act_stage,
+    stage,
     part,
     from_core,
     from_line,
@@ -327,224 +364,11 @@
     halo_send,
     halo_recv,
     keep,
-    *sems,
-):
-    p = Place(seqs, models)
-    chips = p.chips
-    g_sems, s_sems = sems[:2], sems[2:]
-    slots, block = rows.shape[0], rows.shape[1]
-    tile = block // chips
-    share = tile // 2
-    channels = in_full.shape[2]
-    p.enter()
-
-    firsts = [Gather(p, rows.at[slot], normed_ref.at[slot], picks(g_sems, slot)) for slot in range(slots)]
-    tops = [Gather(p, top_rows.at[slot], top_ref.at[slot], picks(g_sems, slots + slot)) for slot in range(slots)]
-    sums = [
-        Scatter(p, part.at[slot], from_core.at[slot], from_line.at[slot], picks(s_sems, slot)) for slot in range(slots)
-    ]
-    weights = [
-        Shards(p, shard, full, dim, (w_send.at[i], w_recv.at[i], w_local.at[i]))
-        for i, (shard, full, dim) in enumerate(
-            ((in_ref, in_full, 1), (out_ref, out_full, 1), (pair_ref, pair_rows, 1), (down_ref, down_rows, 1))
-        )
-    ]
-
-    def own(slot, which, source):
-        span = pl.ds(p.m * share, share)
-        return pltpu.make_async_copy(source.at[slot], which.at[slot, span], keep.at[slot + (slots if which is top_rows else 0)])
-
-    for slot in range(slots):
-        own(slot, rows, normed_ref).start()
-        own(slot, top_rows, top_ref).start()
-
-    def halo(slot):
-        return remote(
-            product.at[slot, pl.ds(block, 8)],
-            product.at[slot, pl.ds(0, 8)],
-            halo_send.at[slot],
-            halo_recv.at[slot],
-            p.peer(1),
-        )
-
-    has_later, has_earlier = p.s < seqs - 1, p.s > 0
-    for slot in range(slots):
-
-        @pl.when(jnp.logical_not(has_earlier))
-        def _(slot=slot):
-            product[slot, pl.ds(0, 8)] = jnp.zeros((8, channels), F32)
-
-    def project(slot):
-        @pl.loop(0, chips)
-        def _(i):
-            span = pl.ds(i * tile, tile)
-            source = rows[slot, span]
-            b_gate = nn(source, in_full[0])
-            x_value = nn(source, in_full[2])
-            gates[slot, 0, span] = b_gate
-            gates[slot, 1, span] = nn(source, in_full[1])
-            gates[slot, 2, span] = x_value
-            product[slot, pl.ds(8 + i * tile, tile)] = b_gate * x_value
-
-        pl.when(has_later)(lambda: halo(slot).start())
-
-    def convolve(slot):
-        pl.when(has_earlier)(lambda: halo(slot).wait_recv())
-        for i in range(chips):
-            conv = 0.0
-            for offset in range(taps_ref.shape[0]):
-                conv = conv + taps_ref[offset : offset + 1] * product[slot, pl.ds(8 + i * tile - offset, tile)]
-            mixed[slot, pl.ds(i * tile, tile)] = (gates[slot, 1, pl.ds(i * tile, tile)] * conv).astype(BF)
-
-    def project_out(slot):
-        for chip in far_first(p):
-            span = pl.ds(chip * tile, tile)
-            part[slot, span] = nn(mixed[slot, span], out_full[...]).astype(BF)
-            sums[slot].give(chip)
-
-    def finish(slot):
-        def store(first, size, value):
-            total[slot, pl.ds(first, size)] = value
-
-        sums[slot].finish(store)
-
-    firsts[0].start()
-    weights[0].start()
-    weights[1].start()
-    steps = firsts[0].rounds()
-    for step in steps[:-1]:
-        step()
-    firsts[1].start()
-    steps[-1]()
-    own(0, rows, normed_ref).wait()
-    firsts[0].arrived()
-    weights[0].arrived()
-    weights[1].arrived()
-    project(0)
-    weights[3].start()
-    steps = firsts[1].rounds()
-    steps[0]()
-    convolve(0)
-    project_out(0)
-    weave(sums[0].rounds(), steps[1:])
-    tops[0].start()
-    own(1, rows, normed_ref).wait()
-    firsts[1].arrived()
-    project(1)
-    weights[2].start()
-    steps = tops[0].rounds()
-    steps[0]()
-    convolve(1)
-    project_out(1)
-    finish(0)
-    weave(sums[1].rounds(), steps[1:])
-    tops[1].start()
-    finish(1)
-    stores = [
-        pltpu.make_async_copy(src, dst, keep.at[2 * slots + i])
-        for i, (src, dst) in enumerate(
-            (
-                (rows, normed_rows),
-                (in_full, in_rows),
-                (out_full, out_rows),
-                (gates, gates_out),
-                (product, product_out),
-                (mixed, mixed_out),
-                (total, mix_out),
-            )
-        )
-    ]
-    for store in stores:
-        store.start()
-    weave(tops[1].rounds())
-    for slot in range(slots):
-        own(slot, top_rows, top_ref).wait()
-        tops[slot].arrived()
-    weights[2].arrived()
-    weights[3].arrived()
-    for store in stores:
-        store.wait()
-    for thing in firsts + tops + sums + weights:
-        thing.drain()
-    for slot in range(slots):
-        pl.when(has_later)(lambda slot=slot: halo(slot).wait_send())
-
-
-def mixer_forward(seqs, models, normed, top, taps, mixer_in, mixer_out, gate_up, mlp_down):
-    slots, share, width = normed.shape
-    chips = models // 2
-    block = share * models
-    channels = mixer_in.shape[2]
-    units = gate_up.shape[2]
-    hbm = pl.BlockSpec(memory_space=pltpu.HBM)
-    shape = jax.ShapeDtypeStruct
-    return pl.pallas_call(
-        functools.partial(mixer_forward_kernel, seqs, models),
-        out_shape=[
-            shape((slots, block, width), BF),
-            shape((slots, block, width), BF),
-            shape((3, width, channels), BF),
-            shape((channels, width), BF),
-            shape((2, width, units), BF),
-            shape((units, width), BF),
-            shape((slots, 3, block, channels), F32),
-            shape((slots, block + 8, channels), F32),
-            shape((slots, block, channels), BF),
-            shape((slots, share, width), F32),
-        ],
-        in_specs=[hbm, hbm, pl.BlockSpec(memory_space=pltpu.VMEM)] + [hbm] * 4,
-        out_specs=[hbm] * 10,
-        scratch_shapes=[
-            pltpu.VMEM((3, width, channels), BF),
-            pltpu.VMEM((channels, width), BF),
-            pltpu.VMEM((slots, block, width), BF),
-            pltpu.VMEM((slots, 3, block, channels), F32),
-            pltpu.VMEM((slots, block + 8, channels), F32),
-            pltpu.VMEM((slots, block, channels), BF),
-            pltpu.VMEM((slots, block, width), BF),
-            pltpu.VMEM((slots, chips, share, width), BF),
-            pltpu.VMEM((slots, chips + 1, share, width), BF),
-            pltpu.VMEM((slots, share, width), F32),
-            pltpu.SemaphoreType.DMA((4, seqs - 1)),
-            pltpu.SemaphoreType.DMA((4, seqs - 1)),
-            pltpu.SemaphoreType.DMA((4,)),
-            pltpu.SemaphoreType.DMA((slots,)),
-            pltpu.SemaphoreType.DMA((slots,)),
-            pltpu.SemaphoreType.DMA((2 * slots + 7,)),
-            *gather_sems(2 * slots, chips),
-            *scatter_sems(slots, chips),
-        ],
-        compiler_params=pltpu.CompilerParams(collective_id=1, has_side_effects=True, vmem_limit_bytes=VMEM_LIMIT),
-    )(normed, top, taps, mixer_in, mixer_out, gate_up, mlp_down)
-
-
-def mlp_kernel(
-    seqs,
-    models,
-    normed_ref,
-    top_rows,
-    pair_ref,
-    down_ref,
-    grad_out,
-    mlp_part,
-    pair_grad,
-    down_grad,
-    pair,
-    down,
-    rows,
-    top_tile,
-    top_cols,
-    acts,
-    stage,
-    part,
-    from_core,
-    from_line,
-    total,
-    load,
     tile_sem,
+    out_sem,
     cols_sem,
-    stage_sem,
-    keep,
+    pair_sem,
+    ends_sem,
     *sems,
 ):
     p = Place(seqs, models)
@@ -554,47 +378,199 @@
     units = down.shape[0]
     tile = block // chips
     share = tile // 2
+    channels = in_full.shape[2]
+    shard = width // seqs
     unit_block = min(512, units)
     wide_block = 512
-    columns = top_cols.shape[-1]
-    loads = [pltpu.make_async_copy(pair_ref, pair, load.at[0]), pltpu.make_async_copy(down_ref, down, load.at[1])]
-    for thing in loads:
-        thing.start()
     p.enter()
-    gathers = [Gather(p, rows.at[slot], normed_ref.at[slot], picks(g_sems, slot)) for slot in range(slots)]
-    sums = [
-        Scatter(p, part.at[slot], from_core.at[slot], from_line.at[slot], picks(s_sems, slot)) for slot in range(slots)
+
+    firsts = [Gather(p, rows.at[slot], normed_ref.at[slot], picks(g_sems, slot)) for slot in range(slots)]
+    tops = [Gather(p, top_rows.at[slot], top_ref.at[slot], picks(g_sems, slots + slot)) for slot in range(slots)]
+    seconds = [Gather(p, rows.at[slot], None, picks(g_sems, 2 * slots + slot)) for slot in range(slots)]
+
+    def scatter(slot, index):
+        return Scatter(p, part.at[slot], from_core.at[slot], from_line.at[slot], picks(s_sems, index))
+
+    mix_sums = [scatter(slot, slot) for slot in range(slots)]
+    grad_sums = [scatter(slot, slots + slot) for slot in range(slots)]
+
+    def columns_of(owner):
+        return pl.ds(pl.multiple_of(owner * shard, shard), shard)
+
+    def pair_views(k):
+        return (
+            lambda first, size: pair_ref.at[k, pl.ds(first, size)],
+            lambda owner, first, size: pair.at[k, pl.ds(owner * shard + first, size)],
+        )
+
+    views = [
+        (
+            lambda first, size: in_ref.at[:, pl.ds(first, size)],
+            lambda owner, first, size: in_full.at[:, pl.ds(owner * shard + first, size)],
+            0,
+            shard,
+        ),
+        (
+            lambda first, size: out_ref.at[pl.ds(first, size)],
+            lambda owner, first, size: out_full.at[pl.ds(first, size), columns_of(owner)],
+            0,
+            channels,
+        ),
     ]
-
-    def own(slot):
-        return pltpu.make_async_copy(
-            normed_ref.at[slot], rows.at[slot, pl.ds(p.m * share, share)], load.at[2 + slot]
+    for i in range(2):
+        views.append(
+            (
+                lambda first, size: down_ref.at[pl.ds(first, size)],
+                lambda owner, first, size: down.at[pl.ds(first, size), columns_of(owner)],
+                i * (units // 2),
+                units // 2,
+            )
         )
-
-    order = far_first(p)[::-1]
-    tiles = [(slot, chip) for slot in range(slots) for chip in order]
+    for i in range(4):
+        views.append((*pair_views(i // 2), (i % 2) * (shard // 2), shard // 2))
+    pieces = [Relay(p, *view, (w_send.at[i], w_recv.at[i], w_local.at[i])) for i, view in enumerate(views)]
+    early, late = pieces[:2], pieces[2:]
+    pending = [late[0].start]
+    for i in range(len(late)):
+
+        def step(i=i):
+            late[i].forward()
+            if i + 1 < len(late):
+                late[i + 1].start()
+
+        pending.append(step)
+
+    def push():
+        if pending:
+            pending.pop(0)()
+
+    def own(slot, which, source):
+        span = pl.ds(p.m * share, share)
+        return pltpu.make_async_copy(source.at[slot], which.at[slot, span], keep.at[slot + (slots if which is top_rows else 0)])
+
+    for slot in range(slots):
+        own(slot, rows, normed_ref).start()
+        own(slot, top_rows, top_ref).start()
+
+    def saved(index, src, dst):
+        return pltpu.make_async_copy(src, dst, keep.at[2 * slots + index])
+
+    rows_saved = [saved(slot, rows.at[slot], normed_rows.at[slot]) for slot in range(slots)]
+    gates_saved = [saved(slots + slot, gates, gates_out.at[slot, 1]) for slot in range(slots)]
+    middle_saved = [saved(2 * slots + slot, total.at[slot], middle_out.at[slot]) for slot in range(slots)]
+    grad_saved = [saved(3 * slots + slot, total.at[slot], grad_out.at[slot]) for slot in range(slots)]
+    in_saved = saved(4 * slots, in_full, in_rows)
+    out_saved = saved(4 * slots + 1, out_full, out_rows)
+    product_saved = saved(4 * slots + 2, product, product_out)
+    mixed_saved = saved(4 * slots + 3, mixed, mixed_out)
+    down_saved = saved(4 * slots + 4, down, down_grad)
+    act_load = saved(4 * slots + 5, act_rows, acts.at[0])
+
+    def halo(slot):
+        return remote(
+            product.at[slot, pl.ds(block, 8)],
+            product.at[slot, pl.ds(0, 8)],
+            halo_send.at[slot],
+            halo_recv.at[slot],
+            p.peer(1),
+        )
+
+    has_later, has_earlier = p.s < seqs - 1, p.s > 0
+    for slot in range(slots):
+
+        @pl.when(jnp.logical_not(has_earlier))
+        def _(slot=slot):
+            product[slot, pl.ds(0, 8)] = jnp.zeros((8, channels), F32)
+
+    def ends_saved(slot, i):
+        span = pl.ds(i * tile, tile)
+        return [
+            pltpu.make_async_copy(ends.at[j], gates_out.at[slot, 2 * j, span], ends_sem.at[j]) for j in range(2)
+        ]
+
+    def project(slot):
+        @pl.loop(0, chips)
+        def _(i):
+            span = pl.ds(i * tile, tile)
+            source = rows[slot, span]
+            b_gate = nn(source, in_full[0])
+            x_value = nn(source, in_full[2])
+            gates[span] = nn(source, in_full[1])
+
+            @pl.when(i > 0)
+            def _():
+                for thing in ends_saved(slot, i - 1):
+                    thing.wait()
+
+            ends[0] = b_gate
+            ends[1] = x_value
+            for thing in ends_saved(slot, i):
+                thing.start()
+            product[slot, pl.ds(8 + i * tile, tile)] = b_gate * x_value
+
+        for thing in ends_saved(slot, chips - 1):
+            thing.wait()
+        pl.when(has_later)(lambda: halo(slot).start())
+
+    def convolve(slot):
+        pl.when(has_earlier)(lambda: halo(slot).wait_recv())
+        for i in range(chips):
+            conv = 0.0
+            for offset in range(taps_ref.shape[0]):
+                conv = conv + taps_ref[offset : offset + 1] * product[slot, pl.ds(8 + i * tile - offset, tile)]
+            mixed[slot, pl.ds(i * tile, tile)] = (gates[pl.ds(i * tile, tile)] * conv).astype(BF)
+
+    def project_out(slot):
+        for chip in far_first(p):
+            span = pl.ds(chip * tile, tile)
+            part[slot, span] = nn(mixed[slot, span], out_full[...]).astype(BF)
+            mix_sums[slot].give(chip)
+
+    def middle(slot):
+        def store(first, size, value):
+            span = pl.ds(first, size)
+            value = value + source_ref[slot, span].astype(F32)
+            total[slot, span] = value
+            scale = lax.rsqrt(jnp.mean(value * value, axis=-1, keepdims=True) + EPS)
+            rows[slot, pl.ds(p.m * share + first, size)] = (value * scale * gain_ref[...]).astype(BF)
+
+        mix_sums[slot].finish(store)
+        middle_saved[slot].start()
+        mix_sums[slot].drain()
+
+    def finish_grad(slot):
+        middle_saved[slot].wait()
+
+        def store(first, size, value):
+            total[slot, pl.ds(first, size)] = value
+
+        grad_sums[slot].finish(store)
+        grad_saved[slot].start()
+
+    order = far_first(p)
+    tiles = [(0, chip) for chip in order] + [(slot, chip) for slot in range(1, slots) for chip in order[::-1]]
 
     def fetch(index):
         slot, chip = tiles[index]
-        return pltpu.make_async_copy(
-            top_rows.at[slot, pl.ds(chip * tile, tile)], top_tile.at[index % 2], tile_sem.at[index % 2]
-        )
-
-    def put(index):
+        return pltpu.make_async_copy(top_rows.at[slot, pl.ds(chip * tile, tile)], top_tile, tile_sem)
+
+    def puts(index):
         slot, chip = tiles[index]
-        return pltpu.make_async_copy(
-            stage.at[index % 2], mlp_part.at[slot, pl.ds(chip * tile, tile)], stage_sem.at[index % 2]
-        )
+        span = pl.ds(chip * tile, tile)
+        return [
+            pltpu.make_async_copy(stage, mlp_part.at[slot, span], out_sem.at[0]),
+            pltpu.make_async_copy(act_stage, act_rows.at[slot, span], out_sem.at[1]),
+        ]
 
     def work(index):
         slot, chip = tiles[index]
-        buf = index % 2
         span = pl.ds(chip * tile, tile)
+        if index == 0 or slot > 0:
+            fetch(index).start()
         fetch(index).wait()
-        if index + 1 < len(tiles):
-            fetch(index + 1).start()
-        if index >= 2:
-            put(index - 2).wait()
+        if index:
+            for thing in puts(index - 1):
+                thing.wait()
 
         @pl.loop(0, units // unit_block)
         def _(i):
@@ -602,149 +578,240 @@
             source = rows[slot, span]
             gate = nn(source, pair[0, :, cut])
             up = nn(source, pair[1, :, cut])
-            act_grad = nt(top_tile[buf], down[cut])
+            act_grad = nt(top_tile[...], down[cut])
             sigma = jax.nn.sigmoid(gate)
             silu = gate * sigma
-            acts[0, slot, span, cut] = (silu * up).astype(BF)
-            acts[1, slot, span, cut] = (act_grad * up * sigma * (1.0 + gate * (1.0 - sigma))).astype(BF)
-            acts[2, slot, span, cut] = (act_grad * silu).astype(BF)
+            act_stage[:, cut] = (silu * up).astype(BF)
+            acts[0, slot, span, cut] = (act_grad * up * sigma * (1.0 + gate * (1.0 - sigma))).astype(BF)
+            acts[1, slot, span, cut] = (act_grad * silu).astype(BF)
+
+        if index + 1 < len(tiles) and tiles[index + 1][0] == 0:
+            fetch(index + 1).start()
 
         @pl.loop(0, width // wide_block)
         def _(i):
             cut = pl.ds(pl.multiple_of(i * wide_block, wide_block), wide_block)
-            value = nt(acts[1, slot, span], pair[0, cut]) + nt(acts[2, slot, span], pair[1, cut])
+            value = nt(acts[0, slot, span], pair[0, cut]) + nt(acts[1, slot, span], pair[1, cut])
             part[slot, span, cut] = value.astype(BF)
-            stage[buf, :, cut] = nn(acts[0, slot, span], down[:, cut]).astype(BF)
-
-        sums[slot].give(chip)
-        put(index).start()
-
-    def finish(slot):
-        def store(first, size, value):
-            total[slot, pl.ds(first, size)] = value
-
-        sums[slot].finish(store)
+            stage[:, cut] = nn(act_stage[...], down[:, cut]).astype(BF)
+
+        grad_sums[slot].give(chip)
+        for thing in puts(index):
+            thing.start()
+
+    pair_steps = 2 * (width // wide_block)
+
+    def pair_saved(index):
+        k, first = divmod(index, width // wide_block)
+        cut = pl.ds(first * wide_block, wide_block)
+        return pltpu.make_async_copy(pair.at[k, cut], pair_grad.at[k, cut], pair_sem.at[index])
 
     def pair_step(index):
         k, first = divmod(index, width // wide_block)
         cut = pl.ds(first * wide_block, wide_block)
         value = 0.0
         for slot in range(slots):
-            value = value + tn(rows[slot, :, cut], acts[1 + k, slot])
+            value = value + tn(rows[slot, :, cut], acts[k, slot])
         pair[k, cut] = value.astype(BF)
-        pltpu.make_async_copy(pair.at[k, cut], pair_grad.at[k, cut], keep.at[index]).start()
-
-    pair_steps = 2 * (width // wide_block)
+        pair_saved(index).start()
+        if first == width // wide_block - 1 and k == 0:
+            act_load.start()
 
     def fetch_columns(index):
-        return pltpu.make_async_copy(
-            top_rows.at[:, :, pl.ds(index * columns, columns)], top_cols.at[index % 2], cols_sem.at[index % 2]
-        )
+        cut = pl.ds(index * channels, channels)
+        return [
+            pltpu.make_async_copy(
+                top_rows.at[slot, :, cut], in_full.at[index % 2, pl.ds(slot * block, block)], cols_sem.at[index % 2, slot]
+            )
+            for slot in range(slots)
+        ]
 
     def down_step(index):
-        fetch_columns(index).wait()
+        if index == 0:
+            act_load.wait()
+        for thing in fetch_columns(index):
+            thing.wait()
         for first in range(0, units, unit_block):
             cut = pl.ds(first, unit_block)
             value = 0.0
             for slot in range(slots):
-                value = value + tn(acts[0, slot, :, cut], top_cols[index % 2, slot])
-            down[cut, pl.ds(index * columns, columns)] = value.astype(BF)
-        if index + 2 < width // columns:
-            fetch_columns(index + 2).start()
-
-    for slot in range(slots):
-        own(slot).start()
-    fetch(0).start()
-    gathers[0].start()
-    own(0).wait()
-    own(1).wait()
-    for thing in loads:
-        thing.wait()
+                value = value + tn(acts[0, slot, :, cut], in_full[index % 2, pl.ds(slot * block, block)])
+            down[cut, pl.ds(index * channels, channels)] = value.astype(BF)
+        if index + 2 < width // channels:
+            for thing in fetch_columns(index + 2):
+                thing.start()
+
+    firsts[0].start()
+    for piece in early:
+        piece.start()
+    steps = firsts[0].rounds()
+    for step in steps[:-1]:
+        step()
+    for piece in early:
+        piece.forward()
+    firsts[1].start()
+    steps[-1]()
+    own(0, rows, normed_ref).wait()
+    firsts[0].arrived()
+    rows_saved[0].start()
+    for piece in early:
+        piece.arrived()
+    in_saved.start()
+    out_saved.start()
+    project(0)
+    gates_saved[0].start()
+    push()
+    steps = firsts[1].rounds()
+    steps[0]()
+    push()
+    rows_saved[0].wait()
+    firsts[0].drain()
+    convolve(0)
+    project_out(0)
+    weave(mix_sums[0].rounds(), steps[1:], [push] * chips)
+    own(1, rows, normed_ref).wait()
+    firsts[1].arrived()
+    rows_saved[1].start()
+    gates_saved[0].wait()
+    project(1)
+    gates_saved[1].start()
+    push()
+    middle(0)
+    seconds[0].start()
+    rows_saved[1].wait()
+    firsts[1].drain()
+    convolve(1)
+    project_out(1)
+    steps = seconds[0].rounds()
+    weave(mix_sums[1].rounds(), steps[:-1] + [tops[0].start, steps[-1]], [push] * chips)
+    steps = tops[0].rounds()
+    steps[0]()
+    push()
+    middle(1)
+    product_saved.start()
+    mixed_saved.start()
+    for step in steps[1:-1]:
+        step()
+        push()
+    seconds[1].start()
+    steps[-1]()
+    while pending:
+        push()
+    own(0, top_rows, top_ref).wait()
+    tops[0].arrived()
+    seconds[0].arrived()
+    for piece in late:
+        piece.arrived()
+    hops, steps, more = grad_sums[0].rounds(), seconds[1].rounds(), tops[1].rounds()
+    for index in range(chips):
+        work(index)
+        if index < len(steps):
+            steps[index]()
+        if index == len(steps) - 2:
+            tops[1].start()
+        if index < len(hops):
+            hops[index]()
+    own(1, top_rows, top_ref).wait()
     for index in range(chips):
         if index:
-            gathers[0].round(index)
-        if index == chips - 2:
-            gathers[1].start()
-        gathers[0].other_core(order[index])
-        work(index)
-    hops = sums[0].rounds()
-    for index in range(chips):
-        if index < len(hops):
-            hops[index]()
-        if index:
-            gathers[1].round(index)
-        gathers[1].other_core(order[index])
+            more[index - 1]()
+        seconds[1].other_core(tiles[chips + index][1])
+        tops[1].other_core(tiles[chips + index][1])
         work(chips + index)
-    hops = sums[1].rounds()
+    in_saved.wait()
+    for piece in pieces:
+        piece.drain()
+    for index in range(2):
+        for thing in fetch_columns(index):
+            thing.start()
+    hops = grad_sums[1].rounds()
     hops[0]()
-    finish(0)
-    fetch_columns(0).start()
-    fetch_columns(1).start()
+    finish_grad(0)
+    for index in range(len(tiles) - 1, len(tiles)):
+        for thing in puts(index):
+            thing.wait()
     work_steps = [functools.partial(pair_step, index) for index in range(pair_steps)]
-    work_steps += [functools.partial(down_step, index) for index in range(width // columns)]
+    work_steps += [functools.partial(down_step, index) for index in range(width // channels)]
     spaced = len(work_steps) // len(hops)
     for index, step in enumerate(work_steps):
         step()
         if (index + 1) % spaced == 0 and (index + 1) // spaced < len(hops):
             hops[(index + 1) // spaced]()
-    finish(1)
-    last = [
-        pltpu.make_async_copy(down, down_grad, keep.at[pair_steps]),
-        pltpu.make_async_copy(total, grad_out, keep.at[pair_steps + 1]),
-    ]
-    for thing in last:
-        thing.start()
+    down_saved.start()
+    finish_grad(1)
     for index in range(pair_steps):
-        k, first = divmod(index, width // wide_block)
-        cut = pl.ds(first * wide_block, wide_block)
-        pltpu.make_async_copy(pair.at[k, cut], pair_grad.at[k, cut], keep.at[index]).wait()
-    for index in range(len(tiles) - 2, len(tiles)):
-        put(index).wait()
-    for thing in last:
+        pair_saved(index).wait()
+    for thing in [gates_saved[1], out_saved, product_saved, mixed_saved, down_saved, *grad_saved]:
         thing.wait()
-    for thing in gathers + sums:
+    for thing in tops + seconds + grad_sums:
         thing.drain()
-
-
-def mlp(seqs, models, normed, top_rows, pair_full, down_full):
+    for slot in range(slots):
+        pl.when(has_later)(lambda slot=slot: halo(slot).wait_send())
+
+
+def forward(seqs, models, normed, source, gain, top, taps, mixer_in, mixer_out, gate_up, mlp_down):
     slots, share, width = normed.shape
     chips = models // 2
     block = share * models
-    units = down_full.shape[0]
+    channels = mixer_in.shape[2]
+    units = gate_up.shape[2]
+    tile = block // chips
     hbm = pl.BlockSpec(memory_space=pltpu.HBM)
+    vmem = pl.BlockSpec(memory_space=pltpu.VMEM)
     shape = jax.ShapeDtypeStruct
     return pl.pallas_call(
-        functools.partial(mlp_kernel, seqs, models),
+        functools.partial(forward_kernel, seqs, models),
         out_shape=[
+            shape((slots, block, width), BF),
+            shape((slots, block, width), BF),
+            shape((3, width, channels), BF),
+            shape((channels, width), BF),
+            shape((slots, 3, block, channels), F32),
+            shape((slots, block + 8, channels), F32),
+            shape((slots, block, channels), BF),
+            shape((slots, share, width), F32),
             shape((slots, share, width), F32),
             shape((slots, block, width), BF),
+            shape((slots, block, units), BF),
             shape((2, width, units), BF),
             shape((units, width), BF),
         ],
-        in_specs=[hbm] * 4,
-        out_specs=[hbm] * 4,
+        in_specs=[hbm, vmem, vmem, hbm, vmem] + [hbm] * 4,
+        out_specs=[hbm] * 13,
         scratch_shapes=[
+            pltpu.VMEM((3, width, channels), BF),
+            pltpu.VMEM((channels, width), BF),
+            pltpu.VMEM((slots, block, width), BF),
+            pltpu.VMEM((block, channels), F32),
+            pltpu.VMEM((2, tile, channels), F32),
+            pltpu.VMEM((slots, block + 8, channels), F32),
+            pltpu.VMEM((slots, block, channels), BF),
             pltpu.VMEM((2, width, units), BF),
             pltpu.VMEM((units, width), BF),
-            pltpu.VMEM((slots, block, width), BF),
-            pltpu.VMEM((2, block // chips, width), BF),
-            pltpu.VMEM((2, slots, block, 256), BF),
-            pltpu.VMEM((3, slots, block, units), BF),
-            pltpu.VMEM((2, block // chips, width), BF),
+            pltpu.VMEM((tile, width), BF),
+            pltpu.VMEM((2, slots, block, units), BF),
+            pltpu.VMEM((tile, units), BF),
+            pltpu.VMEM((tile, width), BF),
             pltpu.VMEM((slots, block, width), BF),
             pltpu.VMEM((slots, chips, share, width), BF),
             pltpu.VMEM((slots, chips + 1, share, width), BF),
             pltpu.VMEM((slots, share, width), F32),
-            pltpu.SemaphoreType.DMA((2 + slots,)),
+            pltpu.SemaphoreType.DMA((8, max(4, seqs - 1))),
+            pltpu.SemaphoreType.DMA((8, max(4, seqs - 1))),
+            pltpu.SemaphoreType.DMA((8,)),
+            pltpu.SemaphoreType.DMA((slots,)),
+            pltpu.SemaphoreType.DMA((slots,)),
+            pltpu.SemaphoreType.DMA((6 * slots + 6,)),
+            pltpu.SemaphoreType.DMA,
             pltpu.SemaphoreType.DMA((2,)),
+            pltpu.SemaphoreType.DMA((2, slots)),
+            pltpu.SemaphoreType.DMA((2 * (width // 512),)),
             pltpu.SemaphoreType.DMA((2,)),
-            pltpu.SemaphoreType.DMA((2,)),
-            pltpu.SemaphoreType.DMA((2 * (width // 512) + 2,)),
-            *gather_sems(slots, chips),
-            *scatter_sems(slots, chips),
+            *gather_sems(3 * slots, chips),
+            *scatter_sems(2 * slots, chips),
         ],
-        compiler_params=pltpu.CompilerParams(collective_id=2, has_side_effects=True, vmem_limit_bytes=VMEM_LIMIT),
-    )(normed, top_rows, pair_full, down_full)
+        compiler_params=pltpu.CompilerParams(collective_id=1, has_side_effects=True, vmem_limit_bytes=VMEM_LIMIT),
+    )(normed, source, gain, top, taps, mixer_in, mixer_out, gate_up, mlp_down)
 
 
 class Spread:
@@ -1201,19 +1268,24 @@
     normed, scale_mix = normalize(source, gain_mix)
     (
         normed_rows,
-        top_rows,
+        _,
         in_full,
         out_full,
-        pair_full,
-        down_full,
         gates,
         product,
         mixed,
-        mix_share,
-    ) = mixer_forward(
+        middle,
+        middle_grad,
+        mlp_part,
+        _,
+        pair_total,
+        down_total,
+    ) = forward(
         seqs,
         models,
         normed.astype(BF),
+        hidden,
+        gain_mlp[None],
         top_grad.astype(BF),
         local_taps,
         mixer_in,
@@ -1221,11 +1293,7 @@
         gate_up,
         mlp_down,
     )
-    middle = source + mix_share
-    normed_two, scale_mlp = normalize(middle, gain_mlp)
-    middle_grad, mlp_part, pair_total, down_total = mlp(
-        seqs, models, normed_two.astype(BF), top_rows, pair_full, down_full
-    )
+    scale_mlp = lax.rsqrt(jnp.mean(middle * middle, axis=-1, keepdims=True) + EPS)
     middle_grad, gain_mlp_grad = norm_back(middle_grad, middle, scale_mlp, gain_mlp)
     middle_grad = middle_grad + top_grad
     mlp_share, source_grad, taps_part, in_got, out_got, pair_got, down_got = mixer_backward(

time: 601 us -> 635 us (1.057)
  Pallas kernels: 547 us -> 585 us
    pallas_call x2 -> x1, Pallas kernels: 344 us -> 383 us  [forward(): pl.pallas_call(functools.partial(forward_kernel, seqs, models), out_shape...]
where the time goes in v5:
time: 635 us; the launch traced here: 626 us
  Pallas kernels  585 us (92%)
  other arithmetic  32.8 us (5%)
  local copies, waits for them, and re-layouts  6.68 us (1%)
    pallas_call x1, Pallas kernels, forward(): pl.pallas_call(functools.partial(forward_kernel, seqs, models), out_shape...  383 us
    pallas_call x1, Pallas kernels, mixer_backward(): pl.pallas_call(functools.partial(mixer_backward_kernel, seqs, models), ou...  188 us
    pallas_call x1, Pallas kernels, small_sum(): pl.pallas_call(functools.partial(small_sum_kernel, seqs, models), out_sha...  13.8 us

profile of v5, /device:TPU:0, one launch (start us, length us, event | category | flops | bytes accessed | tf_op | source)
XLA Modules:
  0.0 625.7 jit_solution(12493155972655707799)
XLA Ops:
  0.6 0.0 copy-start
  0.7 0.7 copy-done
  1.4 0.6 constant_dynamic-slice_fusion.taps_ref
  2.0 0.7 compare_convert_fusion
  2.7 1.5 fusion.10
  4.2 3.3 fusion.4
  7.5 0.0 copy-start.11
  7.5 383.3 %shard_map.169 = (bf16[2,1024,2048]{2,1,0:T(8,128)(2,1)}, bf16[2,1024,2048]{2,1,0:T(8,128)(2,1)}, bf16[3,2048,256]{2,1,0:T(8,128)(2,1)}, bf16[256,2048]{1,0:T(8,...) custom-call(bf16[2,128,2048]{2,1,0:T(8,128)(2,1)} %get-tuple-element, ...), custom_call_target="tpu_custom_call" | custom-call | tf_op jit(solution)/shard_map/pallas_call | solution.py:762
  390.8 0.0 copy-start.2
  390.8 2.0 multiply_reduce_fusion.2
  392.8 0.0 copy-done.11
  392.8 0.2 copy-done.2
  393.0 0.0 copy-start.5
  393.0 0.0 copy-start.6
  393.0 2.4 multiply_reduce_fusion
  395.4 0.0 copy-done.5
  395.4 0.1 copy-done.6
  395.5 1.7 fusion.12.low_ref
  397.2 188.1 %shard_map.170 = (f32[2,128,2048]{2,1,0:T(8,128)}, f32[2,128,2048]{2,1,0:T(8,128)}, f32[8,256]{1,0:T(8,128)}, bf16[4,3,512,256]{3,2,1,0:T(8,128)(2,1)}, bf16[4,2...) custom-call(bf16[2,128,2048]{2,1,0:T(8,128)(2,1)} %fusion.12.low_ref, ...), custom_call_target="tpu_custom_call" | custom-call | tf_op jit(solution)/shard_map/pallas_call | solution.py:1125
  585.3 0.0 copy-start.13
  585.3 0.0 copy-start.4
  585.3 0.0 copy-start.12
  585.3 8.0 %convert_reduce_fusion = f32[2,512,1024]{2,1,0:T(8,128)} fusion(bf16[4,2,512,1024]{3,2,1,0:T(8,128)(2,1)} %get-tuple-element.67), kind=kLoop, calls=%fused_computation | loop fusion | flops 7340032 | bytes 12582912 | tf_op jit(solution)/shard_map/reduce_sum | solution.py:1322
  593.3 0.0 copy-start.3
  593.3 0.0 copy-done.13
  593.3 0.4 dynamic_update_slice.3
  593.8 0.0 copy-done.4
  593.8 0.0 copy-done.12
  593.8 2.4 fusion.9
  596.2 0.2 scatter.6
  596.4 0.2 scatter.9.value_ref
  596.6 0.0 copy-start.10
  596.6 0.6 copy-done.10
  597.2 13.8 %shard_map.171 = f32[8,2048]{1,0:T(8,128)} custom-call(f32[8,2048]{1,0:T(8,128)} %copy-done.10), custom_call_target="tpu_custom_call" | custom-call | tf_op jit(solution)/shard_map/pallas_call | solution.py:1214
  611.0 1.5 slice.45
  612.5 1.5 fusion.13
  614.0 0.0 copy-done.3
  614.0 0.0 copy-start.7
  614.0 6.4 %fusion.8 = (f32[2,128,2048]{2,1,0:T(8,128)}, bf16[2,128,2048]{2,1,0:T(8,128)(2,1)}) fusion(bf16[2,128,2048]{2,1,0:T(8,128)(2,1)S(1)} %copy-done.4, f32[2,128,2048]{2,1,0:T(8,128)} %get-tuple-element.63, f32[2,128]{1,0:T(2,128)S(1)} %broadcast_multiply_fusion, f32[2048]{0:T(1024)S(1)} %copy-done.12, f32[2,128]{1,0:T(2,128)S(1)} %add_rsqrt_fusion.1, ...), kind=kLoop, calls=%fused_computation.13 | loop fusion | flops 9437184 | bytes 13652992 | tf_op jit(solution)/shard_map/add | solution.py:1326
  620.4 0.0 copy-done.7
  620.4 0.0 copy-start.8
  620.4 2.0 convert_reduce_fusion.1
  622.4 0.0 copy-start.1
  622.4 0.5 copy-done.8
  622.9 0.0 copy-start.9
  622.9 1.6 convert_reduce_fusion.2
  624.5 0.0 copy-done.9
  624.5 1.0 convert_reduce_fusion.3
  625.4 0.0 copy-done.1
  (7 shorter events, 0.0 us)
Async XLA Ops:
  0.6 0.8 copy-start
  7.5 385.3 %copy-start.11 = (f32[2048]{0:T(1024)S(1)}, f32[2048]{0:T(1024)}, u32[]{:S(2)}) copy-start(f32[2048]{0:T(1024)} %param.18) | copy-start | bytes 24580
  390.8 2.2 copy-start.2
  393.0 2.4 copy-start.5
  393.0 2.5 copy-start.6
  585.3 8.0 %copy-start.13 = (f32[8,256]{1,0:T(8,128)S(1)}, f32[8,256]{1,0:T(8,128)}, u32[]{:S(2)}) copy-start(f32[8,256]{1,0:T(8,128)} %get-tuple-element.64) | copy-start | bytes 24580
  585.3 8.5 %copy-start.4 = (bf16[2,128,2048]{2,1,0:T(8,128)(2,1)S(1)}, bf16[2,128,2048]{2,1,0:T(8,128)(2,1)}, u32[]{:S(2)}) copy-start(bf16[2,128,2048]{2,1,0:T(8,128)(2,1)} %source_ref.1) | copy-start | bytes 3145732
  585.3 8.5 %copy-start.12 = (f32[2048]{0:T(1024)S(1)}, f32[2048]{0:T(1024)}, u32[]{:S(2)}) copy-start(f32[2048]{0:T(1024)} %param.17) | copy-start | bytes 24580
  593.3 20.7 %copy-start.3 = (f32[2,128,2048]{2,1,0:T(8,128)S(1)}, f32[2,128,2048]{2,1,0:T(8,128)}, u32[]{:S(2)}) copy-start(f32[2,128,2048]{2,1,0:T(8,128)} %get-tuple-element.51) | copy-start | bytes 6291460
  596.6 0.6 copy-start.10
  614.0 6.4 %copy-start.7 = (bf16[4,1024,512]{2,1,0:T(8,128)(2,1)S(1)}, bf16[4,1024,512]{2,1,0:T(8,128)(2,1)}, u32[]{:S(2)}) copy-start(bf16[4,1024,512]{2,1,0:T(8,128)(2,1)} %get-tuple-element.68) | copy-start | bytes 12582916
  620.4 2.5 copy-start.8
  622.4 3.1 copy-start.1
  622.9 1.6 copy-start.9

commit v6 on v5

--- a/solution.py
+++ b/solution.py
@@ -430,19 +430,12 @@
         views.append((*pair_views(i // 2), (i % 2) * (shard // 2), shard // 2))
     pieces = [Relay(p, *view, (w_send.at[i], w_recv.at[i], w_local.at[i])) for i, view in enumerate(views)]
     early, late = pieces[:2], pieces[2:]
-    pending = [late[0].start]
-    for i in range(len(late)):
-
-        def step(i=i):
-            late[i].forward()
-            if i + 1 < len(late):
-                late[i + 1].start()
-
-        pending.append(step)
+    moves = [[("start", 0), ("start", 1)], [("forward", 0), ("start", 2)], [("forward", 1), ("start", 3)]]
+    moves += [[("forward", 2)], [("forward", 3)], [("start", 4), ("start", 5)], [("forward", 4)], [("forward", 5)]]
 
     def push():
-        if pending:
-            pending.pop(0)()
+        for name, index in moves.pop(0):
+            getattr(late[index], name)()
 
     def own(slot, which, source):
         span = pl.ds(p.m * share, share)
@@ -668,7 +661,7 @@
     firsts[0].drain()
     convolve(0)
     project_out(0)
-    weave(mix_sums[0].rounds(), steps[1:], [push] * chips)
+    weave(mix_sums[0].rounds(), steps[1:-1] + [tops[0].start, steps[-1]], [push] * 3)
     own(1, rows, normed_ref).wait()
     firsts[1].arrived()
     rows_saved[1].start()
@@ -682,41 +675,34 @@
     firsts[1].drain()
     convolve(1)
     project_out(1)
-    steps = seconds[0].rounds()
-    weave(mix_sums[1].rounds(), steps[:-1] + [tops[0].start, steps[-1]], [push] * chips)
-    steps = tops[0].rounds()
-    steps[0]()
-    push()
+    hops, steps, more = mix_sums[1].rounds(), tops[0].rounds(), seconds[0].rounds()
+    weave(steps, hops, [push] * 2)
+    weave(more[:-1])
+    tops[1].start()
+    more[-1]()
     middle(1)
+    seconds[1].start()
     product_saved.start()
     mixed_saved.start()
-    for step in steps[1:-1]:
-        step()
-        push()
-    seconds[1].start()
-    steps[-1]()
-    while pending:
-        push()
     own(0, top_rows, top_ref).wait()
     tops[0].arrived()
     seconds[0].arrived()
     for piece in late:
         piece.arrived()
-    hops, steps, more = grad_sums[0].rounds(), seconds[1].rounds(), tops[1].rounds()
+    own(1, top_rows, top_ref).wait()
+    hops, steps, more = grad_sums[0].rounds(), tops[1].rounds(), seconds[1].rounds()
     for index in range(chips):
         work(index)
         if index < len(steps):
             steps[index]()
-        if index == len(steps) - 2:
-            tops[1].start()
-        if index < len(hops):
-            hops[index]()
-    own(1, top_rows, top_ref).wait()
+        if 0 < index:
+            hops[index - 1]()
     for index in range(chips):
         if index:
             more[index - 1]()
+        else:
+            tops[1].arrived()
         seconds[1].other_core(tiles[chips + index][1])
-        tops[1].other_core(tiles[chips + index][1])
         work(chips + index)
     in_saved.wait()
     for piece in pieces:
@@ -814,37 +800,104 @@
     )(normed, source, gain, top, taps, mixer_in, mixer_out, gate_up, mlp_down)
 
 
-class Spread:
-    def __init__(self, place, partial, got, sems):
-        self.p, self.partial, self.got = place, partial, got
+class Exchange:
+    def __init__(self, place, partial, got, first, size, sems, held, came):
+        self.p, self.partial, self.got, self.first, self.size = place, partial, got, first, size
         self.send, self.recv, self.local = sems
-
-    def block(self, owner):
-        size = self.partial.shape[1] // self.p.seqs
-        return self.partial.at[:, pl.ds(pl.multiple_of(owner * size, size), size)]
-
-    def copy(self, step):
+        self.held, self.came = held, came
+        s = place.s
+        self.square = place.seqs == 4
+        if self.square:
+            self.near = (s + 1 - 2 * lax.rem(s, 2), lax.rem(s + 2, 4))
+            self.across = 3 - s
+
+    def half(self, index):
+        return self.first + index * (self.size // 2), self.size // 2
+
+    def to(self, index):
+        return {"seq": self.near[index]}
+
+    def relayed(self, index):
+        return remote(
+            self.partial(self.across, *self.half(index)),
+            self.came.at[index],
+            self.send.at[index],
+            self.recv.at[index],
+            self.to(index),
+        )
+
+    def plain(self, index):
+        span = self.half(index)
+        return remote(
+            self.partial(self.near[index], *span),
+            self.got(1 + index, *span),
+            self.send.at[2 + index],
+            self.recv.at[2 + index],
+            self.to(index),
+        )
+
+    def added(self, index):
+        return remote(
+            self.held.at[1 - index],
+            self.got(1 + index, *self.half(1 - index)),
+            self.send.at[4 + index],
+            self.recv.at[4 + index],
+            self.to(index),
+        )
+
+    def load(self, index):
+        return pltpu.make_async_copy(
+            self.partial(self.near[index], *self.half(1 - index)), self.held.at[1 - index], self.local.at[1 + index]
+        )
+
+    def straight(self, step):
         p = self.p
         return remote(
-            self.block(lax.rem(p.s + step, p.seqs)),
-            self.got(step),
+            self.partial(lax.rem(p.s + step, p.seqs), self.first, self.size),
+            self.got(step, self.first, self.size),
             self.send.at[step - 1],
             self.recv.at[step - 1],
             p.peer(step),
         )
 
-    def local_copy(self):
-        return pltpu.make_async_copy(self.block(self.p.s), self.got(0), self.local)
+    def own(self):
+        return pltpu.make_async_copy(
+            self.partial(self.p.s, self.first, self.size), self.got(0, self.first, self.size), self.local.at[0]
+        )
+
+    def copies(self):
+        if self.square:
+            return [self.relayed(0), self.relayed(1), self.plain(0), self.plain(1)]
+        return [self.straight(step) for step in range(1, self.p.seqs)]
 
     def start(self):
-        for step in range(1, self.p.seqs):
-            self.copy(step).start()
-        self.local_copy().start()
+        for thing in self.copies():
+            thing.start()
+        if self.square:
+            for index in range(2):
+                self.load(index).start()
+        self.own().start()
+
+    def forward(self):
+        if self.square:
+            for index in range(2):
+                self.load(index).wait()
+                self.relayed(1 - index).wait_recv()
+                total = self.held[1 - index].astype(F32) + self.came[1 - index].astype(F32)
+                self.held[1 - index] = total.astype(BF)
+                self.added(index).start()
 
     def finish(self):
-        self.local_copy().wait()
-        for step in range(1, self.p.seqs):
-            self.copy(step).wait()
+        self.own().wait()
+        if self.square:
+            for thing in self.copies():
+                thing.wait_send()
+            for index in range(2):
+                self.plain(index).wait_recv()
+                self.added(index).wait()
+        else:
+            for thing in self.copies():
+                thing.wait()
 
 
 def mixer_backward_kernel(
@@ -882,6 +935,10 @@
     from_line,
     mlp_total,
     grad_total,
+    down_room,
+    pair_room,
+    in_room,
+    out_room,
     load,
     cols_sem,
     w_send,
@@ -929,18 +986,62 @@
 
     mlp_sums = [scatter(slot, slot) for slot in range(slots)]
     sums = [scatter(slot, slots + slot) for slot in range(slots)]
-    spreads = [
-        Spread(p, partial, got, (w_send.at[i], w_recv.at[i], w_local.at[i]))
-        for i, (partial, got) in enumerate(
+    shard = width // seqs
+    units = down_grad.shape[0]
+
+    def columns_of(owner):
+        return pl.ds(pl.multiple_of(owner * shard, shard), shard)
+
+    views = []
+    for i in range(2):
+        views.append(
             (
-                (pair_grad.at[pl.ds(0, 1)], lambda step: pair_got.at[step, pl.ds(0, 1)]),
-                (down_grad, lambda step: down_got.at[step]),
-                (in_full, lambda step: in_got.at[step]),
-                (out_full, lambda step: out_got.at[step]),
-                (pair_grad.at[pl.ds(1, 1)], lambda step: pair_got.at[step, pl.ds(1, 1)]),
+                lambda owner, first, size: down_grad.at[pl.ds(first, size), columns_of(owner)],
+                lambda index, first, size: down_got.at[index, pl.ds(first, size)],
+                i * (units // 2),
+                units // 2,
+                down_room.at[i],
             )
         )
+    for i in range(4):
+        views.append(
+            (
+                lambda owner, first, size, k=i // 2: pair_grad.at[k, pl.ds(owner * shard + first, size)],
+                lambda index, first, size, k=i // 2: pair_got.at[index, k, pl.ds(first, size)],
+                (i % 2) * (shard // 2),
+                shard // 2,
+                pair_room.at[i],
+            )
+        )
+    views.append(
+        (
+            lambda owner, first, size: in_full.at[:, pl.ds(owner * shard + first, size)],
+            lambda index, first, size: in_got.at[index, :, pl.ds(first, size)],
+            0,
+            shard,
+            in_room,
+        )
+    )
+    views.append(
+        (
+            lambda owner, first, size: out_full.at[pl.ds(first, size), columns_of(owner)],
+            lambda index, first, size: out_got.at[index, pl.ds(first, size)],
+            0,
+            channels,
+            out_room,
+        )
+    )
+    pieces = [
+        Exchange(p, *view[:4], (w_send.at[i], w_recv.at[i], w_local.at[i]), view[4].at[0], view[4].at[1])
+        for i, view in enumerate(views)
     ]
+    moves = [[("start", 0), ("start", 1)], [("forward", 0), ("start", 2)], [("forward", 1), ("start", 3)]]
+    moves += [[("forward", 2)], [("forward", 3)], [("start", 4), ("start", 5)], [("forward", 4)], [("forward", 5)]]
+
+    def push():
+        for name, index in moves.pop(0):
+            getattr(pieces[index], name)()
+
     has_later, has_earlier = p.s < seqs - 1, p.s > 0
     order = far_first(p)
 
@@ -1046,15 +1147,15 @@
                 value = value + tn(mixed[slot], rows[slot, :, cut])
             out_full[:, cut] = value.astype(BF)
 
-    spreads[1].start()
     gathers[0].start()
+    push()
     loads[0].wait()
     for chip in order:
         mlp_sums[0].give(chip)
     hops, next_rows = mlp_sums[0].rounds(), gathers[0].rounds()
-    weave(hops[:-1], next_rows[:-1])
+    weave(hops[:-1], next_rows[:-1], [push] * 2)
     gathers[1].start()
-    weave(hops[-1:], next_rows[-1:])
+    weave(hops[-1:], next_rows[-1:], [push])
     loads[1].wait()
     for chip in order:
         mlp_sums[1].give(chip)
@@ -1062,22 +1163,22 @@
     for thing in loads[2 + slots :]:
         thing.wait()
     gathers[0].arrived()
+    push()
     fetch_columns(0).start()
     fetch_columns(1).start()
     mlp_hops, next_rows, hops = mlp_sums[1].rounds(), gathers[1].rounds(), sums[0].rounds()
     first_pass(0)
-    spreads[0].start()
+    push()
     finish(mlp_sums, mlp_total, 0)
     give_free(0)
     weave(mlp_hops[:1], next_rows[:1])
     second_pass(0)
     take_free(0)
     third_pass(0)
-    weave(mlp_hops[1:], next_rows[1:], hops[:1])
+    weave(mlp_hops[1:], next_rows[1:], hops[:1], [push] * 2)
     loads[3].wait()
     gathers[1].arrived()
     first_pass(1)
-    spreads[4].start()
     finish(mlp_sums, mlp_total, 1)
     give_free(1)
     hops[1]()
@@ -1088,11 +1189,14 @@
     hops = sums[1].rounds()
     hops[0]()
     out_step()
-    spreads[3].start()
+    pieces[7].start()
     for index in range(steps_in):
         in_step(index)
-    spreads[2].start()
-    weave(hops[1:])
+    pieces[6].start()
+    hops[1]()
+    pieces[7].forward()
+    pieces[6].forward()
+    weave(hops[2:])
     finish(sums, grad_total, 0)
     finish(sums, grad_total, 1)
     last = [
@@ -1101,7 +1205,7 @@
     ]
     for thing in last:
         thing.start()
-    for thing in spreads:
+    for thing in pieces:
         thing.finish()
     for thing in last:
         thing.wait()
@@ -1119,6 +1223,8 @@
     block = share * models
     channels = out_full.shape[0]
     units = down_grad.shape[0]
+    shard = width // seqs
+    gots = 3 if seqs == 4 else seqs
     hbm = pl.BlockSpec(memory_space=pltpu.HBM)
     vmem = pl.BlockSpec(memory_space=pltpu.VMEM)
     shape = jax.ShapeDtypeStruct
@@ -1128,10 +1234,10 @@
             shape((slots, share, width), F32),
             shape((slots, share, width), F32),
             shape((8, channels), F32),
-            shape((seqs, 3, width // seqs, channels), BF),
-            shape((seqs, channels, width // seqs), BF),
-            shape((seqs, 2, width // seqs, units), BF),
-            shape((seqs, units, width // seqs), BF),
+            shape((gots, 3, shard, channels), BF),
+            shape((gots, channels, shard), BF),
+            shape((gots, 2, shard, units), BF),
+            shape((gots, units, shard), BF),
         ],
         in_specs=[hbm, hbm, vmem] + [hbm] * 8,
         out_specs=[hbm, hbm, vmem] + [hbm] * 4,
@@ -1150,11 +1256,15 @@
             pltpu.VMEM((slots, chips + 1, share, width), BF),
             pltpu.VMEM((slots, share, width), F32),
             pltpu.VMEM((slots, share, width), F32),
+            pltpu.VMEM((2, 2, 2, units // 4, shard), BF),
+            pltpu.VMEM((4, 2, 2, shard // 4, units), BF),
+            pltpu.VMEM((2, 2, 3, shard // 2, channels), BF),
+            pltpu.VMEM((2, 2, channels // 2, shard), BF),
             pltpu.SemaphoreType.DMA((2 * slots + 5,)),
             pltpu.SemaphoreType.DMA((2,)),
-            pltpu.SemaphoreType.DMA((5, seqs - 1)),
-            pltpu.SemaphoreType.DMA((5, seqs - 1)),
-            pltpu.SemaphoreType.DMA((5,)),
+            pltpu.SemaphoreType.DMA((8, max(6, seqs - 1))),
+            pltpu.SemaphoreType.DMA((8, max(6, seqs - 1))),
+            pltpu.SemaphoreType.DMA((8, 3)),
             pltpu.SemaphoreType.DMA((slots,)),
             pltpu.SemaphoreType.DMA((slots,)),
             pltpu.SemaphoreType.REGULAR((slots,)),

time: 635 us -> 570 us (0.90)
  Pallas kernels: 585 us -> 522 us
    pallas_call x1, Pallas kernels: 383 us -> 328 us  [forward(): pl.pallas_call(functools.partial(forward_kernel, seqs, models), out_shape...]
    pallas_call x1, Pallas kernels: 188 us -> 179 us  [mixer_backward(): pl.pallas_call(functools.partial(mixer_backward_kernel, seqs, models), ou...]
where the time goes in v6:
time: 570 us; the launch traced here: 561 us
  Pallas kernels  522 us (92%)
  other arithmetic  31.3 us (5%)
  local copies, waits for them, and re-layouts  6.35 us (1%)
    pallas_call x1, Pallas kernels, forward(): pl.pallas_call(functools.partial(forward_kernel, seqs, models), out_shape...  328 us
    pallas_call x1, Pallas kernels, mixer_backward(): pl.pallas_call(functools.partial(mixer_backward_kernel, seqs, models), ou...  179 us
    pallas_call x1, Pallas kernels, small_sum(): pl.pallas_call(functools.partial(small_sum_kernel, seqs, models), out_sha...  15.5 us

profile of v6, /device:TPU:0, one launch (start us, length us, event | category | flops | bytes accessed | tf_op | source)
XLA Modules:
  0.0 561.1 jit_solution(11920924391031724610)
XLA Ops:
  0.6 0.0 copy-start
  0.7 0.7 copy-done
  1.4 0.6 constant_dynamic-slice_fusion.taps_ref
  2.0 0.7 compare_convert_fusion
  2.7 1.5 fusion.10
  4.2 3.3 fusion.4
  7.5 0.0 copy-start.11
  7.5 327.9 %shard_map.169 = (bf16[2,1024,2048]{2,1,0:T(8,128)(2,1)}, bf16[2,1024,2048]{2,1,0:T(8,128)(2,1)}, bf16[3,2048,256]{2,1,0:T(8,128)(2,1)}, bf16[256,2048]{1,0:T(8,...) custom-call(bf16[2,128,2048]{2,1,0:T(8,128)(2,1)} %get-tuple-element, ...), custom_call_target="tpu_custom_call" | custom-call | tf_op jit(solution)/shard_map/pallas_call | solution.py:748
  335.4 0.0 copy-start.2
  335.4 2.0 multiply_reduce_fusion.2
  337.4 0.0 copy-done.11
  337.4 0.2 copy-done.2
  337.6 0.0 copy-start.5
  337.6 0.0 copy-start.6
  337.6 2.4 multiply_reduce_fusion
  340.0 0.0 copy-done.5
  340.0 0.1 copy-done.6
  340.1 1.7 fusion.12.low_ref
  341.8 179.0 %shard_map.170 = (f32[2,128,2048]{2,1,0:T(8,128)}, f32[2,128,2048]{2,1,0:T(8,128)}, f32[8,256]{1,0:T(8,128)}, bf16[3,3,512,256]{3,2,1,0:T(8,128)(2,1)}, bf16[3,2...) custom-call(bf16[2,128,2048]{2,1,0:T(8,128)(2,1)} %fusion.12.low_ref, ...), custom_call_target="tpu_custom_call" | custom-call | tf_op jit(solution)/shard_map/pallas_call | solution.py:1231
  520.8 0.0 copy-start.13
  520.8 0.0 copy-start.4
  520.8 0.0 copy-start.12
  520.8 6.8 %convert_reduce_fusion = f32[2,512,1024]{2,1,0:T(8,128)} fusion(bf16[3,2,512,1024]{3,2,1,0:T(8,128)(2,1)} %get-tuple-element.67), kind=kLoop, calls=%fused_computation | loop fusion | flops 5242880 | bytes 10485760 | tf_op jit(solution)/shard_map/reduce_sum | solution.py:1432
  527.6 0.0 copy-start.3
  527.6 0.0 copy-done.13
  527.7 0.4 dynamic_update_slice.3
  528.1 0.0 copy-done.4
  528.1 0.0 copy-done.12
  528.1 2.4 fusion.9
  530.5 0.2 scatter.6
  530.7 0.2 scatter.9.value_ref
  530.9 0.0 copy-start.10
  530.9 0.6 copy-done.10
  531.5 15.5 %shard_map.171 = f32[8,2048]{1,0:T(8,128)} custom-call(f32[8,2048]{1,0:T(8,128)} %copy-done.10), custom_call_target="tpu_custom_call" | custom-call | tf_op jit(solution)/shard_map/pallas_call | solution.py:1324
  547.1 1.5 slice.45
  548.6 1.5 fusion.13
  550.1 0.0 copy-done.3
  550.1 0.0 copy-start.7
  550.1 6.4 %fusion.8 = (f32[2,128,2048]{2,1,0:T(8,128)}, bf16[2,128,2048]{2,1,0:T(8,128)(2,1)}) fusion(bf16[2,128,2048]{2,1,0:T(8,128)(2,1)S(1)} %copy-done.4, f32[2,128,2048]{2,1,0:T(8,128)} %get-tuple-element.63, f32[2,128]{1,0:T(2,128)S(1)} %broadcast_multiply_fusion, f32[2048]{0:T(1024)S(1)} %copy-done.12, f32[2,128]{1,0:T(2,128)S(1)} %add_rsqrt_fusion.1, ...), kind=kLoop, calls=%fused_computation.13 | loop fusion | flops 9437184 | bytes 13652992 | tf_op jit(solution)/shard_map/add | solution.py:1436
  556.4 0.0 copy-done.7
  556.4 0.0 copy-start.8
  556.4 1.9 convert_reduce_fusion.1
  558.3 0.0 copy-start.9
  558.3 0.0 copy-start.1
  558.3 0.2 copy-done.8
  558.5 1.5 convert_reduce_fusion.2
  560.0 0.0 copy-done.9
  560.0 0.9 convert_reduce_fusion.3
  560.9 0.0 copy-done.1
  (7 shorter events, 0.0 us)
Async XLA Ops:
  0.6 0.8 copy-start
  7.5 329.9 %copy-start.11 = (f32[2048]{0:T(1024)S(1)}, f32[2048]{0:T(1024)}, u32[]{:S(2)}) copy-start(f32[2048]{0:T(1024)} %param.18) | copy-start | bytes 24580
  335.4 2.2 copy-start.2
  337.6 2.4 copy-start.5
  337.6 2.5 copy-start.6
  520.8 6.9 %copy-start.13 = (f32[8,256]{1,0:T(8,128)S(1)}, f32[8,256]{1,0:T(8,128)}, u32[]{:S(2)}) copy-start(f32[8,256]{1,0:T(8,128)} %get-tuple-element.64) | copy-start | bytes 24580
  520.8 7.3 %copy-start.4 = (bf16[2,128,2048]{2,1,0:T(8,128)(2,1)S(1)}, bf16[2,128,2048]{2,1,0:T(8,128)(2,1)}, u32[]{:S(2)}) copy-start(bf16[2,128,2048]{2,1,0:T(8,128)(2,1)} %source_ref.1) | copy-start | bytes 3145732
  520.8 7.3 %copy-start.12 = (f32[2048]{0:T(1024)S(1)}, f32[2048]{0:T(1024)}, u32[]{:S(2)}) copy-start(f32[2048]{0:T(1024)} %param.17) | copy-start | bytes 24580
  527.6 22.4 %copy-start.3 = (f32[2,128,2048]{2,1,0:T(8,128)S(1)}, f32[2,128,2048]{2,1,0:T(8,128)}, u32[]{:S(2)}) copy-start(f32[2,128,2048]{2,1,0:T(8,128)} %get-tuple-element.51) | copy-start | bytes 6291460
  530.9 0.6 copy-start.10
  550.1 6.4 %copy-start.7 = (bf16[3,1024,512]{2,1,0:T(8,128)(2,1)S(1)}, bf16[3,1024,512]{2,1,0:T(8,128)(2,1)}, u32[]{:S(2)}) copy-start(bf16[3,1024,512]{2,1,0:T(8,128)(2,1)} %get-tuple-element.68) | copy-start | bytes 9437188
  556.4 2.0 copy-start.8
  558.3 1.7 copy-start.9
  558.3 2.6 copy-start.1

commit v7 on v6

--- a/solution.py
+++ b/solution.py
@@ -45,18 +45,11 @@
 
     def enter(self):
         barrier = pltpu.get_barrier_semaphore()
-
-        def greet(where):
+        models = 2 * self.chips
+        peers = [{"mp": lax.rem(self.m + step, models)} for step in range(1, models)]
+        for where in peers + [self.peer(step) for step in range(1, self.seqs)]:
             pl.semaphore_signal(barrier, inc=1, device_id=where, device_id_type=MESH)
-
-        greet(self.sibling)
-        for step in range(1, self.seqs):
-            greet(self.peer(step))
-        pl.when(self.has_above)(lambda: greet(self.above))
-        pl.when(self.has_below)(lambda: greet(self.below))
-        chips = self.chips
-        lines = (self.z + chips - 1) // chips + (2 * chips - 2 - self.z) // chips
-        pl.semaphore_wait(barrier, self.seqs + lines)
+        pl.semaphore_wait(barrier, models + self.seqs - 2)
 
 
 def remote(src, dst, send, recv, where):
@@ -225,6 +218,45 @@
                 pl.when(p.has_below & (chip < p.z))(lambda ch=chip, h=half: self.line_copy(1, ch, ch, h).wait_send())
 
 
+class StraightScatter(Scatter):
+    def straight(self, chip, half):
+        p = self.p
+        return remote(
+            self.mine(chip, half),
+            self.from_line.at[p.z, pl.ds(half * self.piece, self.piece)],
+            self.line_send.at[0, chip, half],
+            self.line_recv.at[p.z, half],
+            {"mp": chip * 2 + p.c},
+        )
+
+    def came(self, chip, half):
+        view = self.from_line.at[chip, pl.ds(half * self.piece, self.piece)]
+        return remote(view, view, self.line_send.at[0, chip, half], self.line_recv.at[chip, half], self.p.sibling)
+
+    def go(self, chip):
+        self.core_copy(chip).wait_recv()
+        for half in range(HALVES):
+            self.mine(chip, half)[...] = self.total(chip, half, []).astype(BF)
+            self.straight(chip, half).start()
+
+    def others(self):
+        return [lax.rem(self.p.z + step, self.p.chips) for step in range(1, self.p.chips)]
+
+    def finish(self, store):
+        self.core_copy(self.p.z).wait_recv()
+        for half in range(HALVES):
+            for chip in self.others():
+                self.came(chip, half).wait_recv()
+            store(half * self.piece, self.piece, self.total(self.p.z, half, self.others()))
+
+    def drain(self):
+        for chip in range(self.p.chips):
+            self.core_copy(chip).wait_send()
+        for chip in self.others():
+            for half in range(HALVES):
+                self.straight(chip, half).wait_send()
+
+
 def gather_sems(count, chips):
     return [pltpu.SemaphoreType.DMA((count, 3, chips, HALVES)), pltpu.SemaphoreType.DMA((count, 2, chips, HALVES))]
 
@@ -319,8 +351,8 @@
 def forward_kernel(
     seqs,
     models,
-    normed_ref,
     source_ref,
+    gain_mix_ref,
     gain_ref,
     top_ref,
     taps_ref,
@@ -337,6 +369,8 @@
     mixed_out,
     middle_out,
     grad_out,
+    low_out,
+    gain_out,
     mlp_part,
     act_rows,
     pair_grad,
@@ -382,17 +416,27 @@
     shard = width // seqs
     unit_block = min(512, units)
     wide_block = 512
+    gain_out[...] = jnp.zeros_like(gain_out)
+
+    def first_norm(slot):
+        for first in range(0, share, share // HALVES):
+            value = source_ref[slot, pl.ds(first, share // HALVES)].astype(F32)
+            scale = lax.rsqrt(jnp.mean(value * value, axis=-1, keepdims=True) + EPS)
+            rows[slot, pl.ds(p.m * share + first, share // HALVES)] = (value * scale * gain_mix_ref[...]).astype(BF)
+
+    for slot in range(slots):
+        first_norm(slot)
     p.enter()
 
-    firsts = [Gather(p, rows.at[slot], normed_ref.at[slot], picks(g_sems, slot)) for slot in range(slots)]
+    firsts = [Gather(p, rows.at[slot], None, picks(g_sems, slot)) for slot in range(slots)]
     tops = [Gather(p, top_rows.at[slot], top_ref.at[slot], picks(g_sems, slots + slot)) for slot in range(slots)]
     seconds = [Gather(p, rows.at[slot], None, picks(g_sems, 2 * slots + slot)) for slot in range(slots)]
 
-    def scatter(slot, index):
-        return Scatter(p, part.at[slot], from_core.at[slot], from_line.at[slot], picks(s_sems, index))
+    def scatter(slot, index, kind=Scatter):
+        return kind(p, part.at[slot], from_core.at[slot], from_line.at[slot], picks(s_sems, index))
 
     mix_sums = [scatter(slot, slot) for slot in range(slots)]
-    grad_sums = [scatter(slot, slots + slot) for slot in range(slots)]
+    grad_sums = [scatter(0, slots), scatter(1, slots + 1, StraightScatter)]
 
     def columns_of(owner):
         return pl.ds(pl.multiple_of(owner * shard, shard), shard)
@@ -437,13 +481,12 @@
         for name, index in moves.pop(0):
             getattr(late[index], name)()
 
-    def own(slot, which, source):
+    def own(slot):
         span = pl.ds(p.m * share, share)
-        return pltpu.make_async_copy(source.at[slot], which.at[slot, span], keep.at[slot + (slots if which is top_rows else 0)])
+        return pltpu.make_async_copy(top_ref.at[slot], top_rows.at[slot, span], keep.at[slot])
 
     for slot in range(slots):
-        own(slot, rows, normed_ref).start()
-        own(slot, top_rows, top_ref).start()
+        own(slot).start()
 
     def saved(index, src, dst):
         return pltpu.make_async_copy(src, dst, keep.at[2 * slots + index])
@@ -452,10 +495,16 @@
     gates_saved = [saved(slots + slot, gates, gates_out.at[slot, 1]) for slot in range(slots)]
     middle_saved = [saved(2 * slots + slot, total.at[slot], middle_out.at[slot]) for slot in range(slots)]
     grad_saved = [saved(3 * slots + slot, total.at[slot], grad_out.at[slot]) for slot in range(slots)]
+    low_saved = [
+        saved(4 * slots + 6 + slot, stage.at[pl.ds(slot * share, share)], low_out.at[slot]) for slot in range(slots)
+    ]
+    own_tops = [
+        saved(5 * slots + 6 + slot, top_ref.at[slot], top_tile.at[pl.ds(slot * share, share)]) for slot in range(slots)
+    ]
     in_saved = saved(4 * slots, in_full, in_rows)
     out_saved = saved(4 * slots + 1, out_full, out_rows)
     product_saved = saved(4 * slots + 2, product, product_out)
-    mixed_saved = saved(4 * slots + 3, mixed, mixed_out)
+    mixed_saved = [saved(6 * slots + 6 + slot, mixed, mixed_out.at[slot]) for slot in range(slots)]
     down_saved = saved(4 * slots + 4, down, down_grad)
     act_load = saved(4 * slots + 5, act_rows, acts.at[0])
 
@@ -511,13 +560,14 @@
             conv = 0.0
             for offset in range(taps_ref.shape[0]):
                 conv = conv + taps_ref[offset : offset + 1] * product[slot, pl.ds(8 + i * tile - offset, tile)]
-            mixed[slot, pl.ds(i * tile, tile)] = (gates[pl.ds(i * tile, tile)] * conv).astype(BF)
+            mixed[pl.ds(i * tile, tile)] = (gates[pl.ds(i * tile, tile)] * conv).astype(BF)
 
     def project_out(slot):
         for chip in far_first(p):
             span = pl.ds(chip * tile, tile)
-            part[slot, span] = nn(mixed[slot, span], out_full[...]).astype(BF)
+            part[slot, span] = nn(mixed[span], out_full[...]).astype(BF)
             mix_sums[slot].give(chip)
+        mixed_saved[slot].start()
 
     def middle(slot):
         def store(first, size, value):
@@ -535,10 +585,21 @@
         middle_saved[slot].wait()
 
         def store(first, size, value):
-            total[slot, pl.ds(first, size)] = value
+            span = pl.ds(first, size)
+            at = pl.ds(slot * share + first, size)
+            middle = total[slot, span]
+            scale = lax.rsqrt(jnp.mean(middle * middle, axis=-1, keepdims=True) + EPS)
+            unit = middle * scale
+            gain_out[0:1] += jnp.sum(value * unit, axis=0, keepdims=True)
+            scaled = value * gain_ref[...]
+            grad = scale * (scaled - unit * jnp.mean(scaled * unit, axis=-1, keepdims=True))
+            grad = grad + top_tile[at].astype(F32)
+            total[slot, span] = grad
+            stage[at] = grad.astype(BF)
 
         grad_sums[slot].finish(store)
         grad_saved[slot].start()
+        low_saved[slot].start()
 
     order = far_first(p)
     tiles = [(0, chip) for chip in order] + [(slot, chip) for slot in range(1, slots) for chip in order[::-1]]
@@ -592,22 +653,23 @@
         for thing in puts(index):
             thing.start()
 
-    pair_steps = 2 * (width // wide_block)
+    pair_block = 512
+    pair_steps = 2 * (width // pair_block)
 
     def pair_saved(index):
-        k, first = divmod(index, width // wide_block)
-        cut = pl.ds(first * wide_block, wide_block)
+        k, first = divmod(index, width // pair_block)
+        cut = pl.ds(first * pair_block, pair_block)
         return pltpu.make_async_copy(pair.at[k, cut], pair_grad.at[k, cut], pair_sem.at[index])
 
     def pair_step(index):
-        k, first = divmod(index, width // wide_block)
-        cut = pl.ds(first * wide_block, wide_block)
+        k, first = divmod(index, width // pair_block)
+        cut = pl.ds(first * pair_block, pair_block)
         value = 0.0
         for slot in range(slots):
             value = value + tn(rows[slot, :, cut], acts[k, slot])
         pair[k, cut] = value.astype(BF)
         pair_saved(index).start()
-        if first == width // wide_block - 1 and k == 0:
+        if first == width // pair_block - 1 and k == 0:
             act_load.start()
 
     def fetch_columns(index):
@@ -644,7 +706,6 @@
         piece.forward()
     firsts[1].start()
     steps[-1]()
-    own(0, rows, normed_ref).wait()
     firsts[0].arrived()
     rows_saved[0].start()
     for piece in early:
@@ -662,7 +723,6 @@
     convolve(0)
     project_out(0)
     weave(mix_sums[0].rounds(), steps[1:-1] + [tops[0].start, steps[-1]], [push] * 3)
-    own(1, rows, normed_ref).wait()
     firsts[1].arrived()
     rows_saved[1].start()
     gates_saved[0].wait()
@@ -673,6 +733,7 @@
     seconds[0].start()
     rows_saved[1].wait()
     firsts[1].drain()
+    mixed_saved[0].wait()
     convolve(1)
     project_out(1)
     hops, steps, more = mix_sums[1].rounds(), tops[0].rounds(), seconds[0].rounds()
@@ -683,13 +744,12 @@
     middle(1)
     seconds[1].start()
     product_saved.start()
-    mixed_saved.start()
-    own(0, top_rows, top_ref).wait()
+    own(0).wait()
     tops[0].arrived()
     seconds[0].arrived()
     for piece in late:
         piece.arrived()
-    own(1, top_rows, top_ref).wait()
+    own(1).wait()
     hops, steps, more = grad_sums[0].rounds(), tops[1].rounds(), seconds[1].rounds()
     for index in range(chips):
         work(index)
@@ -704,30 +764,31 @@
             tops[1].arrived()
         seconds[1].other_core(tiles[chips + index][1])
         work(chips + index)
+        if index > 1:
+            grad_sums[1].go(tiles[chips + index - 1][1])
+    for thing in puts(len(tiles) - 1):
+        thing.wait()
+    for thing in own_tops:
+        thing.start()
+    grad_sums[1].go(tiles[-1][1])
     in_saved.wait()
     for piece in pieces:
         piece.drain()
     for index in range(2):
         for thing in fetch_columns(index):
             thing.start()
-    hops = grad_sums[1].rounds()
-    hops[0]()
+    for thing in own_tops:
+        thing.wait()
     finish_grad(0)
-    for index in range(len(tiles) - 1, len(tiles)):
-        for thing in puts(index):
-            thing.wait()
     work_steps = [functools.partial(pair_step, index) for index in range(pair_steps)]
     work_steps += [functools.partial(down_step, index) for index in range(width // channels)]
-    spaced = len(work_steps) // len(hops)
-    for index, step in enumerate(work_steps):
+    for step in work_steps:
         step()
-        if (index + 1) % spaced == 0 and (index + 1) // spaced < len(hops):
-            hops[(index + 1) // spaced]()
     down_saved.start()
     finish_grad(1)
     for index in range(pair_steps):
         pair_saved(index).wait()
-    for thing in [gates_saved[1], out_saved, product_saved, mixed_saved, down_saved, *grad_saved]:
+    for thing in [gates_saved[1], out_saved, product_saved, mixed_saved[1], down_saved, *grad_saved, *low_saved]:
         thing.wait()
     for thing in tops + seconds + grad_sums:
         thing.drain()
@@ -735,8 +796,8 @@
         pl.when(has_later)(lambda slot=slot: halo(slot).wait_send())
 
 
-def forward(seqs, models, normed, source, gain, top, taps, mixer_in, mixer_out, gate_up, mlp_down):
-    slots, share, width = normed.shape
+def forward(seqs, models, source, gain_mix, gain, top, taps, mixer_in, mixer_out, gate_up, mlp_down):
+    slots, share, width = source.shape
     chips = models // 2
     block = share * models
     channels = mixer_in.shape[2]
@@ -757,13 +818,15 @@
             shape((slots, block, channels), BF),
             shape((slots, share, width), F32),
             shape((slots, share, width), F32),
+            shape((slots, share, width), BF),
+            shape((8, width), F32),
             shape((slots, block, width), BF),
             shape((slots, block, units), BF),
             shape((2, width, units), BF),
             shape((units, width), BF),
         ],
-        in_specs=[hbm, vmem, vmem, hbm, vmem] + [hbm] * 4,
-        out_specs=[hbm] * 13,
+        in_specs=[vmem, vmem, vmem, hbm, vmem] + [hbm] * 4,
+        out_specs=[hbm] * 10 + [vmem] + [hbm] * 4,
         scratch_shapes=[
             pltpu.VMEM((3, width, channels), BF),
             pltpu.VMEM((channels, width), BF),
@@ -771,7 +834,7 @@
             pltpu.VMEM((block, channels), F32),
             pltpu.VMEM((2, tile, channels), F32),
             pltpu.VMEM((slots, block + 8, channels), F32),
-            pltpu.VMEM((slots, block, channels), BF),
+            pltpu.VMEM((block, channels), BF),
             pltpu.VMEM((2, width, units), BF),
             pltpu.VMEM((units, width), BF),
             pltpu.VMEM((tile, width), BF),
@@ -787,7 +850,7 @@
             pltpu.SemaphoreType.DMA((8,)),
             pltpu.SemaphoreType.DMA((slots,)),
             pltpu.SemaphoreType.DMA((slots,)),
-            pltpu.SemaphoreType.DMA((6 * slots + 6,)),
+            pltpu.SemaphoreType.DMA((10 * slots + 6,)),
             pltpu.SemaphoreType.DMA,
             pltpu.SemaphoreType.DMA((2,)),
             pltpu.SemaphoreType.DMA((2, slots)),
@@ -797,7 +860,7 @@
             *scatter_sems(2 * slots, chips),
         ],
         compiler_params=pltpu.CompilerParams(collective_id=1, has_side_effects=True, vmem_limit_bytes=VMEM_LIMIT),
-    )(normed, source, gain, top, taps, mixer_in, mixer_out, gate_up, mlp_down)
+    )(source, gain_mix, gain, top, taps, mixer_in, mixer_out, gate_up, mlp_down)
 
 
 class Exchange:
@@ -905,6 +968,9 @@
     models,
     low_ref,
     mlp_part,
+    source_ref,
+    gain_ref,
+    gain_mlp_ref,
     taps_ref,
     in_ref,
     out_ref,
@@ -916,7 +982,7 @@
     down_grad,
     mlp_out,
     grad_out,
-    taps_out,
+    small_out,
     in_got,
     out_got,
     pair_got,
@@ -939,6 +1005,10 @@
     pair_room,
     in_room,
     out_room,
+    taps_out,
+    small,
+    by_model,
+    by_seq,
     load,
     cols_sem,
     w_send,
@@ -947,6 +1017,10 @@
     halo_send,
     halo_recv,
     free,
+    mp_send,
+    mp_recv,
+    seq_send,
+    seq_recv,
     *sems,
 ):
     p = Place(seqs, models)
@@ -1061,6 +1135,8 @@
             conv_grad[slot, pl.ds(block, 8)] = jnp.zeros((8, channels), F32)
 
     taps_out[...] = jnp.zeros_like(taps_out)
+    small[...] = jnp.zeros_like(small)
+    small[1:2] = gain_mlp_ref[0:1]
 
     def first_pass(slot):
         for i in range(chips):
@@ -1101,11 +1177,57 @@
 
             sums[slot].give(chip)
 
-    def finish(what, total, slot):
+    def finish_mlp(slot):
         def store(first, size, value):
-            total[slot, pl.ds(first, size)] = value
-
-        what[slot].finish(store)
+            mlp_total[slot, pl.ds(first, size)] = value
+
+        mlp_sums[slot].finish(store)
+
+    def finish_grad(slot):
+        def store(first, size, value):
+            span = pl.ds(first, size)
+            source = source_ref[slot, span].astype(F32)
+            scale = lax.rsqrt(jnp.mean(source * source, axis=-1, keepdims=True) + EPS)
+            unit = source * scale
+            small[0:1] += jnp.sum(value * unit, axis=0, keepdims=True)
+            scaled = value * gain_ref[...]
+            grad_total[slot, span] = scale * (scaled - unit * jnp.mean(scaled * unit, axis=-1, keepdims=True))
+
+        sums[slot].finish(store)
+
+    def mine(owner):
+        return pl.ds(pl.multiple_of(owner * channels, channels), channels)
+
+    def small_sums():
+        small[2 : 2 + taps, mine(p.m)] = taps_out[0:taps]
+        along = [lax.rem(p.m + step, models) for step in range(1, models)]
+        by_model[p.m] = small[:, mine(p.m)]
+        copies = [
+            remote(small.at[:, mine(peer)], by_model.at[p.m], mp_send.at[0, i], mp_recv.at[0, i], {"mp": peer})
+            for i, peer in enumerate(along)
+        ]
+        for thing in copies:
+            thing.start()
+        for thing in copies:
+            thing.wait()
+        by_seq[p.s] = functools.reduce(lambda a, b: a + b, [by_model[i] for i in range(models)])
+        copies = [
+            remote(by_seq.at[p.s], by_seq.at[p.s], seq_send.at[step - 1], seq_recv.at[step - 1], p.peer(step))
+            for step in range(1, seqs)
+        ]
+        for thing in copies:
+            thing.start()
+        for thing in copies:
+            thing.wait()
+        small_out[:, mine(p.m)] = functools.reduce(lambda a, b: a + b, [by_seq[i] for i in range(seqs)])
+        copies = [
+            remote(small_out.at[:, mine(p.m)], small_out.at[:, mine(p.m)], mp_send.at[1, i], mp_recv.at[1, i], {"mp": peer})
+            for i, peer in enumerate(along)
+        ]
+        for thing in copies:
+            thing.start()
+        for thing in copies:
+            thing.wait()
 
     def neighbours(act):
         act(p.sibling)
@@ -1169,7 +1291,7 @@
     mlp_hops, next_rows, hops = mlp_sums[1].rounds(), gathers[1].rounds(), sums[0].rounds()
     first_pass(0)
     push()
-    finish(mlp_sums, mlp_total, 0)
+    finish_mlp(0)
     give_free(0)
     weave(mlp_hops[:1], next_rows[:1])
     second_pass(0)
@@ -1179,7 +1301,7 @@
     loads[3].wait()
     gathers[1].arrived()
     first_pass(1)
-    finish(mlp_sums, mlp_total, 1)
+    finish_mlp(1)
     give_free(1)
     hops[1]()
     second_pass(1)
@@ -1197,14 +1319,15 @@
     pieces[7].forward()
     pieces[6].forward()
     weave(hops[2:])
-    finish(sums, grad_total, 0)
-    finish(sums, grad_total, 1)
+    finish_grad(0)
+    finish_grad(1)
     last = [
         pltpu.make_async_copy(mlp_total, mlp_out, load.at[0]),
         pltpu.make_async_copy(grad_total, grad_out, load.at[1]),
     ]
     for thing in last:
         thing.start()
+    small_sums()
     for thing in pieces:
         thing.finish()
     for thing in last:
@@ -1216,7 +1339,7 @@
 
 
 def mixer_backward(
-    seqs, models, low, mlp_part, taps, in_full, out_full, normed_rows, gates, product, mixed, pair_grad, down_grad
+    seqs, models, low, mlp_part, source, gain, gain_mlp_part, taps, in_full, out_full, normed_rows, gates, product, mixed, pair_grad, down_grad
 ):
     slots, share, width = low.shape
     chips = models // 2
@@ -1233,13 +1356,13 @@
         out_shape=[
             shape((slots, share, width), F32),
             shape((slots, share, width), F32),
-            shape((8, channels), F32),
+            shape((8, width), F32),
             shape((gots, 3, shard, channels), BF),
             shape((gots, channels, shard), BF),
             shape((gots, 2, shard, units), BF),
             shape((gots, units, shard), BF),
         ],
-        in_specs=[hbm, hbm, vmem] + [hbm] * 8,
+        in_specs=[hbm, hbm, vmem, vmem, vmem, vmem] + [hbm] * 8,
         out_specs=[hbm, hbm, vmem] + [hbm] * 4,
         scratch_shapes=[
             pltpu.VMEM((3, width, channels), BF),
@@ -1260,6 +1383,10 @@
             pltpu.VMEM((4, 2, 2, shard // 4, units), BF),
             pltpu.VMEM((2, 2, 3, shard // 2, channels), BF),
             pltpu.VMEM((2, 2, channels // 2, shard), BF),
+            pltpu.VMEM((8, channels), F32),
+            pltpu.VMEM((8, width), F32),
+            pltpu.VMEM((models, 8, channels), F32),
+            pltpu.VMEM((seqs, 8, channels), F32),
             pltpu.SemaphoreType.DMA((2 * slots + 5,)),
             pltpu.SemaphoreType.DMA((2,)),
             pltpu.SemaphoreType.DMA((8, max(6, seqs - 1))),
@@ -1268,87 +1395,15 @@
             pltpu.SemaphoreType.DMA((slots,)),
             pltpu.SemaphoreType.DMA((slots,)),
             pltpu.SemaphoreType.REGULAR((slots,)),
+            pltpu.SemaphoreType.DMA((2, models - 1)),
+            pltpu.SemaphoreType.DMA((2, models - 1)),
+            pltpu.SemaphoreType.DMA((seqs - 1,)),
+            pltpu.SemaphoreType.DMA((seqs - 1,)),
             *gather_sems(slots, chips),
             *scatter_sems(2 * slots, chips),
         ],
         compiler_params=pltpu.CompilerParams(collective_id=3, has_side_effects=True, vmem_limit_bytes=VMEM_LIMIT),
-    )(low, mlp_part, taps, in_full, out_full, normed_rows, gates, product, mixed, pair_grad, down_grad)
-
-
-def small_sum_kernel(seqs, models, value_ref, out_ref, by_model, by_seq, send, recv, seq_send, seq_recv):
-    s, m = lax.axis_index("seq"), lax.axis_index("mp")
-    cols = by_seq.shape[-1]
-    along = [lax.rem(m + step, models) for step in range(1, models)]
-    across = [lax.rem(s + step, seqs) for step in range(1, seqs)]
-
-    def span(owner):
-        return pl.ds(pl.multiple_of(owner * cols, cols), cols)
-
-    barrier = pltpu.get_barrier_semaphore()
-    for where in [{"mp": peer} for peer in along] + [{"seq": peer} for peer in across]:
-        pl.semaphore_signal(barrier, inc=1, device_id=where, device_id_type=MESH)
-    pl.semaphore_wait(barrier, models + seqs - 2)
-    by_model[m] = value_ref[:, span(m)]
-    copies = [
-        remote(value_ref.at[:, span(peer)], by_model.at[m], send.at[0, i], recv.at[0, i], {"mp": peer})
-        for i, peer in enumerate(along)
-    ]
-    for thing in copies:
-        thing.start()
-    for thing in copies:
-        thing.wait()
-    by_seq[s] = functools.reduce(lambda a, b: a + b, [by_model[i] for i in range(models)])
-    copies = [
-        remote(by_seq.at[s], by_seq.at[s], seq_send.at[i], seq_recv.at[i], {"seq": peer})
-        for i, peer in enumerate(across)
-    ]
-    for thing in copies:
-        thing.start()
-    for thing in copies:
-        thing.wait()
-    out_ref[:, span(m)] = functools.reduce(lambda a, b: a + b, [by_seq[i] for i in range(seqs)])
-    copies = [
-        remote(out_ref.at[:, span(m)], out_ref.at[:, span(m)], send.at[1, i], recv.at[1, i], {"mp": peer})
-        for i, peer in enumerate(along)
-    ]
-    for thing in copies:
-        thing.start()
-    for thing in copies:
-        thing.wait()
-
-
-def small_sum(seqs, models, value):
-    vmem = pl.BlockSpec(memory_space=pltpu.VMEM)
-    height, width = value.shape
-    cols = width // models
-    return pl.pallas_call(
-        functools.partial(small_sum_kernel, seqs, models),
-        out_shape=jax.ShapeDtypeStruct(value.shape, F32),
-        in_specs=[vmem],
-        out_specs=vmem,
-        scratch_shapes=[
-            pltpu.VMEM((models, height, cols), F32),
-            pltpu.VMEM((seqs, height, cols), F32),
-            pltpu.SemaphoreType.DMA((2, models - 1)),
-            pltpu.SemaphoreType.DMA((2, models - 1)),
-            pltpu.SemaphoreType.DMA((seqs - 1,)),
-            pltpu.SemaphoreType.DMA((seqs - 1,)),
-        ],
-        compiler_params=pltpu.CompilerParams(collective_id=4, has_side_effects=True),
-    )(value)
-
-
-def normalize(values, gain):
-    scale = lax.rsqrt(jnp.mean(values * values, axis=-1, keepdims=True) + EPS)
-    return (values * scale * gain, scale)
-
-
-def norm_back(grad, values, scale, gain):
-    unit = values * scale
-    scaled = grad * gain
-    gain_grad = jnp.sum(grad * unit, axis=(0, 1))
-    input_grad = scale * (scaled - unit * jnp.mean(scaled * unit, axis=-1, keepdims=True))
-    return (input_grad, gain_grad)
+    )(low, mlp_part, source, gain, gain_mlp_part, taps, in_full, out_full, normed_rows, gates, product, mixed, pair_grad, down_grad)
 
 
 def local(
@@ -1366,16 +1421,14 @@
     seqs, models = lax.axis_size("seq"), lax.axis_size("mp")
     seq_pos = lax.axis_index("seq")
     model_pos = lax.axis_index("mp")
-    slots, share, width = hidden.shape
+    share = hidden.shape[1]
     channels = mixer_in.shape[2]
     taps = conv_weight.shape[0]
     local_taps = lax.dynamic_slice_in_dim(conv_weight, model_pos * channels, channels, 1)
     share_start = (seq_pos * models + model_pos) * share
     share_pos = share_start + jnp.arange(share, dtype=jnp.int32)
     mask = (share_pos[None, :] < lengths[:, None]).astype(F32)[:, :, None]
-    source = hidden.astype(F32)
-    top_grad = cotangent.astype(F32) * mask
-    normed, scale_mix = normalize(source, gain_mix)
+    top_low = (cotangent.astype(F32) * mask).astype(BF)
     (
         normed_rows,
         _,
@@ -1386,6 +1439,8 @@
         mixed,
         middle,
         middle_grad,
+        low,
+        gain_mlp_part,
         mlp_part,
         _,
         pair_total,
@@ -1393,24 +1448,24 @@
     ) = forward(
         seqs,
         models,
-        normed.astype(BF),
         hidden,
+        gain_mix[None],
         gain_mlp[None],
-        top_grad.astype(BF),
+        top_low,
         local_taps,
         mixer_in,
         mixer_out,
         gate_up,
         mlp_down,
     )
-    scale_mlp = lax.rsqrt(jnp.mean(middle * middle, axis=-1, keepdims=True) + EPS)
-    middle_grad, gain_mlp_grad = norm_back(middle_grad, middle, scale_mlp, gain_mlp)
-    middle_grad = middle_grad + top_grad
-    mlp_share, source_grad, taps_part, in_got, out_got, pair_got, down_got = mixer_backward(
+    mlp_share, source_grad, small, in_got, out_got, pair_got, down_got = mixer_backward(
         seqs,
         models,
-        middle_grad.astype(BF),
+        low,
         mlp_part,
+        hidden,
+        gain_mix[None],
+        gain_mlp_part,
         local_taps,
         in_full,
         out_full,
@@ -1421,18 +1476,12 @@
         pair_total,
         down_total,
     )
-    output = (mask * (middle + mlp_share)).astype(BF)
-    source_grad, gain_mix_grad = norm_back(source_grad, source, scale_mix, gain_mix)
-    small = jnp.zeros((8, width), F32)
-    small = lax.dynamic_update_slice(small, taps_part[:taps], (2, model_pos * channels))
-    small = small.at[0].set(gain_mix_grad).at[1].set(gain_mlp_grad)
-    small = small_sum(seqs, models, small)
 
     def total(got):
         return jnp.sum(got.astype(F32), axis=0)
 
     return (
-        output,
+        (mask * (middle + mlp_share)).astype(BF),
         source_grad + middle_grad,
         small[0],
         small[1],

time: 570 us -> 552 us (0.968)
  other arithmetic: 31.3 us -> 16.2 us
    pallas_call x1 -> x0, Pallas kernels: 15.5 us -> none  [small_sum(): pl.pallas_call(functools.partial(small_sum_kernel, seqs, models), out_sha...]
    pallas_call x1, Pallas kernels: 179 us -> 191 us  [mixer_backward(): pl.pallas_call(functools.partial(mixer_backward_kernel, seqs, models), ou...]
    reduce_sum x4 -> x0, other arithmetic: 8.2 us -> none  [the longest x2 4.73 us: norm_back(): gain_grad = jnp.sum(grad * unit, axis=(0, 1))]
    pallas_call x1, Pallas kernels: 328 us -> 334 us  [forward(): pl.pallas_call(functools.partial(forward_kernel, seqs, models), out_shape...]
where the time goes in v7:
time: 552 us; the launch traced here: 543 us
  Pallas kernels  524 us (95%)
  other arithmetic  16.2 us (3%)
    pallas_call x1, Pallas kernels, forward(): pl.pallas_call(functools.partial(forward_kernel, seqs, models), out_shape...  334 us
    pallas_call x1, Pallas kernels, mixer_backward(): pl.pallas_call(functools.partial(mixer_backward_kernel, seqs, models), ou...  191 us

profile of v7, /device:TPU:0, one launch (start us, length us, event | category | flops | bytes accessed | tf_op | source)
XLA Modules:
  0.0 543.5 jit_solution(2287130754704619141)
XLA Ops:
  0.6 0.0 copy-start
  0.7 0.7 compare_convert_fusion
  1.4 0.0 copy-done
  1.4 0.6 constant_dynamic-slice_fusion.taps_ref
  2.0 2.4 multiply_convert_fusion.1.top_ref
  4.4 333.9 %shard_map.169 = (bf16[2,1024,2048]{2,1,0:T(8,128)(2,1)}, bf16[2,1024,2048]{2,1,0:T(8,128)(2,1)}, bf16[3,2048,256]{2,1,0:T(8,128)(2,1)}, bf16[256,2048]{1,0:T(8,...) custom-call(bf16[2,128,2048]{2,1,0:T(8,128)(2,1)} %source_ref.3, ...), custom_call_target="tpu_custom_call" | custom-call | tf_op jit(solution)/shard_map/pallas_call | solution.py:809
  338.4 190.5 %shard_map.170 = (f32[2,128,2048]{2,1,0:T(8,128)}, f32[2,128,2048]{2,1,0:T(8,128)}, f32[8,2048]{1,0:T(8,128)}, bf16[3,3,512,256]{3,2,1,0:T(8,128)(2,1)}, bf16[3,...) custom-call(bf16[2,128,2048]{2,1,0:T(8,128)(2,1)} %get-tuple-element.30.low_ref, ...), custom_call_target="tpu_custom_call" | custom-call | tf_op jit(solution)/shard_map/pallas_call | solution.py:1354
  528.9 0.0 copy-start.4
  528.9 0.0 copy-start.5
  528.9 0.0 copy-start.7
  528.9 0.0 copy-start.6
  529.0 3.6 multiply_convert_fusion
  532.5 0.0 copy-done.4
  532.5 0.0 copy-done.5
  532.5 0.0 copy-start.3
  532.5 0.0 slice-start
  532.5 1.6 add.27
  534.1 0.0 copy-done.7
  534.1 0.6 fusion
  534.7 0.6 slice.11
  535.4 0.0 copy-done.6
  535.4 0.0 copy-start.2
  535.4 0.9 convert_reduce_fusion.3
  536.3 0.0 copy-done.3
  536.3 0.0 slice-start.1
  536.3 1.5 convert_reduce_fusion.2
  537.8 0.0 copy-done.2
  537.8 1.8 convert_reduce_fusion.1
  539.6 0.0 slice-done
  539.6 0.0 slice-done.1
  539.7 0.0 copy-start.1
  539.7 3.6 convert_reduce_fusion
  543.3 0.0 copy-done.1
  (2 shorter events, 0.0 us)
Async XLA Ops:
  0.6 0.8 copy-start
  528.9 3.6 copy-start.4
  528.9 3.6 copy-start.5
  528.9 5.2 copy-start.7
  528.9 6.4 %copy-start.6 = (bf16[3,256,512]{2,1,0:T(8,128)(2,1)S(1)}, bf16[3,256,512]{2,1,0:T(8,128)(2,1)}, u32[]{:S(2)}) copy-start(bf16[3,256,512]{2,1,0:T(8,128)(2,1)} %get-tuple-element.46) | copy-start | bytes 2359300
  532.5 3.7 copy-start.3
  532.5 7.1 %slice-start = ((s8[6291456]{0:T(1024)(128)(4,1)}), s8[4194304]{0:T(1024)(128)(4,1)S(1)}, s32[]{:S(2)}) async-start(s8[6291456]{0:T(1024)(128)(4,1)} %bitcast.4), calls=%async_computation | async-start | bytes 8388608
  535.4 2.5 copy-start.2
  536.3 3.4 slice-start.1
  539.7 3.6 copy-start.1

commit v8 on v7

--- a/solution.py
+++ b/solution.py
@@ -619,7 +619,7 @@
     def work(index):
         slot, chip = tiles[index]
         span = pl.ds(chip * tile, tile)
-        if index == 0 or slot > 0:
+        if index % chips == 0:
             fetch(index).start()
         fetch(index).wait()
         if index:
@@ -639,7 +639,7 @@
             acts[0, slot, span, cut] = (act_grad * up * sigma * (1.0 + gate * (1.0 - sigma))).astype(BF)
             acts[1, slot, span, cut] = (act_grad * silu).astype(BF)
 
-        if index + 1 < len(tiles) and tiles[index + 1][0] == 0:
+        if (index + 1) % chips:
             fetch(index + 1).start()
 
         @pl.loop(0, width // wide_block)
@@ -757,13 +757,13 @@
             steps[index]()
         if 0 < index:
             hops[index - 1]()
+    more[0]()
+    tops[1].arrived()
     for index in range(chips):
-        if index:
-            more[index - 1]()
-        else:
-            tops[1].arrived()
         seconds[1].other_core(tiles[chips + index][1])
         work(chips + index)
+        if index + 1 < len(more):
+            more[index + 1]()
         if index > 1:
             grad_sums[1].go(tiles[chips + index - 1][1])
     for thing in puts(len(tiles) - 1):
@@ -1050,8 +1050,9 @@
             ]
         )
     ]
-    for thing in loads:
-        thing.start()
+    for index, thing in enumerate(loads):
+        if index != 1:
+            thing.start()
     p.enter()
     gathers = [Gather(p, rows.at[slot], low_ref.at[slot], picks(g_sems, slot)) for slot in range(slots)]
 
@@ -1059,7 +1060,7 @@
         return Scatter(p, part.at[slot], from_core.at[slot], from_line.at[slot], picks(s_sems, index))
 
     mlp_sums = [scatter(slot, slot) for slot in range(slots)]
-    sums = [scatter(slot, slots + slot) for slot in range(slots)]
+    sums = [scatter(1 - slot, slots + slot) for slot in range(slots)]
     shard = width // seqs
     units = down_grad.shape[0]
 
@@ -1173,7 +1174,7 @@
                 value = 0.0
                 for k in range(3):
                     value = value + nt(stacked[slot, span, pl.ds(k * channels, channels)], in_full[k, cut])
-                part[slot, span, cut] = value.astype(BF)
+                part[1 - slot, span, cut] = value.astype(BF)
 
             sums[slot].give(chip)
 
@@ -1198,44 +1199,44 @@
     def mine(owner):
         return pl.ds(pl.multiple_of(owner * channels, channels), channels)
 
-    def small_sums():
-        small[2 : 2 + taps, mine(p.m)] = taps_out[0:taps]
-        along = [lax.rem(p.m + step, models) for step in range(1, models)]
-        by_model[p.m] = small[:, mine(p.m)]
-        copies = [
+    along = [lax.rem(p.m + step, models) for step in range(1, models)]
+    small_copies = [
+        [
             remote(small.at[:, mine(peer)], by_model.at[p.m], mp_send.at[0, i], mp_recv.at[0, i], {"mp": peer})
             for i, peer in enumerate(along)
-        ]
-        for thing in copies:
-            thing.start()
-        for thing in copies:
-            thing.wait()
-        by_seq[p.s] = functools.reduce(lambda a, b: a + b, [by_model[i] for i in range(models)])
-        copies = [
+        ],
+        [
             remote(by_seq.at[p.s], by_seq.at[p.s], seq_send.at[step - 1], seq_recv.at[step - 1], p.peer(step))
             for step in range(1, seqs)
-        ]
-        for thing in copies:
-            thing.start()
-        for thing in copies:
-            thing.wait()
-        small_out[:, mine(p.m)] = functools.reduce(lambda a, b: a + b, [by_seq[i] for i in range(seqs)])
-        copies = [
+        ],
+        [
             remote(small_out.at[:, mine(p.m)], small_out.at[:, mine(p.m)], mp_send.at[1, i], mp_recv.at[1, i], {"mp": peer})
             for i, peer in enumerate(along)
-        ]
-        for thing in copies:
-            thing.start()
-        for thing in copies:
-            thing.wait()
+        ],
+    ]
+
+    def small_stage(index):
+        if index:
+            for thing in small_copies[index - 1]:
+                thing.wait()
+        if index == 0:
+            small[2 : 2 + taps, mine(p.m)] = taps_out[0:taps]
+            by_model[p.m] = small[:, mine(p.m)]
+        elif index == 1:
+            by_seq[p.s] = functools.reduce(lambda a, b: a + b, [by_model[i] for i in range(models)])
+        elif index == 2:
+            small_out[:, mine(p.m)] = functools.reduce(lambda a, b: a + b, [by_seq[i] for i in range(seqs)])
+        if index < 3:
+            for thing in small_copies[index]:
+                thing.start()
 
     def neighbours(act):
         act(p.sibling)
         pl.when(p.has_above)(lambda: act(p.above))
         pl.when(p.has_below)(lambda: act(p.below))
 
-    def give_free(slot):
-        mlp_sums[slot].drain()
+    def give_free(slot, user):
+        user.drain()
         neighbours(
             lambda where: pl.semaphore_signal(free.at[slot], inc=1, device_id=where, device_id_type=MESH)
         )
@@ -1278,9 +1279,6 @@
     weave(hops[:-1], next_rows[:-1], [push] * 2)
     gathers[1].start()
     weave(hops[-1:], next_rows[-1:], [push])
-    loads[1].wait()
-    for chip in order:
-        mlp_sums[1].give(chip)
     loads[2].wait()
     for thing in loads[2 + slots :]:
         thing.wait()
@@ -1288,51 +1286,60 @@
     push()
     fetch_columns(0).start()
     fetch_columns(1).start()
-    mlp_hops, next_rows, hops = mlp_sums[1].rounds(), gathers[1].rounds(), sums[0].rounds()
     first_pass(0)
     push()
+    second_pass(0)
+    third_pass(0)
+    next_rows, hops = gathers[1].rounds(), sums[0].rounds()
+    weave(hops[:1], next_rows[:1])
     finish_mlp(0)
-    give_free(0)
-    weave(mlp_hops[:1], next_rows[:1])
-    second_pass(0)
-    take_free(0)
-    third_pass(0)
-    weave(mlp_hops[1:], next_rows[1:], hops[:1], [push] * 2)
+    give_free(0, mlp_sums[0])
+    weave(hops[1:], next_rows[1:], [push] * 2)
     loads[3].wait()
     gathers[1].arrived()
     first_pass(1)
-    finish_mlp(1)
-    give_free(1)
-    hops[1]()
     second_pass(1)
-    take_free(1)
-    weave(hops[2:])
+    take_free(0)
     third_pass(1)
     hops = sums[1].rounds()
     hops[0]()
+    finish_grad(0)
+    give_free(1, sums[0])
+    loads[1].start()
     out_step()
     pieces[7].start()
+    hops[1]()
+    loads[1].wait()
+    take_free(1)
+    for chip in order:
+        mlp_sums[1].give(chip)
     for index in range(steps_in):
         in_step(index)
     pieces[6].start()
+    weave(hops[2:])
+    hops = mlp_sums[1].rounds()
+    hops[0]()
+    pieces[7].forward()
+    finish_grad(1)
+    small_stage(0)
+    pieces[6].forward()
     hops[1]()
-    pieces[7].forward()
-    pieces[6].forward()
+    small_stage(1)
     weave(hops[2:])
-    finish_grad(0)
-    finish_grad(1)
+    small_stage(2)
+    finish_mlp(1)
     last = [
         pltpu.make_async_copy(mlp_total, mlp_out, load.at[0]),
-        pltpu.make_async_copy(grad_total, grad_out, load.at[1]),
+        pltpu.make_async_copy(grad_total, grad_out, load.at[2]),
     ]
     for thing in last:
         thing.start()
-    small_sums()
+    small_stage(3)
     for thing in pieces:
         thing.finish()
     for thing in last:
         thing.wait()
-    for thing in gathers + sums:
+    for thing in gathers + [sums[1], mlp_sums[1]]:
         thing.drain()
     for slot in range(slots):
         pl.when(has_earlier)(lambda slot=slot: halo(slot).wait_send())

time: 552 us -> 561 us (1.016)
  Pallas kernels: 524 us -> 535 us
    pallas_call x1, Pallas kernels: 191 us -> 199 us  [mixer_backward(): pl.pallas_call(functools.partial(mixer_backward_kernel, seqs, models), ou...]
where the time goes in v8:
time: 561 us; the launch traced here: 554 us
  Pallas kernels  535 us (95%)
  other arithmetic  16.2 us (3%)
    pallas_call x1, Pallas kernels, forward(): pl.pallas_call(functools.partial(forward_kernel, seqs, models), out_shape...  336 us
    pallas_call x1, Pallas kernels, mixer_backward(): pl.pallas_call(functools.partial(mixer_backward_kernel, seqs, models), ou...  199 us

profile of v8, /device:TPU:0, one launch (start us, length us, event | category | flops | bytes accessed | tf_op | source)
XLA Modules:
  0.0 553.6 jit_solution(13359810452755485987)
XLA Ops:
  0.6 0.0 copy-start
  0.7 0.7 compare_convert_fusion
  1.4 0.0 copy-done
  1.4 0.6 constant_dynamic-slice_fusion.taps_ref
  2.0 2.4 multiply_convert_fusion.1.top_ref
  4.4 335.8 %shard_map.169 = (bf16[2,1024,2048]{2,1,0:T(8,128)(2,1)}, bf16[2,1024,2048]{2,1,0:T(8,128)(2,1)}, bf16[3,2048,256]{2,1,0:T(8,128)(2,1)}, bf16[256,2048]{1,0:T(8,...) custom-call(bf16[2,128,2048]{2,1,0:T(8,128)(2,1)} %source_ref.3, ...), custom_call_target="tpu_custom_call" | custom-call | tf_op jit(solution)/shard_map/pallas_call | solution.py:809
  340.2 198.8 %shard_map.170 = (f32[2,128,2048]{2,1,0:T(8,128)}, f32[2,128,2048]{2,1,0:T(8,128)}, f32[8,2048]{1,0:T(8,128)}, bf16[3,3,512,256]{3,2,1,0:T(8,128)(2,1)}, bf16[3,...) custom-call(bf16[2,128,2048]{2,1,0:T(8,128)(2,1)} %get-tuple-element.30.low_ref, ...), custom_call_target="tpu_custom_call" | custom-call | tf_op jit(solution)/shard_map/pallas_call | solution.py:1361
  539.0 0.0 copy-start.4
  539.0 0.0 copy-start.5
  539.0 0.0 copy-start.7
  539.0 0.0 copy-start.6
  539.0 3.6 multiply_convert_fusion
  542.6 0.0 copy-done.4
  542.6 0.0 copy-done.5
  542.6 0.0 copy-start.3
  542.6 0.0 slice-start
  542.6 1.6 add.27
  544.2 0.0 copy-done.7
  544.2 0.6 fusion
  544.8 0.6 slice.11
  545.4 0.0 copy-done.6
  545.4 0.0 copy-start.2
  545.4 0.9 convert_reduce_fusion.3
  546.3 0.0 copy-done.3
  546.3 0.0 slice-start.1
  546.3 1.5 convert_reduce_fusion.2
  547.9 0.0 copy-done.2
  547.9 1.8 convert_reduce_fusion.1
  549.7 0.0 slice-done
  549.7 0.0 slice-done.1
  549.7 0.0 copy-start.1
  549.7 3.6 convert_reduce_fusion
  553.3 0.0 copy-done.1
  (2 shorter events, 0.0 us)
Async XLA Ops:
  0.6 0.8 copy-start
  539.0 3.6 copy-start.4
  539.0 3.6 copy-start.5
  539.0 5.2 copy-start.7
  539.0 6.4 %copy-start.6 = (bf16[3,256,512]{2,1,0:T(8,128)(2,1)S(1)}, bf16[3,256,512]{2,1,0:T(8,128)(2,1)}, u32[]{:S(2)}) copy-start(bf16[3,256,512]{2,1,0:T(8,128)(2,1)} %get-tuple-element.46) | copy-start | bytes 2359300
  542.6 3.7 copy-start.3
  542.6 7.1 %slice-start = ((s8[6291456]{0:T(1024)(128)(4,1)}), s8[4194304]{0:T(1024)(128)(4,1)S(1)}, s32[]{:S(2)}) async-start(s8[6291456]{0:T(1024)(128)(4,1)} %bitcast.4), calls=%async_computation | async-start | bytes 8388608
  545.4 2.5 copy-start.2
  546.3 3.4 slice-start.1
  549.7 3.6 copy-start.1

commit v9 on v7

--- a/solution.py
+++ b/solution.py
@@ -276,9 +276,10 @@
 
 def far_first(place):
     low, high = 0, place.chips - 1
+    inner = 1 - place.z // (place.chips // 2)
     order = []
     for _ in range(place.chips):
-        left = place.z - low >= high - place.z
+        left = 2 * place.z - low - high + inner > 0
         order.append(jnp.where(left, low, high))
         low, high = jnp.where(left, low + 1, low), jnp.where(left, high, high - 1)
     return order
@@ -424,8 +425,7 @@
             scale = lax.rsqrt(jnp.mean(value * value, axis=-1, keepdims=True) + EPS)
             rows[slot, pl.ds(p.m * share + first, share // HALVES)] = (value * scale * gain_mix_ref[...]).astype(BF)
 
-    for slot in range(slots):
-        first_norm(slot)
+    first_norm(0)
     p.enter()
 
     firsts = [Gather(p, rows.at[slot], None, picks(g_sems, slot)) for slot in range(slots)]
@@ -619,7 +619,7 @@
     def work(index):
         slot, chip = tiles[index]
         span = pl.ds(chip * tile, tile)
-        if index == 0 or slot > 0:
+        if index % chips == 0:
             fetch(index).start()
         fetch(index).wait()
         if index:
@@ -639,7 +639,7 @@
             acts[0, slot, span, cut] = (act_grad * up * sigma * (1.0 + gate * (1.0 - sigma))).astype(BF)
             acts[1, slot, span, cut] = (act_grad * silu).astype(BF)
 
-        if index + 1 < len(tiles) and tiles[index + 1][0] == 0:
+        if (index + 1) % chips:
             fetch(index + 1).start()
 
         @pl.loop(0, width // wide_block)
@@ -699,6 +699,7 @@
     firsts[0].start()
     for piece in early:
         piece.start()
+    first_norm(1)
     steps = firsts[0].rounds()
     for step in steps[:-1]:
         step()
@@ -757,15 +758,15 @@
             steps[index]()
         if 0 < index:
             hops[index - 1]()
+    more[0]()
+    tops[1].arrived()
     for index in range(chips):
-        if index:
-            more[index - 1]()
-        else:
-            tops[1].arrived()
         seconds[1].other_core(tiles[chips + index][1])
         work(chips + index)
-        if index > 1:
-            grad_sums[1].go(tiles[chips + index - 1][1])
+        if 0 < index < chips - 1:
+            grad_sums[1].go(tiles[chips + index][1])
+        if index + 1 < len(more):
+            more[index + 1]()
     for thing in puts(len(tiles) - 1):
         thing.wait()
     for thing in own_tops:

time: 552 us -> 550 us (level)
  no operation moved by 1% of the time
where the time goes in v9:
time: 550 us; the launch traced here: 541 us
  Pallas kernels  522 us (95%)
  other arithmetic  16.2 us (3%)
    pallas_call x1, Pallas kernels, forward(): pl.pallas_call(functools.partial(forward_kernel, seqs, models), out_shape...  334 us
    pallas_call x1, Pallas kernels, mixer_backward(): pl.pallas_call(functools.partial(mixer_backward_kernel, seqs, models), ou...  188 us

profile of v9, /device:TPU:0, one launch (start us, length us, event | category | flops | bytes accessed | tf_op | source)
XLA Modules:
  0.0 541.1 jit_solution(7679365088429443168)
XLA Ops:
  0.6 0.0 copy-start
  0.7 0.7 compare_convert_fusion
  1.4 0.0 copy-done
  1.4 0.6 constant_dynamic-slice_fusion.taps_ref
  2.0 2.4 multiply_convert_fusion.1.top_ref
  4.4 334.4 %shard_map.169 = (bf16[2,1024,2048]{2,1,0:T(8,128)(2,1)}, bf16[2,1024,2048]{2,1,0:T(8,128)(2,1)}, bf16[3,2048,256]{2,1,0:T(8,128)(2,1)}, bf16[256,2048]{1,0:T(8,...) custom-call(bf16[2,128,2048]{2,1,0:T(8,128)(2,1)} %source_ref.3, ...), custom_call_target="tpu_custom_call" | custom-call | tf_op jit(solution)/shard_map/pallas_call | solution.py:810
  338.8 187.7 %shard_map.170 = (f32[2,128,2048]{2,1,0:T(8,128)}, f32[2,128,2048]{2,1,0:T(8,128)}, f32[8,2048]{1,0:T(8,128)}, bf16[3,3,512,256]{3,2,1,0:T(8,128)(2,1)}, bf16[3,...) custom-call(bf16[2,128,2048]{2,1,0:T(8,128)(2,1)} %get-tuple-element.30.low_ref, ...), custom_call_target="tpu_custom_call" | custom-call | tf_op jit(solution)/shard_map/pallas_call | solution.py:1355
  526.6 0.0 copy-start.4
  526.6 0.0 copy-start.5
  526.6 0.0 copy-start.7
  526.6 0.0 copy-start.6
  526.6 3.6 multiply_convert_fusion
  530.2 0.0 copy-done.4
  530.2 0.0 copy-done.5
  530.2 0.0 copy-start.3
  530.2 0.0 slice-start
  530.2 1.6 add.27
  531.8 0.0 copy-done.7
  531.8 0.6 fusion
  532.4 0.6 slice.11
  533.0 0.0 copy-done.6
  533.0 0.0 copy-start.2
  533.0 0.9 convert_reduce_fusion.3
  533.9 0.0 copy-done.3
  533.9 0.0 slice-start.1
  533.9 1.5 convert_reduce_fusion.2
  535.5 0.0 copy-done.2
  535.5 1.8 convert_reduce_fusion.1
  537.3 0.0 slice-done
  537.3 0.0 slice-done.1
  537.3 0.0 copy-start.1
  537.3 3.6 convert_reduce_fusion
  540.9 0.0 copy-done.1
  (2 shorter events, 0.0 us)
Async XLA Ops:
  0.6 0.8 copy-start
  526.6 3.6 copy-start.4
  526.6 3.6 copy-start.5
  526.6 5.2 copy-start.7
  526.6 6.4 %copy-start.6 = (bf16[3,256,512]{2,1,0:T(8,128)(2,1)S(1)}, bf16[3,256,512]{2,1,0:T(8,128)(2,1)}, u32[]{:S(2)}) copy-start(bf16[3,256,512]{2,1,0:T(8,128)(2,1)} %get-tuple-element.46) | copy-start | bytes 2359300
  530.2 3.7 copy-start.3
  530.2 7.1 %slice-start = ((s8[6291456]{0:T(1024)(128)(4,1)}), s8[4194304]{0:T(1024)(128)(4,1)S(1)}, s32[]{:S(2)}) async-start(s8[6291456]{0:T(1024)(128)(4,1)} %bitcast.4), calls=%async_computation | async-start | bytes 8388608
  533.0 2.5 copy-start.2
  533.9 3.4 slice-start.1
  537.3 3.6 copy-start.1

commit v10 on v9

--- a/solution.py
+++ b/solution.py
@@ -616,7 +616,7 @@
             pltpu.make_async_copy(act_stage, act_rows.at[slot, span], out_sem.at[1]),
         ]
 
-    def work(index):
+    def work(index, midway=None):
         slot, chip = tiles[index]
         span = pl.ds(chip * tile, tile)
         if index % chips == 0:
@@ -641,6 +641,9 @@
 
         if (index + 1) % chips:
             fetch(index + 1).start()
+
+        if midway:
+            midway()
 
         @pl.loop(0, width // wide_block)
         def _(i):
@@ -753,20 +756,17 @@
     own(1).wait()
     hops, steps, more = grad_sums[0].rounds(), tops[1].rounds(), seconds[1].rounds()
     for index in range(chips):
-        work(index)
+        work(index, more[0] if index == chips - 1 else None)
         if index < len(steps):
             steps[index]()
         if 0 < index:
             hops[index - 1]()
-    more[0]()
     tops[1].arrived()
     for index in range(chips):
         seconds[1].other_core(tiles[chips + index][1])
-        work(chips + index)
+        work(chips + index, more[index + 1] if index + 1 < len(more) else None)
         if 0 < index < chips - 1:
             grad_sums[1].go(tiles[chips + index][1])
-        if index + 1 < len(more):
-            more[index + 1]()
     for thing in puts(len(tiles) - 1):
         thing.wait()
     for thing in own_tops:

time: 550 us -> 544 us (0.989)
  no operation moved by 1% of the time
where the time goes in v10:
time: 544 us; the launch traced here: 536 us
  Pallas kernels  517 us (95%)
  other arithmetic  16.2 us (3%)
    pallas_call x1, Pallas kernels, forward(): pl.pallas_call(functools.partial(forward_kernel, seqs, models), out_shape...  330 us
    pallas_call x1, Pallas kernels, mixer_backward(): pl.pallas_call(functools.partial(mixer_backward_kernel, seqs, models), ou...  187 us

profile of v10, /device:TPU:0, one launch (start us, length us, event | category | flops | bytes accessed | tf_op | source)
XLA Modules:
  0.0 535.5 jit_solution(1967468376234113175)
XLA Ops:
  0.6 0.0 copy-start
  0.7 0.7 compare_convert_fusion
  1.4 0.0 copy-done
  1.4 0.6 constant_dynamic-slice_fusion.taps_ref
  2.0 2.4 multiply_convert_fusion.1.top_ref
  4.4 329.8 %shard_map.169 = (bf16[2,1024,2048]{2,1,0:T(8,128)(2,1)}, bf16[2,1024,2048]{2,1,0:T(8,128)(2,1)}, bf16[3,2048,256]{2,1,0:T(8,128)(2,1)}, bf16[256,2048]{1,0:T(8,...) custom-call(bf16[2,128,2048]{2,1,0:T(8,128)(2,1)} %source_ref.3, ...), custom_call_target="tpu_custom_call" | custom-call | tf_op jit(solution)/shard_map/pallas_call | solution.py:810
  334.3 186.7 %shard_map.170 = (f32[2,128,2048]{2,1,0:T(8,128)}, f32[2,128,2048]{2,1,0:T(8,128)}, f32[8,2048]{1,0:T(8,128)}, bf16[3,3,512,256]{3,2,1,0:T(8,128)(2,1)}, bf16[3,...) custom-call(bf16[2,128,2048]{2,1,0:T(8,128)(2,1)} %get-tuple-element.30.low_ref, ...), custom_call_target="tpu_custom_call" | custom-call | tf_op jit(solution)/shard_map/pallas_call | solution.py:1355
  521.0 0.0 copy-start.4
  521.0 0.0 copy-start.5
  521.0 0.0 copy-start.7
  521.0 0.0 copy-start.6
  521.0 3.6 multiply_convert_fusion
  524.6 0.0 copy-done.4
  524.6 0.0 copy-done.5
  524.6 0.0 copy-start.3
  524.6 0.0 slice-start
  524.6 1.6 add.27
  526.2 0.0 copy-done.7
  526.2 0.6 fusion
  526.8 0.6 slice.11
  527.4 0.0 copy-done.6
  527.4 0.0 copy-start.2
  527.4 0.9 convert_reduce_fusion.3
  528.3 0.0 copy-done.3
  528.3 0.0 slice-start.1
  528.3 1.5 convert_reduce_fusion.2
  529.9 0.0 copy-done.2
  529.9 1.8 convert_reduce_fusion.1
  531.7 0.0 slice-done
  531.7 0.0 slice-done.1
  531.7 0.0 copy-start.1
  531.7 3.6 convert_reduce_fusion
  535.3 0.0 copy-done.1
  (2 shorter events, 0.0 us)
Async XLA Ops:
  0.6 0.8 copy-start
  521.0 3.6 copy-start.4
  521.0 3.6 copy-start.5
  521.0 5.2 copy-start.7
  521.0 6.4 %copy-start.6 = (bf16[3,256,512]{2,1,0:T(8,128)(2,1)S(1)}, bf16[3,256,512]{2,1,0:T(8,128)(2,1)}, u32[]{:S(2)}) copy-start(bf16[3,256,512]{2,1,0:T(8,128)(2,1)} %get-tuple-element.46) | copy-start | bytes 2359300
  524.6 3.7 copy-start.3
  524.6 7.1 %slice-start = ((s8[6291456]{0:T(1024)(128)(4,1)}), s8[4194304]{0:T(1024)(128)(4,1)S(1)}, s32[]{:S(2)}) async-start(s8[6291456]{0:T(1024)(128)(4,1)} %bitcast.4), calls=%async_computation | async-start | bytes 8388608
  527.4 2.5 copy-start.2
  528.3 3.4 slice-start.1
  531.7 3.6 copy-start.1
